TPU v7x, 32 devices: a whole 2x2x4 slice. The times are simulated.
32 devices in a mesh: replica: 4 (over x, core), shard: 8 (over z, y).
Axes of the slice: x: 2, y: 2, z: 4, core: 2. Of those that a mesh axis runs over, the one named last changes fastest.
Arguments:
- tokens: bfloat16 [32, 1024, 1024], P(('replica', 'shard')), may hold values from -6 to 6
- lengths: int32 [32], P(('replica', 'shard')), may hold values from 256 to 1024, as said below
- cotangent: bfloat16 [32, 1024, 1024], P(('replica', 'shard')), may hold values from -6 to 6
- w_qkv: bfloat16 [1024, 3072], P('shard'), may hold values from -0.1875 to 0.1875
- b_qv: bfloat16 [2048], P('shard'), may hold values from -3 to 3
- w_attn_out: bfloat16 [1024, 1024], P('shard'), may hold values from -1.5 to 1.5
- b_attn_out: bfloat16 [1024], P('shard'), may hold values from -3 to 3
- ln1_gain: bfloat16 [1024], P('shard'), may hold values from 0.099609375 to 1.8984375
- ln1_bias: bfloat16 [1024], P('shard'), may hold values from -3 to 3
- w_ffn_in: bfloat16 [1024, 4096], P('shard'), may hold values from -0.1875 to 0.1875
- b_ffn_in: bfloat16 [4096], P('shard'), may hold values from -3 to 3
- w_ffn_out: bfloat16 [4096, 1024], P('shard'), may hold values from -0.09375 to 0.09375
- b_ffn_out: bfloat16 [1024], P('shard'), may hold values from -3 to 3
- ln2_gain: bfloat16 [1024], P('shard'), may hold values from 0.099609375 to 1.8984375
- ln2_bias: bfloat16 [1024], P('shard'), may hold values from -3 to 3
Outputs:
- out: bfloat16 [32, 1024, 1024], P(('replica', 'shard'))
- grad_tokens: bfloat16 [32, 1024, 1024], P(('replica', 'shard'))
- grad_w_qkv: float32 [1024, 3072], P('shard')
- grad_b_qv: float32 [2048], P('shard')
- grad_w_attn_out: float32 [1024, 1024], P('shard')
- grad_b_attn_out: float32 [1024], P('shard')
- grad_ln1_gain: float32 [1024], P('shard')
- grad_ln1_bias: float32 [1024], P('shard')
- grad_w_ffn_in: float32 [1024, 4096], P('shard')
- grad_b_ffn_in: float32 [4096], P('shard')
- grad_w_ffn_out: float32 [4096, 1024], P('shard')
- grad_b_ffn_out: float32 [1024], P('shard')
- grad_ln2_gain: float32 [1024], P('shard')
- grad_ln2_bias: float32 [1024], P('shard')
Inputs may be any that keep to these rules, and one draw needn't show every extreme that they name: `lengths`: sequence 0 holds exactly 1024 tokens; the others take any count in the range.
All inputs are finite; a program needn't handle non-finite values.
Results may differ from a plain program's by a relative error of at most 0.017.
Values may be sent and summed in bfloat16 or wider, within the bound.
No kernel may reach another device: no remote copies, remote signals or barrier semaphores. Data moves between devices by JAX's collectives and lax.ppermute only.
A program may use at most 384 MiB of HBM per device.

v0:
```python
import jax
import jax.numpy as jnp
from jax import lax
from jax.sharding import PartitionSpec as P

HEADS = 16
HEAD_DIM = 64


SQRT_HALF = 0.7071067811865476
INV_ROOT_TAU = 0.3989422804014327


def gelu_value(pre_act):
    return 0.5 * pre_act * (1.0 + jax.scipy.special.erf(pre_act * SQRT_HALF))


def gelu_slope(pre_act):
    cumul = 0.5 * (1.0 + jax.scipy.special.erf(pre_act * SQRT_HALF))
    return cumul + pre_act * INV_ROOT_TAU * jnp.exp(-0.5 * pre_act * pre_act)


def inner_rows(left, right):
    return lax.dot_general(
        left, right, (((0,), (0,)), ((), ())), preferred_element_type=jnp.float32
    )


def times_trans(left, right):
    return lax.dot_general(
        left, right, (((1,), (1,)), ((), ())), preferred_element_type=jnp.float32
    )


def layer_norm(resid, gain, shift):
    mean_row = jnp.mean(resid, axis=-1, keepdims=True)
    centred = resid - mean_row
    inv_dev = lax.rsqrt(jnp.mean(centred * centred, axis=-1, keepdims=True) + 1e-05)
    normed = centred * inv_dev
    return (normed * gain + shift, normed, inv_dev)


def norm_back(grad_out, normed, inv_dev, gain):
    scaled = grad_out * gain
    return inv_dev * (
        scaled
        - jnp.mean(scaled, axis=-1, keepdims=True)
        - normed * jnp.mean(scaled * normed, axis=-1, keepdims=True)
    )


def shards(
    tokens,
    lengths,
    cotangent,
    w_qkv,
    b_qv,
    w_attn_out,
    b_attn_out,
    ln1_gain,
    ln1_bias,
    w_ffn_in,
    b_ffn_in,
    w_ffn_out,
    b_ffn_out,
    ln2_gain,
    ln2_bias,
):
    seq_count, slots, width = tokens.shape
    rows = seq_count * slots
    attn_set = (
        lax.all_gather(w_qkv, "shard", axis=0, tiled=True),
        lax.all_gather(b_qv, "shard", axis=0, tiled=True),
        lax.all_gather(w_attn_out, "shard", axis=0, tiled=True),
        lax.all_gather(b_attn_out, "shard", axis=0, tiled=True),
        lax.all_gather(ln1_gain, "shard", axis=0, tiled=True),
        lax.all_gather(ln1_bias, "shard", axis=0, tiled=True),
    )
    ffn_set = (
        lax.all_gather(w_ffn_in, "shard", axis=0, tiled=True),
        lax.all_gather(b_ffn_in, "shard", axis=0, tiled=True),
        lax.all_gather(w_ffn_out, "shard", axis=0, tiled=True),
        lax.all_gather(b_ffn_out, "shard", axis=0, tiled=True),
        lax.all_gather(ln2_gain, "shard", axis=0, tiled=True),
        lax.all_gather(ln2_bias, "shard", axis=0, tiled=True),
    )
    full_qkv, full_bqv, full_ao, full_bao, gain_one, shift_one = attn_set
    full_in, full_bin, full_out, full_bout, gain_two, shift_two = ffn_set
    gain_one = gain_one.astype(jnp.float32)
    gain_two = gain_two.astype(jnp.float32)
    position = lax.broadcasted_iota(jnp.int32, (seq_count, slots), 1)
    valid = position < lengths[:, None]
    valid_rows = valid.astype(jnp.float32).reshape(rows, 1)
    key_ok = valid[:, None, None, :]
    flat_in = tokens.reshape(rows, width)
    bias_full = jnp.concatenate(
        [
            full_bqv[:width].astype(jnp.float32),
            jnp.zeros((width,), jnp.float32),
            full_bqv[width:].astype(jnp.float32),
        ]
    )
    proj_all = (jnp.dot(flat_in, full_qkv, preferred_element_type=jnp.float32) + bias_full).astype(
        jnp.bfloat16
    )
    query_heads = proj_all[:, :width].reshape(seq_count, slots, HEADS, HEAD_DIM)
    key_heads = proj_all[:, width : 2 * width].reshape(seq_count, slots, HEADS, HEAD_DIM)
    value_heads = proj_all[:, 2 * width :].reshape(seq_count, slots, HEADS, HEAD_DIM)
    block = min(512, slots)
    nblocks = slots // block

    def block_scores(query_block):
        raw = (
            jnp.einsum(
                "sqhd,skhd->shqk", query_block, key_heads, preferred_element_type=jnp.float32
            )
            * 0.125
        )
        return jnp.where(key_ok, raw, -1e30)

    ctx_parts = []
    lse_parts = []
    for blk_index in range(nblocks):
        query_block = query_heads[:, blk_index * block : (blk_index + 1) * block]
        scores = block_scores(query_block)
        top = jnp.max(scores, axis=-1, keepdims=True)
        expo = jnp.exp(scores - top)
        total_exp = jnp.sum(expo, axis=-1, keepdims=True)
        probs_low = (expo / total_exp).astype(jnp.bfloat16)
        lse_parts.append(top + jnp.log(total_exp))
        ctx_parts.append(
            jnp.einsum(
                "shqk,skhd->sqhd", probs_low, value_heads, preferred_element_type=jnp.float32
            )
        )
    context = jnp.concatenate(ctx_parts, axis=1).reshape(rows, width).astype(jnp.bfloat16)
    resid_one = (
        flat_in.astype(jnp.float32)
        + jnp.dot(context, full_ao, preferred_element_type=jnp.float32)
        + full_bao.astype(jnp.float32)
    )
    hidden, normed_one, inv_one = layer_norm(resid_one, gain_one, shift_one.astype(jnp.float32))
    hidden_low = hidden.astype(jnp.bfloat16)
    pre_act = jnp.dot(hidden_low, full_in, preferred_element_type=jnp.float32) + full_bin.astype(
        jnp.float32
    )
    act_low = gelu_value(pre_act).astype(jnp.bfloat16)
    resid_two = (
        hidden
        + jnp.dot(act_low, full_out, preferred_element_type=jnp.float32)
        + full_bout.astype(jnp.float32)
    )
    final, normed_two, inv_two = layer_norm(resid_two, gain_two, shift_two.astype(jnp.float32))
    out = (final * valid_rows).astype(jnp.bfloat16).reshape(seq_count, slots, width)
    back_attn = (
        lax.all_gather(w_qkv, "shard", axis=0, tiled=True),
        lax.all_gather(b_qv, "shard", axis=0, tiled=True),
        lax.all_gather(w_attn_out, "shard", axis=0, tiled=True),
        lax.all_gather(b_attn_out, "shard", axis=0, tiled=True),
        lax.all_gather(ln1_gain, "shard", axis=0, tiled=True),
        lax.all_gather(ln1_bias, "shard", axis=0, tiled=True),
    )
    back_ffn = (
        lax.all_gather(w_ffn_in, "shard", axis=0, tiled=True),
        lax.all_gather(b_ffn_in, "shard", axis=0, tiled=True),
        lax.all_gather(w_ffn_out, "shard", axis=0, tiled=True),
        lax.all_gather(b_ffn_out, "shard", axis=0, tiled=True),
        lax.all_gather(ln2_gain, "shard", axis=0, tiled=True),
        lax.all_gather(ln2_bias, "shard", axis=0, tiled=True),
    )
    back_qkv = back_attn[0]
    back_ao = back_attn[2]
    back_gain_one = back_attn[4].astype(jnp.float32)
    back_in = back_ffn[0]
    back_out = back_ffn[2]
    back_gain_two = back_ffn[4].astype(jnp.float32)
    grad_final = cotangent.reshape(rows, width).astype(jnp.float32) * valid_rows
    grad_gain_two = jnp.sum(grad_final * normed_two, axis=0)
    grad_shift_two = jnp.sum(grad_final, axis=0)
    grad_resid_two = norm_back(grad_final, normed_two, inv_two, back_gain_two)
    grad_ffn = grad_resid_two.astype(jnp.bfloat16)
    grad_bout = jnp.sum(grad_ffn.astype(jnp.float32), axis=0)
    grad_wout = inner_rows(act_low, grad_ffn)
    grad_pre = (times_trans(grad_ffn, back_out) * gelu_slope(pre_act)).astype(jnp.bfloat16)
    grad_bin = jnp.sum(grad_pre.astype(jnp.float32), axis=0)
    grad_win = inner_rows(hidden_low, grad_pre)
    grad_hidden = grad_resid_two + times_trans(grad_pre, back_in)
    grad_gain_one = jnp.sum(grad_hidden * normed_one, axis=0)
    grad_shift_one = jnp.sum(grad_hidden, axis=0)
    grad_resid_one = norm_back(grad_hidden, normed_one, inv_one, back_gain_one)
    grad_attn = grad_resid_one.astype(jnp.bfloat16)
    grad_bao = jnp.sum(grad_attn.astype(jnp.float32), axis=0)
    grad_wao = inner_rows(context, grad_attn)
    grad_context = (
        times_trans(grad_attn, back_ao)
        .astype(jnp.bfloat16)
        .reshape(seq_count, slots, HEADS, HEAD_DIM)
    )
    grad_key = jnp.zeros((seq_count, slots, HEADS, HEAD_DIM), jnp.float32)
    grad_value = jnp.zeros((seq_count, slots, HEADS, HEAD_DIM), jnp.float32)
    query_grads = []
    for blk_index in range(nblocks):
        query_block = query_heads[:, blk_index * block : (blk_index + 1) * block]
        ctx_grad_block = grad_context[:, blk_index * block : (blk_index + 1) * block]
        probs_full = jnp.exp(block_scores(query_block) - lse_parts[blk_index])
        grad_probs = jnp.einsum(
            "sqhd,skhd->shqk", ctx_grad_block, value_heads, preferred_element_type=jnp.float32
        )
        row_dot = jnp.sum(grad_probs * probs_full, axis=-1, keepdims=True)
        grad_scores = (probs_full * (grad_probs - row_dot)).astype(jnp.bfloat16)
        query_grads.append(
            jnp.einsum(
                "shqk,skhd->sqhd", grad_scores, key_heads, preferred_element_type=jnp.float32
            )
            * 0.125
        )
        grad_key = (
            grad_key
            + jnp.einsum(
                "shqk,sqhd->skhd", grad_scores, query_block, preferred_element_type=jnp.float32
            )
            * 0.125
        )
        grad_value = grad_value + jnp.einsum(
            "shqk,sqhd->skhd",
            probs_full.astype(jnp.bfloat16),
            ctx_grad_block,
            preferred_element_type=jnp.float32,
        )
    grad_query = jnp.concatenate(query_grads, axis=1)
    grad_proj = jnp.concatenate(
        [
            grad_query.reshape(rows, width),
            grad_key.reshape(rows, width),
            grad_value.reshape(rows, width),
        ],
        axis=1,
    ).astype(jnp.bfloat16)
    grad_proj_wide = grad_proj.astype(jnp.float32)
    grad_bqv = jnp.concatenate(
        [
            jnp.sum(grad_proj_wide[:, :width], axis=0),
            jnp.sum(grad_proj_wide[:, 2 * width :], axis=0),
        ]
    )
    grad_wqkv = inner_rows(flat_in, grad_proj)
    grad_tokens = (
        (grad_resid_one + times_trans(grad_proj, back_qkv))
        .astype(jnp.bfloat16)
        .reshape(seq_count, slots, width)
    )
    ffn_owned = (
        lax.psum_scatter(grad_win, "shard", scatter_dimension=0, tiled=True),
        lax.psum_scatter(grad_bin, "shard", scatter_dimension=0, tiled=True),
        lax.psum_scatter(grad_wout, "shard", scatter_dimension=0, tiled=True),
        lax.psum_scatter(grad_bout, "shard", scatter_dimension=0, tiled=True),
        lax.psum_scatter(grad_gain_two, "shard", scatter_dimension=0, tiled=True),
        lax.psum_scatter(grad_shift_two, "shard", scatter_dimension=0, tiled=True),
    )
    attn_owned = (
        lax.psum_scatter(grad_wqkv, "shard", scatter_dimension=0, tiled=True),
        lax.psum_scatter(grad_bqv, "shard", scatter_dimension=0, tiled=True),
        lax.psum_scatter(grad_wao, "shard", scatter_dimension=0, tiled=True),
        lax.psum_scatter(grad_bao, "shard", scatter_dimension=0, tiled=True),
        lax.psum_scatter(grad_gain_one, "shard", scatter_dimension=0, tiled=True),
        lax.psum_scatter(grad_shift_one, "shard", scatter_dimension=0, tiled=True),
    )
    summed = (
        lax.psum(attn_owned[0].astype(jnp.bfloat16), "replica").astype(jnp.float32),
        lax.psum(attn_owned[1].astype(jnp.bfloat16), "replica").astype(jnp.float32),
        lax.psum(attn_owned[2].astype(jnp.bfloat16), "replica").astype(jnp.float32),
        lax.psum(attn_owned[3].astype(jnp.bfloat16), "replica").astype(jnp.float32),
        lax.psum(attn_owned[4].astype(jnp.bfloat16), "replica").astype(jnp.float32),
        lax.psum(attn_owned[5].astype(jnp.bfloat16), "replica").astype(jnp.float32),
        lax.psum(ffn_owned[0].astype(jnp.bfloat16), "replica").astype(jnp.float32),
        lax.psum(ffn_owned[1].astype(jnp.bfloat16), "replica").astype(jnp.float32),
        lax.psum(ffn_owned[2].astype(jnp.bfloat16), "replica").astype(jnp.float32),
        lax.psum(ffn_owned[3].astype(jnp.bfloat16), "replica").astype(jnp.float32),
        lax.psum(ffn_owned[4].astype(jnp.bfloat16), "replica").astype(jnp.float32),
        lax.psum(ffn_owned[5].astype(jnp.bfloat16), "replica").astype(jnp.float32),
    )
    return (
        out,
        grad_tokens,
        summed[0],
        summed[1],
        summed[2],
        summed[3],
        summed[4],
        summed[5],
        summed[6],
        summed[7],
        summed[8],
        summed[9],
        summed[10],
        summed[11],
    )


def solution(mesh):
    return jax.shard_map(
        shards,
        mesh=mesh,
        in_specs=(
            P(("replica", "shard"), None, None),
            P(("replica", "shard")),
            P(("replica", "shard"), None, None),
            P("shard", None),
            P("shard"),
            P("shard", None),
            P("shard"),
            P("shard"),
            P("shard"),
            P("shard", None),
            P("shard"),
            P("shard", None),
            P("shard"),
            P("shard"),
            P("shard"),
        ),
        out_specs=(
            P(("replica", "shard"), None, None),
            P(("replica", "shard"), None, None),
            P("shard", None),
            P("shard"),
            P("shard", None),
            P("shard"),
            P("shard"),
            P("shard"),
            P("shard", None),
            P("shard"),
            P("shard", None),
            P("shard"),
            P("shard"),
            P("shard"),
        ),
        check_vma=False,
    )
```

profile of v0, /device:TPU:0, one launch (start us, length us, event | category | flops | bytes accessed | tf_op | source)
XLA Modules:
  0.0 1564.8 jit_solution(16799600917718266180)
XLA Ops:
  12.6 22.6 %all-gather.1 = bf16[8,1,128]{2,1,0:T(2,128)(2,1)S(1)} all-gather(bf16[1,1,128]{2,1,0:T(2,128)(2,1)} %bitcast.177), channel_id=1, replica_groups=mesh['replica'=4,'shard'=8] {'shard'}, dimensions={0}, use_global_device_ids=true | all-gather | bytes 2304 | tf_op jit(solution)/shard_map/all_gather | solution.py:75
  35.9 16.6 %all-gather.2 = bf16[8,1,128]{2,1,0:T(2,128)(2,1)S(1)} all-gather(bf16[1,1,128]{2,1,0:T(2,128)(2,1)} %bitcast.178), channel_id=1, replica_groups=mesh['replica'=4,'shard'=8] {'shard'}, dimensions={0}, use_global_device_ids=true | all-gather | bytes 2304 | tf_op jit(solution)/shard_map/all_gather | solution.py:76
  53.1 18.6 %all-gather.3 = bf16[8,1,128]{2,1,0:T(2,128)(2,1)S(1)} all-gather(bf16[1,1,128]{2,1,0:T(2,128)(2,1)} %bitcast.179), channel_id=1, replica_groups=mesh['replica'=4,'shard'=8] {'shard'}, dimensions={0}, use_global_device_ids=true | all-gather | bytes 2304 | tf_op jit(solution)/shard_map/all_gather | solution.py:77
  72.3 16.7 %all-gather.5 = bf16[8,1,128]{2,1,0:T(2,128)(2,1)S(1)} all-gather(bf16[1,1,128]{2,1,0:T(2,128)(2,1)} %bitcast.180), channel_id=1, replica_groups=mesh['replica'=4,'shard'=8] {'shard'}, dimensions={0}, use_global_device_ids=true | all-gather | bytes 2304 | tf_op jit(solution)/shard_map/all_gather | solution.py:83
  89.5 18.4 %all-gather.6 = bf16[8,1,128]{2,1,0:T(2,128)(2,1)S(1)} all-gather(bf16[1,1,128]{2,1,0:T(2,128)(2,1)} %bitcast.181), channel_id=1, replica_groups=mesh['replica'=4,'shard'=8] {'shard'}, dimensions={0}, use_global_device_ids=true | all-gather | bytes 2304 | tf_op jit(solution)/shard_map/all_gather | solution.py:84
  108.5 16.4 %all-gather.7 = bf16[8,1,128]{2,1,0:T(2,128)(2,1)S(1)} all-gather(bf16[1,1,128]{2,1,0:T(2,128)(2,1)} %bitcast.182), channel_id=1, replica_groups=mesh['replica'=4,'shard'=8] {'shard'}, dimensions={0}, use_global_device_ids=true | all-gather | bytes 2304 | tf_op jit(solution)/shard_map/all_gather | solution.py:85
  125.5 18.2 %all-gather = bf16[8,1,256]{2,1,0:T(2,128)(2,1)S(1)} all-gather(bf16[1,1,256]{2,1,0:T(2,128)(2,1)S(1)} %reshape.305), channel_id=1, replica_groups=mesh['replica'=4,'shard'=8] {'shard'}, dimensions={0}, use_global_device_ids=true | all-gather | bytes 4608 | tf_op jit(solution)/shard_map/all_gather | solution.py:73
  143.8 26.3 %all-gather.4 = bf16[8,1,512]{2,1,0:T(2,128)(2,1)S(1)} all-gather(bf16[1,1,512]{2,1,0:T(2,128)(2,1)S(1)} %reshape.313), channel_id=1, replica_groups=mesh['replica'=4,'shard'=8] {'shard'}, dimensions={0}, use_global_device_ids=true | all-gather | bytes 9216 | tf_op jit(solution)/shard_map/all_gather | solution.py:81
  173.4 4.1 copy.58
  177.5 9.7 add_convert_fusion
  195.6 15.7 %fusion.17 = (f32[16,512]{1,0:T(8,128)S(1)}, f32[16,512,1024]{2,1,0:T(8,128)}) fusion(pred[1024]{0:T(1024)(128)(4,1)S(1)} %iota_compare_fusion, bf16[1024,16,64]{0,2,1:T(8,128)(2,1)S(1)} %bitcast.132, bf16[1,1024,16,64]{1,3,2,0:T(8,128)(2,1)} %bitcast.140), kind=kOutput, calls=%fused_computation.31 | convolution fusion | flops 1098899456 | bytes 36733952 | tf_op jit(solution)/shard_map/sqhd,skhd->shqk/dot_general | solution.py:114
  211.3 25.8 %fusion = (f32[16,512]{1,0:T(8,128)S(1)}, f32[16,512]{1,0:T(8,128)S(1)}, f32[16,512,1024]{2,1,0:T(8,128)}) fusion(f32[16,512]{1,0:T(8,128)S(1)} %get-tuple-element.102, f32[16,512,1024]{2,1,0:T(8,128)} %get-tuple-element.103, pred[1024]{0:T(1024)(128)(4,1)S(1)} %iota_compare_fusion, bf16[1024,16,64]{0,2,1:T(8,128)(2,1)S(1)} %bitcast.133, ...), kind=kOutput, calls=%fused_computation.12 | convolution fusion | flops 1132445696 | bytes 70353920 | tf_op jit(solution)/shard_map/sqhd,skhd->shqk/dot_general | solution.py:114
  237.0 14.8 fusion.1
  254.8 14.8 fusion.40
  269.6 13.7 fusion.41
  284.0 5.4 fusion.67
  292.1 20.9 %multiply_convert_fusion.2 = (bf16[1024,4096]{1,0:T(8,128)(2,1)}, f32[1024,4096]{1,0:T(8,128)}) fusion(f32[4096]{0:T(1024)S(1)} %bitcast.168, bf16[1024,4096]{1,0:T(8,128)(2,1)} %all-gather.17.cloned.1.call-done, f32[1024,1024]{0,1:T(8,128)} %copy-done.6, f32[1024]{0:T(1024)S(1)} %bitcast.172, f32[1024]{0:T(1024)S(1)} %bitcast.163, ...), kind=kOutput, calls=%fused_computation.27 | convolution fusion | flops 8620343296 | bytes 37781504 | tf_op jit(solution)/shard_map/dot_general | solution.py:144
  313.0 99.7 %all-gather.19.cloned.1.call-done = bf16[4096,1024]{1,0:T(8,128)(2,1)} async-done(((bf16[512,1024]{1,0:T(8,128)(2,1)}), bf16[4096,1024]{1,0:T(8,128)(2,1)}) %all-gather.19.cloned.1.call-update) | async-done | bytes 8388624 | tf_op jit(solution)/shard_map/all_gather | solution.py:82
  412.6 14.9 fusion.68
  429.1 3.2 fusion.28
  432.3 4.0 convert_reduce_fusion.1
  436.4 20.0 %convert_reduce_fusion = (f32[4096]{0:T(1024)}, bf16[1024,4096]{1,0:T(8,128)(2,1)}) fusion(f32[1024,4096]{1,0:T(8,128)} %get-tuple-element.108, f32[4096]{0:T(1024)S(1)} %bitcast.169, bf16[1024,1024]{0,1:T(8,128)(2,1)S(1)} %get-tuple-element.91, bf16[4096,1024]{1,0:T(8,128)(2,1)S(1)} %bitcast.184), kind=kOutput, calls=%fused_computation.24 | convolution fusion | flops 8644456448 | bytes 35684352 | tf_op jit(solution)/shard_map/dot_general | solution.py:30
  456.4 17.1 %multiply_reduce_fusion.2 = (f32[1024]{0:T(1024)}, f32[1024]{0:T(1024)S(1)}, f32[1024]{0:T(1024)S(1)}, f32[1024]{0:T(1024)}, f32[1024,1024]{0,1:T(8,128)S(1)}) fusion(f32[1024,1024]{0,1:T(8,128)S(1)} %copy-done.7, f32[1024]{0:T(1024)S(1)} %add_rsqrt_fusion.1, f32[1024]{0:T(1024)S(1)} %broadcast_multiply_fusion.5, f32[1024]{0:T(1024)S(1)} %bitcast.165, ...), kind=kOutput, calls=%fused_computation.50 | convolution fusion | flops 8609853440 | bytes 31510528 | tf_op jit(solution)/shard_map/dot_general | solution.py:30
  477.5 4.4 fusion.49
  482.0 5.3 convolution_convert_fusion
  487.3 13.4 fusion.45
  500.7 45.2 %multiply_reduce_fusion = (f32[16,512]{1,0:T(8,128)S(1)}, f32[16,512]{1,0:T(8,128)S(1)}, f32[16,512,1024]{2,1,0:T(8,128)}) fusion(f32[16,512]{1,0:T(8,128)S(1)} %get-tuple-element.115, f32[16,512,1024]{2,1,0:T(8,128)} %get-tuple-element.104, pred[1024]{0:T(1024)(128)(4,1)S(1)} %iota_compare_fusion, f32[16,512,1024]{2,1,0:T(8,128)} %fusion.45, ...), kind=kOutput, calls=%fused_computation.1 | convolution fusion | flops 1157611520 | bytes 137495552 | tf_op jit(solution)/shard_map/sqhd,skhd->shqk/dot_general | solution.py:206
  545.9 55.2 %multiply_convert_fusion = (bf16[16,512,1024]{2,1,0:T(8,128)(2,1)}, bf16[16,512,1024]{2,1,0:T(8,128)(2,1)}) fusion(f32[16,512,1024]{2,1,0:T(8,128)} %get-tuple-element.112, f32[16,512]{1,0:T(8,128)S(1)} %get-tuple-element.66, f32[16,512]{1,0:T(8,128)S(1)} %get-tuple-element.115, f32[16,512,1024]{2,1,0:T(8,128)} %get-tuple-element.104, ...), kind=kLoop, calls=%fused_computation | loop fusion | flops 100663296 | bytes 167904256 | tf_op jit(solution)/shard_map/convert_element_type | solution.py:210
  601.2 11.0 fusion.39
  612.2 11.9 fusion.38
  624.1 3.0 pad_maximum_fusion.2
  627.1 9.3 fusion.42
  636.8 5.8 multiply_convert_fusion.3
  642.7 16.5 %fusion.9 = f32[16,64,1024]{2,1,0:T(8,128)} fusion(f32[16,512]{1,0:T(8,128)S(1)} %get-tuple-element.115, f32[16,512,1024]{2,1,0:T(8,128)} %get-tuple-element.104, pred[1024]{0:T(1024)(128)(4,1)S(1)} %iota_compare_fusion, bf16[1,1024,16,64]{1,3,2,0:T(8,128)(2,1)} %bitcast.152), kind=kOutput, calls=%fused_computation.22 | convolution fusion | flops 1107296256 | bytes 38831104 | tf_op jit(solution)/shard_map/shqk,sqhd->skhd/dot_general | solution.py:224
  659.2 17.6 %add_convert_fusion.2 = bf16[16,64,1024]{2,1,0:T(8,128)(2,1)} fusion(f32[16,64,1024]{2,1,0:T(8,128)} %fusion.9, f32[16,512]{1,0:T(8,128)S(1)} %get-tuple-element.116, f32[16,512,1024]{2,1,0:T(8,128)} %get-tuple-element.103, pred[1024]{0:T(1024)(128)(4,1)S(1)} %iota_compare_fusion, bf16[1,1024,16,64]{1,3,2,0:T(8,128)(2,1)} %bitcast.153), kind=kOutput, calls=%fused_computation.53 | convolution fusion | flops 1109393408 | bytes 40928256 | tf_op jit(solution)/shard_map/shqk,sqhd->skhd/dot_general | solution.py:224
  676.8 13.6 convolution_bitcast_fusion
  691.1 16.9 %fusion.61 = f32[1024,4096]{1,0:T(8,128)} fusion(bf16[1024,4096]{1,0:T(8,128)(2,1)} %get-tuple-element.114, f32[1024,1024]{0,1:T(8,128)} %copy-done.6, f32[1024]{0:T(1024)S(1)} %bitcast.174, f32[1024]{0:T(1024)S(1)} %bitcast.167, f32[1024]{0:T(1024)S(1)} %copy-done.29, f32[1024]{0:T(1024)S(1)} %copy-done.20), kind=kOutput, calls=%fused_computation.129 | convolution fusion | flops 8595177472 | bytes 29376512 | tf_op jit(solution)/shard_map/dot_general | solution.py:24
  708.0 16.3 %fusion.69 = f32[4096,1024]{1,0:T(8,128)} fusion(bf16[1024,4096]{1,0:T(8,128)(2,1)} %get-tuple-element.107, bf16[1024,1024]{0,1:T(8,128)(2,1)} %copy-done.11), kind=kOutput, calls=%fused_computation.134 | convolution fusion | flops 8589934592 | bytes 27262976 | tf_op jit(solution)/shard_map/dot_general | solution.py:24
  729.3 167.1 %reduce-scatter.5.cloned.1.call-done = f32[128,3072]{0,1:T(8,128)} async-done(((f32[1024,3072]{0,1:T(8,128)}), f32[128,3072]{0,1:T(8,128)}) %reduce-scatter.5.cloned.1.call-update) | async-done | bytes 1572880 | tf_op jit(solution)/shard_map/reduce_scatter | solution.py:261
  898.8 283.3 %reduce-scatter.9.cloned.1.call-done = f32[128,4096]{1,0:T(8,128)} async-done(((f32[1024,4096]{1,0:T(8,128)}), f32[128,4096]{1,0:T(8,128)}) %reduce-scatter.9.cloned.1.call-update) | async-done | bytes 2097168 | tf_op jit(solution)/shard_map/reduce_scatter | solution.py:253
  1184.8 282.5 %reduce-scatter.11.cloned.1.call-done = f32[512,1024]{1,0:T(8,128)} async-done(((f32[4096,1024]{1,0:T(8,128)}), f32[512,1024]{1,0:T(8,128)}) %reduce-scatter.11.cloned.1.call-update) | async-done | bytes 2097168 | tf_op jit(solution)/shard_map/reduce_scatter | solution.py:255
  1470.1 12.2 fusion.31
  1482.2 4.0 copy.66
  1486.2 3.9 copy.67
  1490.1 8.5 fusion.60
  1498.7 4.0 slice_reduce_fusion.1
  1502.8 35.7 %all-reduce.8 = (bf16[2048]{0:T(1024)(128)(2,1)S(1)}, bf16[1024]{0:T(1024)(128)(2,1)S(1)}, bf16[1024]{0:T(1024)(128)(2,1)S(1)}, bf16[1024]{0:T(1024)(128)(2,1)S(...) all-reduce(f32[2048]{0:T(1024)S(1)} %pad_maximum_fusion.4, ...), channel_id=3, replica_groups=mesh['replica'=4,'shard'=8] {'shard'}, use_global_device_ids=true, to_apply=%region_18.19.clone | all-reduce | flops 12288 | bytes 73728
  1539.1 5.7 all-reduce.9
  (172 shorter events, 57.3 us)
Async XLA Ops:
  7.2 163.6 %copy-start.12 = (bf16[1,1024,1024]{2,1,0:T(8,128)(2,1)S(1)}, bf16[1,1024,1024]{2,1,0:T(8,128)(2,1)}, u32[]{:S(2)}) copy-start(bf16[1,1024,1024]{2,1,0:T(8,128)(2,1)} %param.17) | copy-start | bytes 6291460
  7.2 170.3 %all-gather.13.cloned.1.call-start = ((), (), s32[]{:S(2)}) async-start(), calls=%async_computation.4 | async-start | bytes 7077888 | tf_op jit(solution)/shard_map/all_gather | solution.py:72
  7.9 275.7 %all-gather.15.cloned.1.call-start = ((), (), s32[]{:S(2)}) async-start(), calls=%async_computation.5 | async-start | bytes 2359296 | tf_op jit(solution)/shard_map/all_gather | solution.py:74
  8.7 283.4 %all-gather.17.cloned.1.call-start = ((), (), s32[]{:S(2)}) async-start(), calls=%async_computation.6 | async-start | bytes 9437184 | tf_op jit(solution)/shard_map/all_gather | solution.py:80
  9.4 403.2 %all-gather.19.cloned.1.call-start = ((), (), s32[]{:S(2)}) async-start(), calls=%async_computation.7 | async-start | bytes 9437184 | tf_op jit(solution)/shard_map/all_gather | solution.py:82
  10.0 717.6 %reduce-scatter.7.cloned.1.call-start = ((), (), s32[]{:S(2)}) async-start(), calls=%async_computation.9 | async-start | bytes 4718592 | tf_op jit(solution)/shard_map/reduce_scatter | solution.py:263
  173.4 4.1 copy-start.13
  195.5 15.7 %copy-start = (bf16[1024,1024]{0,1:T(8,128)(2,1)}, bf16[1024,1024]{0,1:T(8,128)(2,1)S(1)}, u32[]{:S(2)}) copy-start(bf16[1024,1024]{0,1:T(8,128)(2,1)S(1)} %copy.61) | copy-start | bytes 6291460
  195.5 15.7 %copy-start.4 = (bf16[1024,1024]{0,1:T(8,128)(2,1)S(1)}, bf16[1024,1024]{0,1:T(8,128)(2,1)}, u32[]{:S(2)}) copy-start(bf16[1024,1024]{0,1:T(8,128)(2,1)} %copy.60) | copy-start | bytes 6291460
  254.7 14.8 copy-start.2
  283.6 5.8 copy-start.14
  289.4 2.1 copy-start.6
  289.4 2.6 copy-start.26
  289.4 2.6 copy-start.31
  289.4 2.6 copy-start.34
  289.4 184.1 %copy-start.19 = (f32[1024]{0:T(1024)}, f32[1024]{0:T(1024)S(1)}, u32[]{:S(2)}) copy-start(f32[1024]{0:T(1024)S(1)} %broadcast_multiply_fusion.5) | copy-start | bytes 12292
  292.0 181.5 %copy-start.28 = (f32[1024]{0:T(1024)}, f32[1024]{0:T(1024)S(1)}, u32[]{:S(2)}) copy-start(f32[1024]{0:T(1024)S(1)} %add_rsqrt_fusion.1) | copy-start | bytes 12292
  292.1 120.6 %copy-start.36 = (f32[8,1,128]{2,1,0:T(1,128)S(1)}, f32[8,1,128]{2,1,0:T(1,128)}, u32[]{:S(2)}) copy-start(f32[8,1,128]{2,1,0:T(1,128)} %convert_element_type.249) | copy-start | bytes 12292
  427.5 1.6 copy-start.5
  427.5 1.6 copy-start.17
  427.6 1.6 copy-start.18
  428.1 4.3 copy-start.22
  429.1 7.2 slice-start.4
  432.3 4.0 slice-start.5
  436.4 20.1 %copy-start.11 = (bf16[1024,1024]{0,1:T(8,128)(2,1)}, bf16[1024,1024]{0,1:T(8,128)(2,1)S(1)}, u32[]{:S(2)}) copy-start(bf16[1024,1024]{0,1:T(8,128)(2,1)S(1)} %get-tuple-element.91) | copy-start | bytes 6291460
  436.4 20.1 %copy-start.7 = (f32[1024,1024]{0,1:T(8,128)S(1)}, f32[1024,1024]{0,1:T(8,128)}, u32[]{:S(2)}) copy-start(f32[1024,1024]{0,1:T(8,128)} %copy-done.6) | copy-start | bytes 12582916
  473.5 4.0 copy-start.15
  475.5 2.0 copy-start.9
  481.9 5.4 copy-start.3
  481.9 414.5 %reduce-scatter.5.cloned.1.call-start = ((), (), s32[]{:S(2)}) async-start(), calls=%async_computation.8 | async-start | bytes 14155776 | tf_op jit(solution)/shard_map/reduce_scatter | solution.py:261
  487.3 13.5 copy-start.10
  545.9 55.2 %copy-start.1 = (bf16[1024,1024]{0,1:T(8,128)(2,1)S(1)}, bf16[1024,1024]{0,1:T(8,128)(2,1)}, u32[]{:S(2)}) copy-start(bf16[1024,1024]{0,1:T(8,128)(2,1)} %copy-done) | copy-start | bytes 6291460
  624.1 12.3 slice-start
  627.1 9.3 slice-start.1
  627.1 9.3 slice-start.2
  627.1 9.7 slice-start.3
  659.2 17.6 %copy-start.8 = (bf16[16,64,1024]{2,1,0:T(8,128)(2,1)S(1)}, bf16[16,64,1024]{2,1,0:T(8,128)(2,1)}, u32[]{:S(2)}) copy-start(bf16[16,64,1024]{2,1,0:T(8,128)(2,1)} %multiply_convert_fusion.3) | copy-start | bytes 6291460
  690.5 491.7 %reduce-scatter.9.cloned.1.call-start = ((), (), s32[]{:S(2)}) async-start(), calls=%async_computation.10 | async-start | bytes 18874368 | tf_op jit(solution)/shard_map/reduce_scatter | solution.py:253
  708.0 759.3 %reduce-scatter.11.cloned.1.call-start = ((), (), s32[]{:S(2)}) async-start(), calls=%async_computation.11 | async-start | bytes 18874368 | tf_op jit(solution)/shard_map/reduce_scatter | solution.py:255
  724.4 824.7 %all-reduce.13.cloned.1.call-start = ((), (), s32[]{:S(2)}) async-start(), calls=%async_computation.12 | async-start | bytes 6291456 | tf_op jit(solution)/shard_map/psum | solution.py:269
  1498.7 4.1 copy-start.21
  1498.7 4.1 copy-start.23
  1498.7 4.1 copy-start.24
  1498.7 4.1 copy-start.25
  1498.7 4.1 copy-start.30
  1498.7 4.1 copy-start.32
  1498.7 4.1 copy-start.33
  1549.1 7.2 copy-start.16
  (6 other events, 4.1 us)
Sparse Core Ops, SparseCore 0:
  10.2 101.9 all-gather.12
  114.4 47.5 all-gather.14
  164.1 123.4 all-gather.16
  289.6 123.0 all-gather.18
  482.0 86.0 reduce-scatter.6
  690.6 205.8 reduce-scatter.4
  900.7 281.3 reduce-scatter.8
  1185.9 281.3 reduce-scatter.10
  1470.7 68.0 all-reduce.12
where the time goes:
time: 1580 us; the launch traced here: 1560 us
  waiting for transfers between devices  835 us (53%)
  matrix products  357 us (23%)
  blocking collectives  195 us (12%)
  other arithmetic  121 us (8%)
  local copies, waits for them, and re-layouts  38.1 us (2%)
  between operations  17.5 us (1%)
    reduce_scatter x1, waiting for transfers between devices, shards(): lax.psum_scatter(grad_win, 'shard', scatter_dimension=0, tiled=True)  283 us
    reduce_scatter x1, waiting for transfers between devices, shards(): lax.psum_scatter(grad_wout, 'shard', scatter_dimension=0, tiled=True)  282 us
    reduce_scatter x1, waiting for transfers between devices, shards(): lax.psum_scatter(grad_wqkv, 'shard', scatter_dimension=0, tiled=True)  167 us
    all_gather x1, waiting for transfers between devices, shards(): lax.all_gather(w_ffn_out, 'shard', axis=0, tiled=True)  99.7 us
    dot_general x2, matrix products, shards(): jnp.einsum('sqhd,skhd->shqk', ctx_grad_block, value_heads, preferred_elem...  58.7 us
    convert_element_type x1, other arithmetic, shards(): grad_scores = (probs_full * (grad_probs - row_dot)).astype(jnp.bfloat16)  55.2 us
    dot_general x4, matrix products, times_trans(): lax.dot_general(left, right, (((1,), (1,)), ((), ())), preferred_element_...  54.6 us
    dot_general x4, matrix products, inner_rows(): lax.dot_general(left, right, (((0,), (0,)), ((), ())), preferred_element_...  51.1 us
  transfers between devices with their start and end apart: 9, of which 4 were waited for; matrix products, arithmetic and copies ran while one was open for 28% of the time, Pallas kernels for 0%

commit v1 on v0

v1 whole, which is shorter than its diff:
```python
import functools
import jax
import jax.numpy as jnp
from jax import lax
from jax.experimental import pallas as pl
from jax.experimental.pallas import tpu as pltpu
from jax.sharding import PartitionSpec as P

HD = 64
F32 = jnp.float32
BF = jnp.bfloat16
SQRT_HALF = 0.7071067811865476
INV_ROOT_TAU = 0.3989422804014327
MIB = 1 << 20


def params(mib):
    return pltpu.CompilerParams(vmem_limit_bytes=mib * MIB)


def dot_nn(a, b):
    return jnp.dot(a, b, preferred_element_type=F32)


def dot_nt(a, b):
    return lax.dot_general(a, b, (((1,), (1,)), ((), ())), preferred_element_type=F32)


def dot_tn(a, b):
    return lax.dot_general(a, b, (((0,), (0,)), ((), ())), preferred_element_type=F32)


def cost(flops, nbytes, trans=0):
    return pl.CostEstimate(flops=int(flops), bytes_accessed=int(nbytes), transcendentals=int(trans))


def qkv_body(x_ref, w_ref, b_ref, o_ref, w_vm, sem):
    step = pl.program_id(0)
    blocks, width = w_vm.shape[0], w_vm.shape[-1]

    def copy(n):
        return pltpu.make_async_copy(w_ref.at[:, n], w_vm.at[n], sem.at[n])

    @pl.when(step == 0)
    def _():
        for n in range(blocks):
            copy(n).start()

    x = x_ref[...]
    for n in range(blocks):
        @pl.when(step == 0)
        def _():
            copy(n).wait()

        w = w_vm[n].reshape(-1, width)
        bias = b_ref[:, n * width : (n + 1) * width]
        o_ref[:, n * width : (n + 1) * width] = (dot_nn(x, w) + bias).astype(BF)


def qkv_call(x, w1, bias, rows=256):
    slots, width = x.shape
    pieces, total, sub, _ = w1.shape
    return pl.pallas_call(
        qkv_body,
        name="qkv",
        grid=(slots // rows,),
        in_specs=[
            pl.BlockSpec((rows, width), lambda i: (i, 0)),
            pl.BlockSpec(memory_space=pl.ANY),
            pl.BlockSpec((1, 3 * width), lambda i: (0, 0)),
        ],
        out_specs=pl.BlockSpec((rows, 3 * width), lambda i: (i, 0)),
        out_shape=jax.ShapeDtypeStruct((slots, 3 * width), BF),
        scratch_shapes=[
            pltpu.VMEM((3, pieces, sub, width), BF),
            pltpu.SemaphoreType.DMA((3,)),
        ],
        compiler_params=params(48),
        cost_estimate=cost(6 * slots * width * width, 8 * slots * width + 6 * width * width),
    )(x, w1, bias)


def lanes(rows):
    return lax.broadcasted_iota(jnp.int32, (rows, 2 * HD), 1)


def split3(v):
    hi = v.astype(BF).astype(F32)
    mid = (v - hi).astype(BF).astype(F32)
    return hi, mid, v - hi - mid


def attn_fwd_body(rows, len_ref, q_ref, k_ref, v_ref, ctx_ref, qa0_ref, qa1_ref):
    slots = k_ref.shape[0]
    lane = lanes(slots)
    key_row = lax.broadcasted_iota(jnp.int32, (slots, 2 * HD), 0)
    bias = jnp.where(key_row < len_ref[0], 0.0, -1e30)
    k = k_ref[...].astype(F32)
    k_aug = []
    for h in range(2):
        own = (lane // HD) == h
        spare = (1 - h) * HD
        k_aug.append(jnp.where(own, k, jnp.where(lane == spare, bias, 0.0)).astype(BF))
    v = v_ref[...]
    lane_q = lanes(rows)

    for blk in range(slots // rows):
        sl = slice(blk * rows, (blk + 1) * rows)
        q = q_ref[sl, :].astype(F32) * 0.125
        outs = []
        for h, qa_ref in enumerate((qa0_ref, qa1_ref)):
            own = (lane_q // HD) == h
            spare = (1 - h) * HD
            qh = jnp.where(own, q, jnp.where(lane_q == spare, 1.0, 0.0))
            s = dot_nt(qh.astype(BF), k_aug[h])
            top = jnp.max(s, axis=-1, keepdims=True)
            e = jnp.exp(s - top)
            total = jnp.sum(e, axis=-1, keepdims=True)
            o = dot_nn(e.astype(BF), v) / total
            outs.append(o)
            hi, mid, lo = split3(-(top + jnp.log(total)))
            qh = jnp.where(lane_q == spare + 1, hi, qh)
            qh = jnp.where(lane_q == spare + 2, mid, qh)
            qh = jnp.where(lane_q == spare + 3, lo, qh)
            qa_ref[sl, :] = qh.astype(BF)
        ctx_ref[sl, :] = jnp.where(lane_q < HD, outs[0], outs[1]).astype(BF)


def attn_fwd_call(qkv, lengths, rows=256):
    slots, wide = qkv.shape
    width = wide // 3
    pairs = width // (2 * HD)
    col = lambda off: pl.BlockSpec((slots, 2 * HD), lambda j, ln: (0, off * pairs + j))
    out = jax.ShapeDtypeStruct((slots, width), BF)
    return pl.pallas_call(
        functools.partial(attn_fwd_body, rows),
        name="attn_fwd",
        grid_spec=pltpu.PrefetchScalarGridSpec(
            num_scalar_prefetch=1,
            grid=(pairs,),
            in_specs=[col(0), col(1), col(2)],
            out_specs=[col(0)] * 3,
        ),
        out_shape=[out, out, out],
        compiler_params=params(48),
        cost_estimate=cost(16 * slots * slots * width, 12 * slots * width, slots * slots * 2 * pairs),
    )(lengths, qkv, qkv, qkv)


def attn_bwd_body(rows, len_ref, qa0_ref, qa1_ref, k_ref, v_ref, ctx_ref, g_ref, dq_ref, dk_ref, dv_ref, sq_ref, sv_ref):
    slots = k_ref.shape[0]
    lane = lanes(slots)
    key_row = lax.broadcasted_iota(jnp.int32, (slots, 2 * HD), 0)
    bias = jnp.where(key_row < len_ref[0], 0.0, -1e30)
    k = k_ref[...].astype(F32)
    v = v_ref[...].astype(F32)
    k_low = k_ref[...]
    k_aug, v_aug = [], []
    for h in range(2):
        own = (lane // HD) == h
        spare = (1 - h) * HD
        near = (lane > spare) & (lane < spare + 4)
        ones = jnp.where(near, 1.0, 0.0)
        k_aug.append(jnp.where(own, k, jnp.where(lane == spare, bias, ones)).astype(BF))
        v_aug.append(jnp.where(own, v, ones).astype(BF))
    lane_q = lanes(rows)
    dk = [jnp.zeros((slots, 2 * HD), F32)] * 2
    dv = [jnp.zeros((slots, 2 * HD), F32)] * 2
    for blk in range(slots // rows):
        sl = slice(blk * rows, (blk + 1) * rows)
        g_low = g_ref[sl, :]
        g = g_low.astype(F32)
        prod = g * ctx_ref[sl, :].astype(F32)
        dqs = []
        for h, qa_ref in enumerate((qa0_ref, qa1_ref)):
            own = (lane_q // HD) == h
            spare = (1 - h) * HD
            delta = jnp.sum(jnp.where(own, prod, 0.0), axis=-1, keepdims=True)
            hi, mid, lo = split3(-delta)
            ga = jnp.where(own, g, 0.0)
            ga = jnp.where(lane_q == spare + 1, hi, ga)
            ga = jnp.where(lane_q == spare + 2, mid, ga)
            ga = jnp.where(lane_q == spare + 3, lo, ga).astype(BF)
            qa = qa_ref[sl, :]
            p = jnp.exp(dot_nt(k_aug[h], qa))
            ds = (p * dot_nt(v_aug[h], ga)).astype(BF)
            dv[h] = dv[h] + dot_nn(p.astype(BF), g_low)
            dk[h] = dk[h] + dot_nn(ds, qa)
            dqs.append(dot_tn(ds, k_low))
        dq_ref[sl, :] = (jnp.where(lane_q < HD, dqs[0], dqs[1]) * 0.125).astype(BF)
    dk_ref[...] = jnp.where(lane < HD, dk[0], dk[1]).astype(BF)
    dv_low = jnp.where(lane < HD, dv[0], dv[1]).astype(BF)
    dv_ref[...] = dv_low
    sq_ref[...] = jnp.sum(dq_ref[...].astype(F32), axis=0, keepdims=True)
    sv_ref[...] = jnp.sum(dv_low.astype(F32), axis=0, keepdims=True)


def attn_bwd_call(qa0, qa1, qkv, ctx, grad_ctx, lengths, rows=256):
    slots, width = ctx.shape
    pairs = width // (2 * HD)
    col = lambda off: pl.BlockSpec((slots, 2 * HD), lambda j, ln: (0, off * pairs + j))
    row = pl.BlockSpec((1, 2 * HD), lambda j, ln: (0, j))
    out = jax.ShapeDtypeStruct((slots, width), BF)
    vec = jax.ShapeDtypeStruct((1, width), F32)
    return pl.pallas_call(
        functools.partial(attn_bwd_body, rows),
        name="attn_bwd",
        grid_spec=pltpu.PrefetchScalarGridSpec(
            num_scalar_prefetch=1,
            grid=(pairs,),
            in_specs=[col(0), col(0), col(1), col(2), col(0), col(0)],
            out_specs=[col(0)] * 3 + [row] * 2,
        ),
        out_shape=[out, out, out, vec, vec],
        compiler_params=params(48),
        cost_estimate=cost(40 * slots * slots * width, 18 * slots * width, slots * slots * 2 * pairs),
    )(lengths, qa0, qa1, qkv, qkv, ctx, grad_ctx)


def norm_stats(resid):
    mean = jnp.mean(resid, axis=-1, keepdims=True)
    centred = resid - mean
    inv = lax.rsqrt(jnp.mean(centred * centred, axis=-1, keepdims=True) + 1e-5)
    return centred * inv, inv


def norm_back(u, normed, inv):
    return inv * (u - jnp.mean(u, axis=-1, keepdims=True) - normed * jnp.mean(u * normed, axis=-1, keepdims=True))


def colsum(v):
    return jnp.sum(v, axis=0, keepdims=True)


def row_body(
    len_ref, x_ref, ctx_ref, cot_ref, wa_ref, w2_ref, vec_ref, bin_ref,
    out_ref, act_ref, hid_ref, gf_ref, gp_ref, ga_ref, gc_ref, sums_ref, sbin_ref,
    wa, wi, wo, slope, sem,
):
    step = pl.program_id(0)
    rows, width = x_ref.shape
    nblk = wi.shape[0]
    copies = [pltpu.make_async_copy(wa_ref.at[:, 3], wa, sem.at[0])]
    copies += [pltpu.make_async_copy(w2_ref.at[:, n], wi.at[n], sem.at[1 + n]) for n in range(nblk)]
    copies += [pltpu.make_async_copy(w2_ref.at[:, pl.ds(nblk, 4)], wo, sem.at[1 + nblk])]

    @pl.when(step == 0)
    def _():
        for c in copies:
            c.start()
        sums_ref[...] = jnp.zeros_like(sums_ref)
        sbin_ref[...] = jnp.zeros_like(sbin_ref)

    def ready(i):
        @pl.when(step == 0)
        def _():
            copies[i].wait()

    bao, gain1, shift1, bout, gain2, shift2 = [vec_ref[i : i + 1, :] for i in range(6)]
    ready(0)
    w_ao = wa[...].reshape(width, width)
    resid1 = x_ref[...].astype(F32) + dot_nn(ctx_ref[...], w_ao) + bao
    normed1, inv1 = norm_stats(resid1)
    hidden = normed1 * gain1 + shift1
    low = hidden.astype(BF)
    hid_ref[...] = low
    acc = jnp.zeros((rows, width), F32)
    per = wo.shape[0] // nblk
    for n in range(nblk):
        ready(1 + n)
        pre = dot_nn(low, wi[n].reshape(width, width)) + bin_ref[n : n + 1, :]
        phi = 0.5 + 0.5 * lax.erf(pre * SQRT_HALF)
        slope[n] = phi + pre * (INV_ROOT_TAU * jnp.exp(-0.5 * pre * pre))
        act = (pre * phi).astype(BF)
        act_ref[:, n * width : (n + 1) * width] = act
        if n == 0:
            ready(1 + nblk)
        acc = acc + dot_nn(act, wo[n * per : (n + 1) * per].reshape(width, width))
    resid2 = hidden + acc + bout
    normed2, inv2 = norm_stats(resid2)
    row_id = lax.broadcasted_iota(jnp.int32, (rows, 1), 0) + step * rows
    valid = (row_id < len_ref[0]).astype(F32)
    out_ref[...] = ((normed2 * gain2 + shift2) * valid).astype(BF)
    gz = cot_ref[...].astype(F32) * valid
    sums_ref[0:1, :] += colsum(gz * normed2)
    sums_ref[1:2, :] += colsum(gz)
    g_resid2 = norm_back(gz * gain2, normed2, inv2)
    gf = g_resid2.astype(BF)
    gf_ref[...] = gf
    sums_ref[2:3, :] += colsum(gf.astype(F32))
    acc = g_resid2
    for n in range(nblk):
        g_act = dot_nt(gf, wo[n * per : (n + 1) * per].reshape(width, width))
        gp = (g_act * slope[n]).astype(BF)
        gp_ref[:, n * width : (n + 1) * width] = gp
        sbin_ref[n : n + 1, :] += colsum(gp.astype(F32))
        acc = acc + dot_nt(gp, wi[n].reshape(width, width))
    sums_ref[3:4, :] += colsum(acc * normed1)
    sums_ref[4:5, :] += colsum(acc)
    g_attn = norm_back(acc * gain1, normed1, inv1).astype(BF)
    ga_ref[...] = g_attn
    sums_ref[5:6, :] += colsum(g_attn.astype(F32))
    gc_ref[...] = dot_nt(g_attn, w_ao).astype(BF)


def row_call(x, ctx, cot, w1, w2, vecs, b_in, lengths, rows=256):
    slots, width = x.shape
    pieces, _, sub, _ = w1.shape
    nblk = b_in.shape[0]
    ff = nblk * width
    blk = pl.BlockSpec((rows, width), lambda i, ln: (i, 0))
    big = pl.BlockSpec((rows, ff), lambda i, ln: (i, 0))
    const = lambda r: pl.BlockSpec((r, width), lambda i, ln: (0, 0))
    anyb = pl.BlockSpec(memory_space=pl.ANY)
    o = jax.ShapeDtypeStruct((slots, width), BF)
    ob = jax.ShapeDtypeStruct((slots, ff), BF)
    return pl.pallas_call(
        row_body,
        name="row_local",
        grid_spec=pltpu.PrefetchScalarGridSpec(
            num_scalar_prefetch=1,
            grid=(slots // rows,),
            in_specs=[blk, blk, blk, anyb, anyb, const(8), const(nblk)],
            out_specs=[blk, big, blk, blk, big, blk, blk, const(8), const(nblk)],
            scratch_shapes=[
                pltpu.VMEM((pieces, sub, width), BF),
                pltpu.VMEM((nblk, pieces, sub, width), BF),
                pltpu.VMEM((pieces, 4, sub, width), BF),
                pltpu.VMEM((nblk, rows, width), F32),
                pltpu.SemaphoreType.DMA((2 + nblk,)),
            ],
        ),
        out_shape=[
            o, ob, o, o, ob, o, o,
            jax.ShapeDtypeStruct((8, width), F32),
            jax.ShapeDtypeStruct((nblk, width), F32),
        ],
        compiler_params=params(60),
        cost_estimate=cost(36 * slots * width * width, 40 * slots * width + 18 * width * width, 2 * slots * ff),
    )(lengths, x, ctx, cot, w1, w2, vecs, b_in)


def wgrad_body(a_ref, b_ref, o_ref):
    o_ref[...] = dot_tn(a_ref[...], b_ref[...]).astype(BF).reshape(o_ref.shape)


def wgrad_rows(a, b, pieces, tile=256):
    slots, m = a.shape
    width = b.shape[1]
    return pl.pallas_call(
        wgrad_body,
        name="wgrad_rows",
        grid=(m // tile,),
        in_specs=[
            pl.BlockSpec((slots, tile), lambda i: (0, i)),
            pl.BlockSpec((slots, width), lambda i: (0, 0)),
        ],
        out_specs=pl.BlockSpec((tile, width), lambda i: (i, 0)),
        out_shape=jax.ShapeDtypeStruct((m, width), BF),
        compiler_params=params(48),
        cost_estimate=cost(2 * slots * m * width, 2 * (slots * (m + width) + m * width)),
    )(a, b)


def wgrad_cols(a, b, pieces, tile=256):
    slots, m = a.shape
    n = b.shape[1] // m
    sub = m // pieces
    per = tile // sub
    return pl.pallas_call(
        wgrad_body,
        name="wgrad_cols",
        grid=(n, m // tile),
        in_specs=[
            pl.BlockSpec((slots, tile), lambda j, i: (0, i)),
            pl.BlockSpec((slots, m), lambda j, i: (0, j)),
        ],
        out_specs=pl.BlockSpec((per, 1, sub, m), lambda j, i: (i, j, 0, 0)),
        out_shape=jax.ShapeDtypeStruct((pieces, n, sub, m), BF),
        compiler_params=params(48),
        cost_estimate=cost(2 * slots * m * m * n, 2 * (slots * m * (n + 1) + m * m * n)),
    )(a, b)


def wgrad3_body(a_ref, q_ref, k_ref, v_ref, o_ref):
    for n, ref in enumerate((q_ref, k_ref, v_ref)):
        o_ref[:, n] = dot_tn(a_ref[...], ref[...]).astype(BF).reshape(o_ref.shape[0], *o_ref.shape[2:])


def wgrad3(a, dq, dk, dv, pieces, tile=256):
    slots, m = a.shape
    sub = m // pieces
    per = tile // sub
    full = pl.BlockSpec((slots, m), lambda i: (0, 0))
    return pl.pallas_call(
        wgrad3_body,
        name="wgrad3",
        grid=(m // tile,),
        in_specs=[pl.BlockSpec((slots, tile), lambda i: (0, i)), full, full, full],
        out_specs=pl.BlockSpec((per, 3, sub, m), lambda i: (i, 0, 0, 0)),
        out_shape=jax.ShapeDtypeStruct((pieces, 3, sub, m), BF),
        compiler_params=params(48),
        cost_estimate=cost(6 * slots * m * m, 14 * slots * m),
    )(a, dq, dk, dv)


def tok_body(g_ref, dq_ref, dk_ref, dv_ref, w_ref, o_ref, w_vm, sem):
    step = pl.program_id(0)
    width = g_ref.shape[1]
    copies = [pltpu.make_async_copy(w_ref.at[:, n], w_vm.at[n], sem.at[n]) for n in range(3)]

    @pl.when(step == 0)
    def _():
        for c in copies:
            c.start()

    acc = g_ref[...].astype(F32)
    for n, ref in enumerate((dq_ref, dk_ref, dv_ref)):
        @pl.when(step == 0)
        def _():
            copies[n].wait()

        acc = acc + dot_nt(ref[...], w_vm[n].reshape(width, width))
    o_ref[...] = acc.astype(BF)


def tok_call(g, dq, dk, dv, w1, rows=256):
    slots, width = g.shape
    pieces, _, sub, _ = w1.shape
    blk = pl.BlockSpec((rows, width), lambda i: (i, 0))
    return pl.pallas_call(
        tok_body,
        name="grad_tok",
        grid=(slots // rows,),
        in_specs=[blk, blk, blk, blk, pl.BlockSpec(memory_space=pl.ANY)],
        out_specs=blk,
        out_shape=jax.ShapeDtypeStruct((slots, width), BF),
        scratch_shapes=[pltpu.VMEM((3, pieces, sub, width), BF), pltpu.SemaphoreType.DMA((3,))],
        compiler_params=params(48),
        cost_estimate=cost(6 * slots * width * width, 16 * slots * width),
    )(g, dq, dk, dv, w1)


SUB = 32
BOTH = ("shard", "replica")


def mine(w, blocks, wide):
    copies = lax.axis_size("replica")
    share = w.shape[0] // copies
    part = lax.dynamic_slice_in_dim(w, lax.axis_index("replica") * share, share, 0)
    if w.shape[1] == wide:
        return part.reshape(blocks, share // blocks, wide)
    return part.reshape(share, blocks, wide).transpose(1, 0, 2)


def spread(packed):
    blocks, rows, wide = packed.shape
    full = lax.all_gather(packed, BOTH, axis=0)
    if rows == SUB:
        return full
    group = SUB // rows
    full = full.reshape(-1, group, blocks, rows, wide).transpose(0, 2, 1, 3, 4)
    return full.reshape(-1, blocks, SUB, wide)


def spread_rows(packed):
    full = lax.all_gather(packed, BOTH, axis=0)
    return full.reshape(-1, 4, SUB, packed.shape[-1])


def collect(grad, devices):
    pieces, blocks, sub, wide = grad.shape
    group = devices // pieces
    rows = sub // group
    if group > 1:
        grad = grad.reshape(pieces, blocks, group, rows, wide).transpose(0, 2, 1, 3, 4)
    grad = grad.reshape(devices, blocks, rows, wide)
    part = lax.psum_scatter(grad, BOTH, scatter_dimension=0, tiled=True)[0]
    part = lax.all_gather(part, "replica", axis=0)
    return part.transpose(0, 2, 1, 3).reshape(-1, blocks * wide).astype(F32)


def collect_rows(grad, devices):
    m, wide = grad.shape
    part = lax.psum_scatter(grad.reshape(devices, m // devices, wide), BOTH, scatter_dimension=0, tiled=True)[0]
    return lax.all_gather(part, "replica", axis=0).reshape(-1, wide).astype(F32)


def shards(
    tokens, lengths, cotangent, w_qkv, b_qv, w_attn_out, b_attn_out, ln1_gain, ln1_bias,
    w_ffn_in, b_ffn_in, w_ffn_out, b_ffn_out, ln2_gain, ln2_bias,
):
    _, slots, width = tokens.shape
    nblk = w_ffn_in.shape[1] // width
    count = lax.axis_size("shard")
    devices = count * lax.axis_size("replica")
    pieces = width // SUB
    x = tokens.reshape(slots, width)
    cot = cotangent.reshape(slots, width)

    first = jnp.concatenate([mine(w_qkv, 3, width), mine(w_attn_out, 1, width)], 0)
    w1 = spread(first)
    if w_ffn_in.shape[0] // lax.axis_size("replica") == SUB:
        w2 = spread(jnp.concatenate([mine(w_ffn_in, nblk, width), mine(w_ffn_out, 4, width)], 0))
    else:
        w2 = jnp.concatenate([spread(mine(w_ffn_in, nblk, width)), spread_rows(mine(w_ffn_out, 4, width))], 1)

    small = [b_qv, b_attn_out, ln1_gain, ln1_bias, b_ffn_in, b_ffn_out, ln2_gain, ln2_bias]
    sizes = [v.shape[0] for v in small]
    ends = [sum(sizes[: i + 1]) for i in range(len(sizes))]
    table = lax.all_gather(jnp.concatenate(small), "shard", axis=0).astype(F32)
    b_qv, bao, gain1, shift1, b_in, bout, gain2, shift2 = [
        table[:, e - s : e].reshape(-1) for s, e in zip(sizes, ends)
    ]
    bias3 = jnp.concatenate([b_qv[:width], jnp.zeros((width,), F32), b_qv[width:]]).reshape(1, -1)
    zero = jnp.zeros((width,), F32)
    vecs = jnp.stack([bao, gain1, shift1, bout, gain2, shift2, zero, zero])

    qkv = qkv_call(x, w1, bias3)
    ctx, qa0, qa1 = attn_fwd_call(qkv, lengths)
    out, act, low, gf, gp, ga, gc, sums, sbin = row_call(
        x, ctx, cot, w1, w2, vecs, b_in.reshape(nblk, width), lengths
    )
    g_wout = collect_rows(wgrad_rows(act, gf, pieces), devices)
    g_win = collect(wgrad_cols(low, gp, pieces), devices)
    g_wao = collect_rows(wgrad_rows(ctx, ga, pieces), devices)
    dq, dk, dv, sq, sv = attn_bwd_call(qa0, qa1, qkv, ctx, gc, lengths)
    g_wqkv = collect(wgrad3(x, dq, dk, dv, pieces), devices)
    g_tok = tok_call(ga, dq, dk, dv, w1)

    parts = [jnp.concatenate([sq[0], sv[0]]), sums[5], sums[3], sums[4], sbin.reshape(-1), sums[2], sums[0], sums[1]]
    table = jnp.concatenate([v.reshape(count, -1) for v in parts], 1)
    table = lax.psum(table, BOTH)
    own = lax.dynamic_index_in_dim(table, lax.axis_index("shard"), 0, keepdims=False)
    g_bqv, g_bao, g_g1, g_s1, g_bin, g_bout, g_g2, g_s2 = [own[e - s : e] for s, e in zip(sizes, ends)]
    return (
        out[None], g_tok[None], g_wqkv, g_bqv, g_wao, g_bao, g_g1, g_s1,
        g_win, g_bin, g_wout, g_bout, g_g2, g_s2,
    )


def solution(mesh):
    rows = P(("replica", "shard"), None, None)
    mat, vec = P("shard", None), P("shard")
    return jax.shard_map(
        shards,
        mesh=mesh,
        in_specs=(rows, P(("replica", "shard")), rows, mat, vec, mat, vec, vec, vec, mat, vec, mat, vec, vec, vec),
        out_specs=(rows, rows, mat, vec, mat, vec, vec, vec, mat, vec, mat, vec, vec, vec),
        check_vma=False,
    )
```

time: 1580 us -> 907 us (0.57)
  matrix products: 357 us -> 0 us
  waiting for transfers between devices: 835 us -> 517 us
  Pallas kernels: 0 us -> 228 us
  other arithmetic: 121 us -> 8.02 us
  blocking collectives: 195 us -> 85.7 us
    dot_general x24 -> x0, matrix products: 357 us -> none  [the longest x2 58.7 us: shards(): jnp.einsum('sqhd,skhd->shqk', ctx_grad_block, value_heads, preferred_elem...]
    reduce_scatter x4, waiting for transfers between devices: 733 us -> 392 us  [the longest x2 228 us: collect_rows(): lax.psum_scatter(grad.reshape(devices, m // devices, wide), BOTH, scatter...]
    pallas_call x0 -> x9, Pallas kernels: none -> 228 us  [the longest x1 61.1 us: row_call(): pl.pallas_call(row_body, name='row_local', grid_spec=pltpu.PrefetchScalar...]
    all_gather x8 -> x3, blocking collectives: 154 us -> 47.9 us  [the longest x1 33.1 us: shards(): table = lax.all_gather(jnp.concatenate(small), 'shard', axis=0).astype(F32)]
    convert_element_type x26 -> x4, other arithmetic: 88.5 us -> 5.27 us  [the longest x2 3.65 us: collect_rows(): return lax.all_gather(part, 'replica', axis=0).reshape(-1, wide).astype(F32)]
    unnamed x1 -> x0, blocking collectives: 35.7 us -> none
    psum x1, blocking collectives: 5.73 us -> 37.8 us  [shards(): table = lax.psum(table, BOTH)]
    reduce_sum x7 -> x0, other arithmetic: 29 us -> none  [the longest x1 14.8 us: shards(): total_exp = jnp.sum(expo, axis=-1, keepdims=True)]
  transfers between devices with their start and end apart: 9 -> 8, of which waited for: 4 -> 8; matrix products, arithmetic and copies ran while one was open for 28% -> 2% of each run, Pallas kernels for 0% -> 16%
where the time goes in v1:
time: 907 us; the launch traced here: 903 us
  waiting for transfers between devices  517 us (57%)
  Pallas kernels  228 us (25%)
  blocking collectives  85.7 us (9%)
  local copies, waits for them, and re-layouts  48.1 us (5%)
  between operations  15.5 us (2%)
    reduce_scatter x2, waiting for transfers between devices, collect_rows(): lax.psum_scatter(grad.reshape(devices, m // devices, wide), BOTH, scatter...  228 us
    reduce_scatter x2, waiting for transfers between devices, collect(): part = lax.psum_scatter(grad, BOTH, scatter_dimension=0, tiled=True)[0]  164 us
    all_gather x2, waiting for transfers between devices, spread(): full = lax.all_gather(packed, BOTH, axis=0)  107 us
    pallas_call x1, Pallas kernels, row_call(): pl.pallas_call(row_body, name='row_local', grid_spec=pltpu.PrefetchScalar...  61.1 us
    pallas_call x1, Pallas kernels, attn_bwd_call(): pl.pallas_call(functools.partial(attn_bwd_body, rows), name='attn_bwd', g...  52 us
    pallas_call x1, Pallas kernels, attn_fwd_call(): pl.pallas_call(functools.partial(attn_fwd_body, rows), name='attn_fwd', g...  38.7 us
    psum x1, blocking collectives, shards(): table = lax.psum(table, BOTH)  37.8 us
    all_gather x1, blocking collectives, shards(): table = lax.all_gather(jnp.concatenate(small), 'shard', axis=0).astype(F32)  33.1 us
  transfers between devices with their start and end apart: 8, of which 8 were waited for; matrix products, arithmetic and copies ran while one was open for 2% of the time, Pallas kernels for 16%

profile of v1, /device:TPU:0, one launch (start us, length us, event | category | flops | bytes accessed | tf_op | source)
XLA Modules:
  0.0 902.6 jit_solution(11570980049334561448)
XLA Ops:
  7.2 1.0 constant_dynamic-slice_fusion.3
  8.6 0.9 dynamic-slice_bitcast_fusion
  9.8 0.8 copy.40
  11.0 1.2 constant_dynamic-slice_fusion.1
  12.3 1.1 pad_maximum_fusion
  15.2 33.1 %all-gather.3 = bf16[8,1,1536]{2,1,0:T(2,128)(2,1)S(1)} all-gather(bf16[1,1,1536]{2,1,0:T(2,128)(2,1)S(1)} %reshape.100), channel_id=3, replica_groups=mesh['replica'=4,'shard'=8] {'shard'}, dimensions={0}, use_global_device_ids=true | all-gather | bytes 27648 | tf_op jit(solution)/shard_map/all_gather | solution.py:512
  49.0 0.6 reshape_reshape.6.bin_ref
  49.7 0.7 stack.7.vec_ref
  50.3 41.4 %all-gather.13.cloned.1.call-done = bf16[128,32,1024]{2,1,0:T(8,128)(2,1)} async-done(((bf16[4,32,1024]{2,1,0:T(8,128)(2,1)}), bf16[128,32,1024]{2,1,0:T(8,128)(2,1)}) %all-gather.13.cloned.1.call-update) | async-done | bytes 8388624 | tf_op jit(solution)/shard_map/all_gather | solution.py:459
  91.8 11.5 %qkv.1.q_ref.k_ref.v_ref = bf16[1024,3072]{1,0:T(8,128)(2,1)} custom-call(bf16[1024,1024]{1,0:T(8,128)(2,1)S(1)} %bitcast.67, bf16[32,4,32,1024]{3,2,1,0:T(8,128)(2,1)} %bitcast.97, f32[1,3072]{1,0:T(1,128)S(1)} %bitcast.65), custom_call_target="tpu_custom_call" | custom-call | flops 6442450944 | bytes 14680064 | tf_op jit(solution)/shard_map/qkv/pallas_call | solution.py:63
  103.2 38.7 %attn_fwd.1 = (bf16[1024,1024]{1,0:T(8,128)(2,1)S(1)}, bf16[1024,1024]{1,0:T(8,128)(2,1)S(1)}, bf16[1024,1024]{1,0:T(8,128)(2,1)}) custom-call(s32[1]{0:T(128)S(6)} %copy.67.len_ref, bf16[1024,3072]{1,0:T(8,128)(2,1)} %qkv.1.q_ref.k_ref.v_ref, bf16[1024,3072]{1,0:T(8,128)(2,1)} %qkv.1.q_ref.k_ref.v_ref, bf16[1024,3072]{1,0:T(8,128)(2,1)} %qkv.1.q_ref.k_ref.v_ref), custom_call_target="tpu_custom_call" | custom-call | flops 17179869184 | bytes 12582912 | tf_op jit(solution)/shard_map/attn_fwd/pallas_call | solution.py:135
  142.0 1.3 copy-done.5
  143.3 1.3 copy-done.12
  144.6 65.6 %all-gather.15.cloned.1.call-done = bf16[256,32,1024]{2,0,1:T(8,128)(2,1)} async-done(((bf16[8,32,1024]{2,0,1:T(8,128)(2,1)}), bf16[256,32,1024]{2,0,1:T(8,128)(2,1)}) %all-gather.15.cloned.1.call-update) | async-done | bytes 16777232 | tf_op jit(solution)/shard_map/all_gather | solution.py:459
  210.2 18.7 %copy.42 = bf16[256,32,1024]{2,1,0:T(8,128)(2,1)} copy(bf16[256,32,1024]{2,0,1:T(8,128)(2,1)} %all-gather.15.cloned.1.call-done) | data formatting | bytes 33554432 | tf_op jit(solution)/shard_map/all_gather | solution.py:459
  228.9 61.1 %row_local.1 = (bf16[1024,1024]{1,0:T(8,128)(2,1)}, bf16[1024,4096]{1,0:T(8,128)(2,1)}, bf16[1024,1024]{1,0:T(8,128)(2,1)}, bf16[1024,1024]{1,0:T(8,128)(2,1)}, ...) custom-call(s32[1]{0:T(128)S(6)} %copy.67.len_ref, ...), custom_call_target="tpu_custom_call" | custom-call | flops 38654705664 | bytes 60817408 | tf_op jit(solution)/shard_map/row_local/pallas_call | solution.py:317
  290.0 1.6 copy-done.11
  291.6 18.5 %wgrad_cols.1 = bf16[32,4,32,1024]{3,2,1,0:T(8,128)(2,1)} custom-call(bf16[1024,1024]{1,0:T(8,128)(2,1)S(1)} %copy-done.11, bf16[1024,4096]{1,0:T(8,128)(2,1)} %get-tuple-element.45.b_ref), custom_call_target="tpu_custom_call" | custom-call | flops 8589934592 | bytes 18874368 | tf_op jit(solution)/shard_map/wgrad_cols/pallas_call | solution.py:370
  310.2 1.5 copy-done.10
  311.7 17.5 %wgrad_rows.3 = bf16[4096,1024]{1,0:T(8,128)(2,1)} custom-call(bf16[1024,4096]{1,0:T(8,128)(2,1)} %get-tuple-element.46.a_ref, bf16[1024,1024]{1,0:T(8,128)(2,1)S(1)} %copy-done.10), custom_call_target="tpu_custom_call" | custom-call | flops 8589934592 | bytes 18874368 | tf_op jit(solution)/shard_map/wgrad_rows/pallas_call | solution.py:350
  329.3 1.5 copy-done.6
  330.8 5.7 wgrad_rows.2
  336.6 52.0 %attn_bwd.1 = (bf16[1024,1024]{1,0:T(8,128)(2,1)S(1)}, bf16[1024,1024]{1,0:T(8,128)(2,1)S(1)}, bf16[1024,1024]{1,0:T(8,128)(2,1)}, f32[1,1024]{1,0:T(1,128)S(1)}, f32[1,1024]{1,0:T(1,128)S(1)}) custom-call(s32[1]{0:T(128)S(6)} %copy.67.len_ref, bf16[1024,1024]{1,0:T(8,128)(2,1)} %copy-done.12, bf16[1024,1024]{1,0:T(8,128)(2,1)} %get-tuple-element.35.qa1_ref, ...), custom_call_target="tpu_custom_call" | custom-call | flops 42949672960 | bytes 18874368 | tf_op jit(solution)/shard_map/attn_bwd/pallas_call | solution.py:205
  388.6 1.3 copy-done.9
  389.9 11.0 %wgrad3.1 = bf16[32,3,32,1024]{3,2,1,0:T(8,128)(2,1)} custom-call(bf16[1024,1024]{1,0:T(8,128)(2,1)S(1)} %bitcast.68, bf16[1024,1024]{1,0:T(8,128)(2,1)S(1)} %get-tuple-element.37.dq_ref.q_ref, bf16[1024,1024]{1,0:T(8,128)(2,1)} %copy-done.9, bf16[1024,1024]{1,0:T(8,128)(2,1)} %get-tuple-element.39.dv_ref.v_ref), custom_call_target="tpu_custom_call" | custom-call | flops 6442450944 | bytes 14680064 | tf_op jit(solution)/shard_map/wgrad3/pallas_call | solution.py:395
  400.9 1.3 copy-done.7
  402.8 0.7 reduce.7
  403.6 0.7 reduce.6
  404.3 53.8 %reduce-scatter.9.cloned.1.call-done = bf16[1,4,32,1024]{3,2,1,0:T(8,128)(2,1)} async-done(((bf16[32,4,32,1024]{3,2,1,0:T(8,128)(2,1)}), bf16[1,4,32,1024]{3,2,1,0:T(8,128)(2,1)}) %reduce-scatter.9.cloned.1.call-update) | async-done | bytes 262160 | tf_op jit(solution)/shard_map/reduce_scatter | solution.py:479
  458.3 1.6 copy-done.8
  459.9 12.0 %grad_tok.1 = bf16[1024,1024]{1,0:T(8,128)(2,1)} custom-call(bf16[1024,1024]{1,0:T(8,128)(2,1)S(1)} %copy-done.4, bf16[1024,1024]{1,0:T(8,128)(2,1)S(1)} %copy-done.8, bf16[1024,1024]{1,0:T(8,128)(2,1)} %copy-done.9, bf16[1024,1024]{1,0:T(8,128)(2,1)} %get-tuple-element.39.dv_ref.v_ref, bf16[32,4,32,1024]{3,2,1,0:T(8,128)(2,1)} %bitcast.99), custom_call_target="tpu_custom_call" | custom-call | flops 6442450944 | bytes 16777216 | tf_op jit(solution)/shard_map/grad_tok/pallas_call | solution.py:431
  471.9 133.0 %reduce-scatter.11.cloned.1.call-done = bf16[1,128,1024]{2,1,0:T(8,128)(2,1)} async-done(((bf16[32,128,1024]{2,1,0:T(8,128)(2,1)}), bf16[1,128,1024]{2,1,0:T(8,128)(2,1)}) %reduce-scatter.11.cloned.1.call-update) | async-done | bytes 262160 | tf_op jit(solution)/shard_map/reduce_scatter | solution.py:486
  605.0 37.8 %psum.7 = f32[8,1536]{1,0:T(8,128)S(1)} all-reduce(f32[8,1536]{1,0:T(8,128)S(1)} %constant_dynamic-update-slice_fusion), channel_id=1, replica_groups=mesh['replica'=4,'shard'=8] {'shard','replica'}, use_global_device_ids=true, to_apply=%region_1.0 | all-reduce | flops 12288 | bytes 98304 | tf_op jit(solution)/shard_map/psum | solution.py:534
  642.8 0.7 dynamic-slice.4
  644.0 0.6 dynamic-slice_bitcast_fusion.1
  644.6 95.2 %reduce-scatter.7.cloned.1.call-done = bf16[1,32,1024]{2,1,0:T(8,128)(2,1)} async-done(((bf16[32,32,1024]{2,1,0:T(8,128)(2,1)}), bf16[1,32,1024]{2,1,0:T(8,128)(2,1)}) %reduce-scatter.7.cloned.1.call-update) | async-done | bytes 65552 | tf_op jit(solution)/shard_map/reduce_scatter | solution.py:486
  739.9 6.0 all_gather.37
  745.8 0.9 bitcast_convert_fusion.1
  746.7 110.0 %reduce-scatter.5.cloned.1.call-done = bf16[1,3,32,1024]{3,2,1,0:T(8,128)(2,1)} async-done(((bf16[32,3,32,1024]{3,2,1,0:T(8,128)(2,1)}), bf16[1,3,32,1024]{3,2,1,0:T(8,128)(2,1)}) %reduce-scatter.5.cloned.1.call-update) | async-done | bytes 196624 | tf_op jit(solution)/shard_map/reduce_scatter | solution.py:479
  856.7 8.8 all_gather.36
  865.7 1.1 copy.43
  866.7 2.4 copy.48
  869.1 5.2 all-gather.9.cloned.1.call-done
  874.3 1.5 convert_bitcast_fusion
  875.8 1.4 copy.44
  877.2 3.0 copy.49
  880.1 12.5 %all-gather.11.cloned.1.call-done = bf16[4,128,1024]{2,1,0:T(8,128)(2,1)} async-done(((bf16[1,128,1024]{2,1,0:T(8,128)(2,1)}), bf16[4,128,1024]{2,1,0:T(8,128)(2,1)}) %all-gather.11.cloned.1.call-update) | async-done | bytes 1048592 | tf_op jit(solution)/shard_map/all_gather | solution.py:487
  892.7 2.8 bitcast_convert_fusion
  (94 shorter events, 4.7 us)
Async XLA Ops:
  7.2 3.6 copy-start
  7.2 84.6 %all-gather.13.cloned.1.call-start = ((), (), s32[]{:S(2)}) async-start(), calls=%async_computation.10 | async-start | bytes 8650752 | tf_op jit(solution)/shard_map/all_gather | solution.py:459
  10.6 2.9 copy-start.16
  10.6 3.1 copy-start.17
  10.6 3.4 copy-start.18
  10.6 3.6 copy-start.19
  10.6 3.8 copy-start.15
  10.6 4.0 copy-start.20
  10.6 4.2 copy-start.21
  10.6 4.4 copy-start.22
  10.7 81.1 %copy-start.2 = (bf16[1,1024,1024]{2,1,0:T(8,128)(2,1)S(1)}, bf16[1,1024,1024]{2,1,0:T(8,128)(2,1)}, u32[]{:S(2)}) copy-start(bf16[1,1024,1024]{2,1,0:T(8,128)(2,1)} %param.15) | copy-start | bytes 6291460
  10.7 199.6 %all-gather.15.cloned.1.call-start = ((), (), s32[]{:S(2)}) async-start(), calls=%async_computation.11 | async-start | bytes 17301504 | tf_op jit(solution)/shard_map/all_gather | solution.py:459
  13.4 444.7 %reduce-scatter.9.cloned.1.call-start = ((), (), s32[]{:S(2)}) async-start(), calls=%async_computation.6 | async-start | bytes 8650752 | tf_op jit(solution)/shard_map/reduce_scatter | solution.py:479
  142.0 1.3 copy-start.5
  143.3 1.3 copy-start.12
  290.0 1.6 copy-start.11
  310.1 1.6 copy-start.10
  310.1 294.8 %reduce-scatter.11.cloned.1.call-start = ((), (), s32[]{:S(2)}) async-start(), calls=%async_computation.8 | async-start | bytes 8650752 | tf_op jit(solution)/shard_map/reduce_scatter | solution.py:486
  329.2 1.6 copy-start.6
  329.2 410.6 %reduce-scatter.7.cloned.1.call-start = ((), (), s32[]{:S(2)}) async-start(), calls=%async_computation.5 | async-start | bytes 2162688 | tf_op jit(solution)/shard_map/reduce_scatter | solution.py:486
  336.5 520.2 %reduce-scatter.5.cloned.1.call-start = ((), (), s32[]{:S(2)}) async-start(), calls=%async_computation.4 | async-start | bytes 6488064 | tf_op jit(solution)/shard_map/reduce_scatter | solution.py:479
  336.6 53.4 %copy-start.3 = (bf16[1,1024,1024]{2,1,0:T(8,128)(2,1)S(1)}, bf16[1,1024,1024]{2,1,0:T(8,128)(2,1)}, u32[]{:S(2)}) copy-start(bf16[1,1024,1024]{2,1,0:T(8,128)(2,1)} %param.15) | copy-start | bytes 6291460
  388.6 1.3 copy-start.9
  400.9 1.3 copy-start.7
  402.2 2.0 copy-start.14
  402.2 55.9 %copy-start.13 = (f32[8,1024]{1,0:T(8,128)S(1)}, f32[8,1024]{1,0:T(8,128)}, u32[]{:S(2)}) copy-start(f32[8,1024]{1,0:T(8,128)} %get-tuple-element.42) | copy-start | bytes 98308
  402.2 56.0 %copy-start.4 = (bf16[1024,1024]{1,0:T(8,128)(2,1)S(1)}, bf16[1024,1024]{1,0:T(8,128)(2,1)}, u32[]{:S(2)}) copy-start(bf16[1024,1024]{1,0:T(8,128)(2,1)} %get-tuple-element.33.g_ref.b_ref) | copy-start | bytes 6291460
  402.3 472.1 %all-gather.9.cloned.1.call-start = ((), (), s32[]{:S(2)}) async-start(), calls=%async_computation.7 | async-start | bytes 1310720 | tf_op jit(solution)/shard_map/all_gather | solution.py:480
  458.1 434.6 %all-gather.11.cloned.1.call-start = ((), (), s32[]{:S(2)}) async-start(), calls=%async_computation.9 | async-start | bytes 1310720 | tf_op jit(solution)/shard_map/all_gather | solution.py:487
  458.3 1.6 copy-start.8
  877.2 18.3 %copy-start.1 = (bf16[128,4096]{1,0:T(8,128)(2,1)S(1)}, bf16[128,4096]{1,0:T(8,128)(2,1)}, u32[]{:S(2)}) copy-start(bf16[128,4096]{1,0:T(8,128)(2,1)} %param.24) | copy-start | bytes 3145732
Sparse Core Ops, SparseCore 0:
  11.5 80.2 all-gather.12
  95.3 114.9 all-gather.14
  310.2 147.7 reduce-scatter.8
  460.2 144.6 reduce-scatter.10
  607.0 132.7 reduce-scatter.6
  746.3 110.3 reduce-scatter.4
  858.3 16.0 all-gather.8
  875.9 16.7 all-gather.10

commit v2 on v1

v2 whole, which is shorter than its diff:
```python
import functools
import jax
import jax.numpy as jnp
from jax import lax
from jax.experimental import pallas as pl
from jax.experimental.pallas import tpu as pltpu
from jax.sharding import PartitionSpec as P

HD = 64
F32 = jnp.float32
BF = jnp.bfloat16
SQRT_HALF = 0.7071067811865476
INV_ROOT_TAU = 0.3989422804014327


def params():
    return pltpu.CompilerParams(vmem_limit_bytes=60 << 20)


def dot_nn(a, b):
    return jnp.dot(a, b, preferred_element_type=F32)


def dot_nt(a, b):
    return lax.dot_general(a, b, (((1,), (1,)), ((), ())), preferred_element_type=F32)


def dot_tn(a, b):
    return lax.dot_general(a, b, (((0,), (0,)), ((), ())), preferred_element_type=F32)


def cost(flops, nbytes, trans=0):
    return pl.CostEstimate(flops=int(flops), bytes_accessed=int(nbytes), transcendentals=int(trans))


SUB = 32
ANY = pl.BlockSpec(memory_space=pltpu.HBM)


def loads(place, bufs, lo, hi, target, sem):
    found = []
    for buf in bufs:
        for m in range(buf.shape[0]):
            i = len(found)
            found.append(pltpu.make_async_copy(buf.at[m, pl.ds(lo, hi - lo)], target(place[i]), sem.at[i]))
    return found


def start_all(copies):
    for c in copies:
        c.start()


def wait_all(copies):
    for c in copies:
        c.wait()


def qkv_body(count, place, x_ref, b_ref, *rest):
    bufs, (o_ref, w_vm, sem) = rest[:count], rest[count:]
    step = pl.program_id(0)
    blocks, width = w_vm.shape[0], w_vm.shape[-1]
    copies = loads(place, bufs, 0, blocks, lambda p: w_vm.at[:, p], sem)

    @pl.when(step == 0)
    def _():
        start_all(copies)
        wait_all(copies)

    x = x_ref[...]
    for n in range(blocks):
        w = w_vm[n].reshape(-1, width)
        bias = b_ref[:, n * width : (n + 1) * width]
        o_ref[:, n * width : (n + 1) * width] = (dot_nn(x, w) + bias).astype(BF)


def qkv_call(x, place, w1, bias, rows=256):
    slots, width = x.shape
    pieces = width // SUB
    return pl.pallas_call(
        functools.partial(qkv_body, len(w1)),
        name="qkv",
        grid_spec=pltpu.PrefetchScalarGridSpec(
            num_scalar_prefetch=1,
            grid=(slots // rows,),
            in_specs=[
                pl.BlockSpec((rows, width), lambda i, p: (i, 0)),
                pl.BlockSpec((1, 3 * width), lambda i, p: (0, 0)),
            ] + [ANY] * len(w1),
            out_specs=pl.BlockSpec((rows, 3 * width), lambda i, p: (i, 0)),
            scratch_shapes=[
                pltpu.VMEM((3, pieces, SUB, width), BF),
                pltpu.SemaphoreType.DMA((pieces,)),
            ],
        ),
        out_shape=jax.ShapeDtypeStruct((slots, 3 * width), BF),
        compiler_params=params(),
        cost_estimate=cost(6 * slots * width * width, 8 * slots * width + 6 * width * width),
    )(place, x, bias, *w1)


def lanes(rows):
    return lax.broadcasted_iota(jnp.int32, (rows, 2 * HD), 1)


def split3(v):
    hi = v.astype(BF).astype(F32)
    mid = (v - hi).astype(BF).astype(F32)
    return hi, mid, v - hi - mid


def attn_fwd_body(rows, len_ref, q_ref, k_ref, v_ref, *rest):
    ctx_ref, qa0_ref, qa1_ref = rest[-3:]
    slots = k_ref.shape[0]
    lane = lanes(slots)
    key_row = lax.broadcasted_iota(jnp.int32, (slots, 2 * HD), 0)
    bias = jnp.where(key_row < len_ref[0], 0.0, -1e30)
    k = k_ref[...].astype(F32)
    k_aug = []
    for h in range(2):
        own = (lane // HD) == h
        spare = (1 - h) * HD
        k_aug.append(jnp.where(own, k, jnp.where(lane == spare, bias, 0.0)).astype(BF))
    v = v_ref[...]
    lane_q = lanes(rows)

    for blk in range(slots // rows):
        sl = slice(blk * rows, (blk + 1) * rows)
        q = q_ref[sl, :].astype(F32) * 0.125
        outs = []
        for h, qa_ref in enumerate((qa0_ref, qa1_ref)):
            own = (lane_q // HD) == h
            spare = (1 - h) * HD
            qh = jnp.where(own, q, jnp.where(lane_q == spare, 1.0, 0.0))
            s = dot_nt(qh.astype(BF), k_aug[h])
            top = jnp.max(s, axis=-1, keepdims=True)
            e = jnp.exp(s - top)
            total = jnp.sum(e, axis=-1, keepdims=True)
            o = dot_nn(e.astype(BF), v) / total
            outs.append(o)
            hi, mid, lo = split3(-(top + jnp.log(total)))
            qh = jnp.where(lane_q == spare + 1, hi, qh)
            qh = jnp.where(lane_q == spare + 2, mid, qh)
            qh = jnp.where(lane_q == spare + 3, lo, qh)
            qa_ref[sl, :] = qh.astype(BF)
        ctx_ref[sl, :] = jnp.where(lane_q < HD, outs[0], outs[1]).astype(BF)


def attn_fwd_call(qkv, lengths, part, parts, before, rows=256):
    slots, wide = qkv.shape
    width = wide // 3
    pairs = width // (2 * HD)
    each = pairs // parts
    col = lambda off: pl.BlockSpec((slots, 2 * HD), lambda j, ln: (0, off * pairs + part * each + j))
    out = jax.ShapeDtypeStruct((slots, width), BF)
    extra = list(before or ())
    return pl.pallas_call(
        functools.partial(attn_fwd_body, rows),
        name=f"attn_fwd{part}",
        grid_spec=pltpu.PrefetchScalarGridSpec(
            num_scalar_prefetch=1,
            grid=(each,),
            in_specs=[col(0), col(1), col(2)] + [ANY] * len(extra),
            out_specs=[col(0)] * 3,
        ),
        out_shape=[out, out, out],
        input_output_aliases={4 + i: i for i in range(3)} if before else {},
        compiler_params=params(),
        cost_estimate=cost(
            16 * slots * slots * width / parts, 12 * slots * width / parts, slots * slots * 2 * each
        ),
    )(lengths, qkv, qkv, qkv, *extra)


def attn_bwd_body(rows, len_ref, qa0_ref, qa1_ref, k_ref, v_ref, ctx_ref, g_ref, *rest):
    dq_ref, dk_ref, dv_ref, sq_ref, sv_ref = rest[-5:]
    slots = k_ref.shape[0]
    lane = lanes(slots)
    key_row = lax.broadcasted_iota(jnp.int32, (slots, 2 * HD), 0)
    bias = jnp.where(key_row < len_ref[0], 0.0, -1e30)
    k = k_ref[...].astype(F32)
    v = v_ref[...].astype(F32)
    k_low = k_ref[...]
    k_aug, v_aug = [], []
    for h in range(2):
        own = (lane // HD) == h
        spare = (1 - h) * HD
        near = (lane > spare) & (lane < spare + 4)
        ones = jnp.where(near, 1.0, 0.0)
        k_aug.append(jnp.where(own, k, jnp.where(lane == spare, bias, ones)).astype(BF))
        v_aug.append(jnp.where(own, v, ones).astype(BF))
    lane_q = lanes(rows)
    dk = [jnp.zeros((slots, 2 * HD), F32)] * 2
    dv = [jnp.zeros((slots, 2 * HD), F32)] * 2
    for blk in range(slots // rows):
        sl = slice(blk * rows, (blk + 1) * rows)
        g_low = g_ref[sl, :]
        g = g_low.astype(F32)
        prod = g * ctx_ref[sl, :].astype(F32)
        dqs = []
        for h, qa_ref in enumerate((qa0_ref, qa1_ref)):
            own = (lane_q // HD) == h
            spare = (1 - h) * HD
            delta = jnp.sum(jnp.where(own, prod, 0.0), axis=-1, keepdims=True)
            hi, mid, lo = split3(-delta)
            ga = jnp.where(own, g, 0.0)
            ga = jnp.where(lane_q == spare + 1, hi, ga)
            ga = jnp.where(lane_q == spare + 2, mid, ga)
            ga = jnp.where(lane_q == spare + 3, lo, ga).astype(BF)
            qa = qa_ref[sl, :]
            p = jnp.exp(dot_nt(k_aug[h], qa))
            ds = (p * dot_nt(v_aug[h], ga)).astype(BF)
            dv[h] = dv[h] + dot_nn(p.astype(BF), g_low)
            dk[h] = dk[h] + dot_nn(ds, qa)
            dqs.append(dot_tn(ds, k_low))
        dq_ref[sl, :] = (jnp.where(lane_q < HD, dqs[0], dqs[1]) * 0.125).astype(BF)
    dk_ref[...] = jnp.where(lane < HD, dk[0], dk[1]).astype(BF)
    dv_low = jnp.where(lane < HD, dv[0], dv[1]).astype(BF)
    dv_ref[...] = dv_low
    sq_ref[...] = jnp.sum(dq_ref[...].astype(F32), axis=0, keepdims=True)
    sv_ref[...] = jnp.sum(dv_low.astype(F32), axis=0, keepdims=True)


def attn_bwd_call(qa0, qa1, qkv, ctx, grad_ctx, lengths, part, parts, before, rows=256):
    slots, width = ctx.shape
    pairs = width // (2 * HD)
    each = pairs // parts
    col = lambda off: pl.BlockSpec((slots, 2 * HD), lambda j, ln: (0, off * pairs + part * each + j))
    row = pl.BlockSpec((1, 2 * HD), lambda j, ln: (0, part * each + j))
    out = jax.ShapeDtypeStruct((slots, width), BF)
    vec = jax.ShapeDtypeStruct((1, width), F32)
    extra = list(before or ())
    return pl.pallas_call(
        functools.partial(attn_bwd_body, rows),
        name=f"attn_bwd{part}",
        grid_spec=pltpu.PrefetchScalarGridSpec(
            num_scalar_prefetch=1,
            grid=(each,),
            in_specs=[col(0), col(0), col(1), col(2), col(0), col(0)] + [ANY] * len(extra),
            out_specs=[col(0)] * 3 + [row] * 2,
        ),
        out_shape=[out, out, out, vec, vec],
        input_output_aliases={7 + i: i for i in range(5)} if before else {},
        compiler_params=params(),
        cost_estimate=cost(
            40 * slots * slots * width / parts, 18 * slots * width / parts, slots * slots * 2 * each
        ),
    )(lengths, qa0, qa1, qkv, qkv, ctx, grad_ctx, *extra)


def norm_stats(resid):
    mean = jnp.mean(resid, axis=-1, keepdims=True)
    centred = resid - mean
    inv = lax.rsqrt(jnp.mean(centred * centred, axis=-1, keepdims=True) + 1e-5)
    return centred * inv, inv


def norm_back(u, normed, inv):
    return inv * (u - jnp.mean(u, axis=-1, keepdims=True) - normed * jnp.mean(u * normed, axis=-1, keepdims=True))


def colsum(v):
    return jnp.sum(v, axis=0, keepdims=True)


def row_body(n2, len_ref, place, x_ref, ctx_ref, cot_ref, vec_ref, bin_ref, *rest):
    b2 = rest[:n2]
    (
        out_ref, act_ref, hid_ref, gf_ref, gp_ref, ga_ref, gc_ref, sums_ref, sbin_ref,
        wa, wi, wo, slope, sem,
    ) = rest[n2:]
    step = pl.program_id(0)
    rows, width = x_ref.shape
    nblk = wi.shape[0]
    copies = [
        loads(place, b2, 0, 1, lambda p: wa.at[pl.ds(p, 1)], sem.at[0]),
        loads(place, b2, 1, 1 + nblk, lambda p: wi.at[:, p], sem.at[1]),
        loads(place, b2, 1 + nblk, 5 + nblk, lambda p: wo.at[p], sem.at[2]),
    ]

    @pl.when(step == 0)
    def _():
        for c in copies:
            start_all(c)
        sums_ref[...] = jnp.zeros_like(sums_ref)
        sbin_ref[...] = jnp.zeros_like(sbin_ref)

    def ready(i):
        @pl.when(step == 0)
        def _():
            wait_all(copies[i])

    bao, gain1, shift1, bout, gain2, shift2 = [vec_ref[i : i + 1, :] for i in range(6)]
    ready(0)
    w_ao = wa[...].reshape(width, width)
    resid1 = x_ref[...].astype(F32) + dot_nn(ctx_ref[...], w_ao) + bao
    normed1, inv1 = norm_stats(resid1)
    hidden = normed1 * gain1 + shift1
    low = hidden.astype(BF)
    hid_ref[...] = low
    acc = jnp.zeros((rows, width), F32)
    per = wo.shape[0] // nblk
    ready(1)
    for n in range(nblk):
        pre = dot_nn(low, wi[n].reshape(width, width)) + bin_ref[n : n + 1, :]
        phi = 0.5 + 0.5 * lax.erf(pre * SQRT_HALF)
        slope[n] = phi + pre * (INV_ROOT_TAU * jnp.exp(-0.5 * pre * pre))
        act = (pre * phi).astype(BF)
        act_ref[:, n * width : (n + 1) * width] = act
        if n == 0:
            ready(2)
        acc = acc + dot_nn(act, wo[n * per : (n + 1) * per].reshape(width, width))
    resid2 = hidden + acc + bout
    normed2, inv2 = norm_stats(resid2)
    row_id = lax.broadcasted_iota(jnp.int32, (rows, 1), 0) + step * rows
    valid = (row_id < len_ref[0]).astype(F32)
    out_ref[...] = ((normed2 * gain2 + shift2) * valid).astype(BF)
    gz = cot_ref[...].astype(F32) * valid
    sums_ref[0:1, :] += colsum(gz * normed2)
    sums_ref[1:2, :] += colsum(gz)
    g_resid2 = norm_back(gz * gain2, normed2, inv2)
    gf = g_resid2.astype(BF)
    gf_ref[...] = gf
    sums_ref[2:3, :] += colsum(gf.astype(F32))
    acc = g_resid2
    for n in range(nblk):
        g_act = dot_nt(gf, wo[n * per : (n + 1) * per].reshape(width, width))
        gp = (g_act * slope[n]).astype(BF)
        gp_ref[:, n * width : (n + 1) * width] = gp
        sbin_ref[n : n + 1, :] += colsum(gp.astype(F32))
        acc = acc + dot_nt(gp, wi[n].reshape(width, width))
    sums_ref[3:4, :] += colsum(acc * normed1)
    sums_ref[4:5, :] += colsum(acc)
    g_attn = norm_back(acc * gain1, normed1, inv1).astype(BF)
    ga_ref[...] = g_attn
    sums_ref[5:6, :] += colsum(g_attn.astype(F32))
    gc_ref[...] = dot_nt(g_attn, w_ao).astype(BF)


def row_call(x, ctx, cot, place, w2, vecs, b_in, lengths, rows=256):
    slots, width = x.shape
    pieces, sub = width // SUB, SUB
    nblk = b_in.shape[0]
    ff = nblk * width
    blk = pl.BlockSpec((rows, width), lambda i, ln, p: (i, 0))
    big = pl.BlockSpec((rows, ff), lambda i, ln, p: (i, 0))
    const = lambda r: pl.BlockSpec((r, width), lambda i, ln, p: (0, 0))
    o = jax.ShapeDtypeStruct((slots, width), BF)
    ob = jax.ShapeDtypeStruct((slots, ff), BF)
    return pl.pallas_call(
        functools.partial(row_body, len(w2)),
        name="row_local",
        grid_spec=pltpu.PrefetchScalarGridSpec(
            num_scalar_prefetch=2,
            grid=(slots // rows,),
            in_specs=[blk, blk, blk, const(8), const(nblk)] + [ANY] * len(w2),
            out_specs=[blk, big, blk, blk, big, blk, blk, const(8), const(nblk)],
            scratch_shapes=[
                pltpu.VMEM((pieces, sub, width), BF),
                pltpu.VMEM((nblk, pieces, sub, width), BF),
                pltpu.VMEM((pieces, 4, sub, width), BF),
                pltpu.VMEM((nblk, rows, width), F32),
                pltpu.SemaphoreType.DMA((3, pieces)),
            ],
        ),
        out_shape=[
            o, ob, o, o, ob, o, o,
            jax.ShapeDtypeStruct((8, width), F32),
            jax.ShapeDtypeStruct((nblk, width), F32),
        ],
        compiler_params=params(),
        cost_estimate=cost(36 * slots * width * width, 40 * slots * width + 18 * width * width, 2 * slots * ff),
    )(lengths, place, x, ctx, cot, vecs, b_in, *w2)


def halves(core, value, group, keep_ref, send_ref):
    value = value.reshape(-1, 2, group, SUB, value.shape[-1])
    even, odd = value[:, 0], value[:, 1]
    shape = keep_ref.shape

    @pl.when(core == 0)
    def _():
        keep_ref[...] = even.reshape(shape)
        send_ref[...] = odd.reshape(shape)

    @pl.when(core != 0)
    def _():
        keep_ref[...] = odd.reshape(shape)
        send_ref[...] = even.reshape(shape)


def wgrad_body(group, core, a_ref, b_ref, keep_ref, send_ref):
    halves(core[0], dot_tn(a_ref[...], b_ref[...]).astype(BF), group, keep_ref, send_ref)


def wgrad_call(name, core, a, b, by_rows, tile=256):
    slots, m = a.shape
    width = a.shape[1] if not by_rows else b.shape[1]
    blocks = m // width if by_rows else b.shape[1] // m
    pieces = width // SUB
    if by_rows:
        group, grid = blocks, (1, m // tile)
        block = (tile // (2 * SUB * blocks), blocks, SUB, width)
        where = lambda j, i, c: (i, 0, 0, 0)
    else:
        group, grid = 1, (blocks, m // tile)
        block = (tile // (2 * SUB), 1, SUB, width)
        where = lambda j, i, c: (i, j, 0, 0)
    out = jax.ShapeDtypeStruct((pieces // 2, blocks, SUB, width), BF)
    return pl.pallas_call(
        functools.partial(wgrad_body, group),
        name=name,
        grid_spec=pltpu.PrefetchScalarGridSpec(
            num_scalar_prefetch=1,
            grid=grid,
            in_specs=[
                pl.BlockSpec((slots, tile), lambda j, i, c: (0, i)),
                pl.BlockSpec((slots, width), lambda j, i, c: (0, j)),
            ],
            out_specs=[pl.BlockSpec(block, where)] * 2,
        ),
        out_shape=[out, out],
        compiler_params=params(),
        cost_estimate=cost(2 * slots * m * b.shape[1], 2 * (slots * (m + b.shape[1]) + m * b.shape[1])),
    )(core, a, b)


def wgrad3_body(core, a_ref, q_ref, k_ref, v_ref, keep_ref, send_ref):
    for n, ref in enumerate((q_ref, k_ref, v_ref)):
        value = dot_tn(a_ref[...], ref[...]).astype(BF)
        halves(core[0], value, 1, keep_ref.at[:, pl.ds(n, 1)], send_ref.at[:, pl.ds(n, 1)])


def wgrad3(core, a, dq, dk, dv, tile=256):
    slots, m = a.shape
    full = pl.BlockSpec((slots, m), lambda i, c: (0, 0))
    block = pl.BlockSpec((tile // (2 * SUB), 3, SUB, m), lambda i, c: (i, 0, 0, 0))
    out = jax.ShapeDtypeStruct((m // SUB // 2, 3, SUB, m), BF)
    return pl.pallas_call(
        wgrad3_body,
        name="wgrad_qkv",
        grid_spec=pltpu.PrefetchScalarGridSpec(
            num_scalar_prefetch=1,
            grid=(m // tile,),
            in_specs=[pl.BlockSpec((slots, tile), lambda i, c: (0, i)), full, full, full],
            out_specs=[block, block],
        ),
        out_shape=[out, out],
        compiler_params=params(),
        cost_estimate=cost(6 * slots * m * m, 14 * slots * m),
    )(core, a, dq, dk, dv)


def tok_body(count, place, g_ref, dq_ref, dk_ref, dv_ref, *rest):
    bufs, (o_ref, w_vm, sem) = rest[:count], rest[count:]
    step = pl.program_id(0)
    width = g_ref.shape[1]
    copies = loads(place, bufs, 0, 3, lambda p: w_vm.at[:, p], sem)

    @pl.when(step == 0)
    def _():
        start_all(copies)
        wait_all(copies)

    acc = g_ref[...].astype(F32)
    for n, ref in enumerate((dq_ref, dk_ref, dv_ref)):
        acc = acc + dot_nt(ref[...], w_vm[n].reshape(width, width))
    o_ref[...] = acc.astype(BF)


def tok_call(g, dq, dk, dv, place, w1, rows=256):
    slots, width = g.shape
    pieces = width // SUB
    blk = pl.BlockSpec((rows, width), lambda i, p: (i, 0))
    return pl.pallas_call(
        functools.partial(tok_body, len(w1)),
        name="grad_tok",
        grid_spec=pltpu.PrefetchScalarGridSpec(
            num_scalar_prefetch=1,
            grid=(slots // rows,),
            in_specs=[blk, blk, blk, blk] + [ANY] * len(w1),
            out_specs=blk,
            scratch_shapes=[pltpu.VMEM((3, pieces, SUB, width), BF), pltpu.SemaphoreType.DMA((pieces,))],
        ),
        out_shape=jax.ShapeDtypeStruct((slots, width), BF),
        compiler_params=params(),
        cost_estimate=cost(6 * slots * width * width, 16 * slots * width),
    )(place, g, dq, dk, dv, *w1)


def total(*terms):
    acc = terms[0].astype(F32)
    for t in terms[1:]:
        acc = acc + t.astype(F32)
    return acc.astype(BF)


def add1_body(count, here, *refs):
    ins, outs = refs[: 8 * count], refs[8 * count :]
    for view in range(4):
        n0 = 0
        for i in range(count):
            a, b = ins[8 * i + 2 * view], ins[8 * i + 2 * view + 1]
            n = a.shape[3]
            outs[view][0, n0 : n0 + n] = total(a[0, 0, 0], b[0, 0, 0])
            n0 += n


def add1(here, pairs):
    width = pairs[0][0].shape[-1]
    views = []
    for half, own in ((0, 0), (0, 1), (1, 0), (1, 1)):
        def where(t, h, half=half, own=own):
            z, j = 2 * half + t // 2, t % 2
            if half == 0:
                return (z, j, h[0] if own else 1 - h[0], 0, 0, 0)
            return (z, h[1] if own else 1 - h[1], j, 0, 0, 0)
        views.append(where)
    specs, args, blocks = [], [], 0
    for keep, got in pairs:
        n = keep.shape[1]
        blocks += n
        for where in views:
            for arr in (keep, got):
                specs.append(pl.BlockSpec((1, 1, 1, n, SUB, width), where))
                args.append(arr.reshape(4, 2, 2, n, SUB, width))
    out = jax.ShapeDtypeStruct((4, blocks, SUB, width), BF)
    return pl.pallas_call(
        functools.partial(add1_body, len(pairs)),
        name="add_core",
        grid_spec=pltpu.PrefetchScalarGridSpec(
            num_scalar_prefetch=1,
            grid=(4,),
            in_specs=specs,
            out_specs=[pl.BlockSpec((1, blocks, SUB, width), lambda t, h: (t, 0, 0, 0))] * 4,
        ),
        out_shape=[out] * 4,
        compiler_params=params(),
        cost_estimate=cost(16 * blocks * SUB * width, 96 * blocks * SUB * width),
    )(here, *args)


def add2_body(here, *refs):
    ins, outs = refs[:8], refs[-4:]
    for view in range(4):
        outs[view][0] = total(ins[2 * view][0, 0], ins[2 * view + 1][0, 0])


def add2(here, first, second):
    _, blocks, _, width = first[0].shape
    specs, args = [], []
    for axis, pair in ((1, first), (0, second)):
        for own in (0, 1):
            for arr in pair:
                specs.append(pl.BlockSpec(
                    (1, 1, blocks, SUB, width),
                    lambda t, h, axis=axis, own=own: (t, h[axis] if own else 1 - h[axis], 0, 0, 0),
                ))
                args.append(arr.reshape(2, 2, blocks, SUB, width))
    out = jax.ShapeDtypeStruct((2, blocks, SUB, width), BF)
    return pl.pallas_call(
        add2_body,
        name="add_plane",
        grid_spec=pltpu.PrefetchScalarGridSpec(
            num_scalar_prefetch=1,
            grid=(2,),
            in_specs=specs,
            out_specs=[pl.BlockSpec((1, blocks, SUB, width), lambda t, h: (t, 0, 0, 0))] * 4,
        ),
        out_shape=[out] * 4,
        compiler_params=params(),
        cost_estimate=cost(8 * blocks * SUB * width, 48 * blocks * SUB * width),
    )(here, *args)


def add3_body(here, ak, ag, bk, bg, *outs):
    for k, out in enumerate(outs):
        to = lax.rem(here[2] + k, 4)
        spot = lax.rem(to, 2)

        @pl.when(to < 2)
        def _():
            out[0] = total(ak[spot], ag[spot])

        @pl.when(to >= 2)
        def _():
            out[0] = total(bk[spot], bg[spot])


def add3(here, first, second):
    _, blocks, _, width = first[0].shape
    full = pl.BlockSpec((2, blocks, SUB, width), lambda t, h: (0, 0, 0, 0))
    one = pl.BlockSpec((1, blocks, SUB, width), lambda t, h: (0, 0, 0, 0))
    return pl.pallas_call(
        add3_body,
        name="add_z",
        grid_spec=pltpu.PrefetchScalarGridSpec(
            num_scalar_prefetch=1, grid=(1,), in_specs=[full] * 4, out_specs=[one] * 4,
        ),
        out_shape=[jax.ShapeDtypeStruct((1, blocks, SUB, width), BF)] * 4,
        compiler_params=params(),
        cost_estimate=cost(4 * blocks * SUB * width, 24 * blocks * SUB * width),
    )(here, *first, *second)


def add4_body(*refs):
    ins, out = refs[:-1], refs[-1]
    n0 = 0
    for i in range(0, len(ins), 4):
        n = ins[i].shape[1]
        out[:, n0 : n0 + n] = total(*[r[...] for r in ins[i : i + 4]])
        n0 += n


def add4(*groups):
    spec = lambda shape: pl.BlockSpec(shape, lambda t: (0,) * len(shape))
    _, _, sub, width = groups[0][0].shape
    shape = (1, sum(g[0].shape[1] for g in groups), sub, width)
    parts = [v for g in groups for v in g]
    size = shape[1] * sub * width
    return pl.pallas_call(
        add4_body,
        name="add_last",
        grid=(1,),
        in_specs=[spec(v.shape) for v in parts],
        out_specs=spec(shape),
        out_shape=jax.ShapeDtypeStruct(shape, BF),
        compiler_params=params(),
        cost_estimate=cost(3 * size, 10 * size),
    )(*parts)


def final_body(kinds, here, own, core, over_x, both, *outs):
    mine_at = 2 * here[0] + here[3]
    for flip, ref in enumerate((own, core, over_x, both)):
        share = jnp.bitwise_xor(mine_at, flip)
        n0 = 0
        for (blocks, by_rows), out in zip(kinds, outs):
            width = ref.shape[-1]
            for n in range(blocks):
                value = ref[0, n0 + n].astype(F32)
                if by_rows:
                    out[pl.ds(pl.multiple_of(share * blocks * SUB, SUB) + n * SUB, SUB), :] = value
                else:
                    out[pl.ds(pl.multiple_of(share * SUB, SUB), SUB), n * width : (n + 1) * width] = value
            n0 += blocks


def final_call(here, parts, kinds):
    shape = parts[0].shape
    width = shape[-1]
    shapes = [
        (4 * blocks * SUB, width) if by_rows else (4 * SUB, blocks * width) for blocks, by_rows in kinds
    ]
    return pl.pallas_call(
        functools.partial(final_body, kinds),
        name="final",
        grid_spec=pltpu.PrefetchScalarGridSpec(
            num_scalar_prefetch=1,
            grid=(1,),
            in_specs=[pl.BlockSpec(shape, lambda t, h: (0, 0, 0, 0))] * 4,
            out_specs=[pl.BlockSpec(sh, lambda t, h: (0, 0)) for sh in shapes],
        ),
        out_shape=[jax.ShapeDtypeStruct(sh, F32) for sh in shapes],
        compiler_params=params(),
        cost_estimate=cost(1, 24 * parts[0].size),
    )(here, *parts)


BOTH = ("shard", "replica")
AXES = ("replica", "shard")


def table(fn):
    pairs = []
    for r in range(4):
        for s in range(8):
            x, y, z, c = fn(r // 2, s % 2, s // 2, r % 2)
            pairs.append((r * 8 + s, (x * 2 + c) * 8 + z * 2 + y))
    return pairs


TO_CORE = table(lambda x, y, z, c: (x, y, z, 1 - c))
TO_X = table(lambda x, y, z, c: (1 - x, y, z, c))
TO_XCORE = table(lambda x, y, z, c: (1 - x, y, z, 1 - c))
TO_Y = table(lambda x, y, z, c: (x, 1 - y, z, c))
TO_Z = [table(lambda x, y, z, c, k=k: (x, y, (z + k) % 4, c)) for k in range(4)]


def move(v, pairs):
    return lax.ppermute(v, AXES, pairs)


def regular():
    return lax.axis_size("shard") == 8 and lax.axis_size("replica") == 4


def place_of():
    r, s = lax.axis_index("replica"), lax.axis_index("shard")
    return r // 2, s % 2, s // 2, r % 2


def pack_body(count, share, *refs):
    ins, smalls, outs = refs[:count], refs[count:-2], refs[-2:]
    out, line = outs
    width = out.shape[-1]
    n0 = 0
    for ref in ins:
        rows, cols = ref.shape
        if rows > SUB:
            out[0, n0 : n0 + rows // SUB] = ref[...].reshape(rows // SUB, SUB, width)
            n0 += rows // SUB
        else:
            for n in range(cols // width):
                out[0, n0 + n] = ref[:, n * width : (n + 1) * width]
            n0 += cols // width
    n0 = 0
    for ref in smalls:
        line[:, n0 : n0 + ref.shape[1]] = ref[...]
        n0 += ref.shape[1]


def pack(share, mats, smalls, width):
    shapes = [(m.shape[0] // 4, m.shape[1]) for m in mats]
    blocks = sum(r * c for r, c in shapes) // (SUB * width)
    smalls = [v.reshape(1, -1) for v in smalls]
    line = (1, sum(v.shape[1] for v in smalls))
    return pl.pallas_call(
        functools.partial(pack_body, len(mats)),
        name="pack",
        grid_spec=pltpu.PrefetchScalarGridSpec(
            num_scalar_prefetch=1,
            grid=(1,),
            in_specs=[pl.BlockSpec(sh, lambda t, r: (r[0], 0)) for sh in shapes]
            + [pl.BlockSpec(v.shape, lambda t, r: (0, 0)) for v in smalls],
            out_specs=[
                pl.BlockSpec((1, blocks, SUB, width), lambda t, r: (0, 0, 0, 0)),
                pl.BlockSpec(line, lambda t, r: (0, 0)),
            ],
        ),
        out_shape=[jax.ShapeDtypeStruct((1, blocks, SUB, width), BF), jax.ShapeDtypeStruct(line, BF)],
        compiler_params=params(),
        cost_estimate=cost(1, 4 * blocks * SUB * width),
    )(share, *mats, *smalls)


def after(v, *deps):
    return lax.optimization_barrier((v,) + deps)[0]


def gather_z(own):
    near = [move(own, TO_Z[k]) for k in (1, 2, 3)]
    return jnp.concatenate([own, near[0]], 0), jnp.concatenate([near[1], near[2]], 0)


def to_core(bufs):
    return [move(v, TO_CORE) for v in bufs]


def tied(*groups):
    flat = lax.optimization_barrier([v for g in groups for v in g])
    out = []
    for g in groups:
        out.append(flat[: len(g)])
        flat = flat[len(g) :]
    return out


def gather_places(order):
    x, y, z, c = place_of()
    spots = []
    for fc in (0, 1):
        for k0, fx, fy in order:
            for k in (k0, k0 + 1):
                spots.append((((z - k) % 4) * 2 + (y ^ fy)) * 4 + (x ^ fx) * 2 + (c ^ fc))
    return jnp.stack(spots).astype(jnp.int32)


def spread(w, blocks, wide):
    full = lax.all_gather(w, "shard", axis=0, tiled=True)
    if full.shape[1] == wide:
        return full.reshape(-1, blocks, SUB, wide)
    return full.reshape(-1, SUB, blocks, wide).transpose(0, 2, 1, 3)


def sum_core(here, pairs):
    a_send, a_keep, b_send, b_keep = add1(here, pairs)
    return (a_keep, move(a_send, TO_X)), (b_keep, move(b_send, TO_Y))


def sum_plane(here, first, second):
    a_send, a_keep, b_send, b_keep = add2(here, first, second)
    return (a_keep, move(a_send, TO_Y)), (b_keep, move(b_send, TO_X))


def sum_z(here, first, second):
    own, *sends = add3(here, first, second)
    return [own] + [move(v, TO_Z[k + 1]) for k, v in enumerate(sends)]


def copies_of(*groups):
    own = add4(*groups)
    return own, move(own, TO_CORE), move(own, TO_X), move(own, TO_XCORE)


def small_gather(plane):
    x, y, z, c = place_of()
    rows = jnp.concatenate([plane] + [move(plane, TO_Z[k]) for k in (1, 2, 3)], 0)
    spots = jnp.stack([((z - k) % 4) * 2 + (y ^ f) for k in range(4) for f in (0, 1)])
    pick = (jnp.arange(8)[:, None] == spots[None, :]).astype(BF)
    return dot_nn(pick, rows)


def small_sum(rows):
    s = lax.axis_index("shard")
    if not regular():
        return lax.dynamic_index_in_dim(lax.psum(rows, BOTH), s, 0, keepdims=False)
    x, y, z, c = place_of()
    rows = rows + move(rows, TO_CORE)
    rows = rows + move(rows, TO_X)
    rows = rows.reshape(4, 2, -1)
    pick = lambda v, i, axis: lax.dynamic_index_in_dim(v, i, axis, keepdims=False)
    rows = pick(rows, y, 1) + move(pick(rows, 1 - y, 1), TO_Y)
    own = pick(rows, z, 0)
    for k in (1, 2, 3):
        own = own + move(pick(rows, (z + k) % 4, 0)[None], TO_Z[k])[0]
    return own


def reduce_any(keep, send, by_rows):
    half, blocks, _, wide = keep.shape
    full = jnp.stack([keep, send], 1).reshape(2 * half, blocks, SUB, wide)
    full = full.reshape(-1, wide) if by_rows else full.transpose(0, 2, 1, 3).reshape(-1, blocks * wide)
    part = lax.psum_scatter(full, "shard", scatter_dimension=0, tiled=True)
    return lax.psum(part, "replica").astype(F32)


def shards(
    tokens, lengths, cotangent, w_qkv, b_qv, w_attn_out, b_attn_out, ln1_gain, ln1_bias,
    w_ffn_in, b_ffn_in, w_ffn_out, b_ffn_out, ln2_gain, ln2_bias,
):
    _, slots, width = tokens.shape
    nblk = w_ffn_in.shape[1] // width
    count = lax.axis_size("shard")
    x = tokens.reshape(slots, width)
    cot = cotangent.reshape(slots, width)
    small = [b_qv, b_attn_out, ln1_gain, ln1_bias, b_ffn_in, b_ffn_out, ln2_gain, ln2_bias]
    sizes = [v.shape[0] for v in small]
    ends = [sum(sizes[: i + 1]) for i in range(len(sizes))]

    if regular():
        share = lax.axis_index("replica").reshape(1).astype(jnp.int32)
        first, line = pack(share, [w_qkv], small, width)
        plane = jnp.concatenate([line, move(line, TO_Y)], 0)
        a1, b1 = gather_z(first)
        rows = small_gather(after(plane, a1, b1))
        second, _ = pack(share, [w_attn_out, w_ffn_in, w_ffn_out], [b_qv], width)
        second = after(second, a1, b1, rows)
        near = move(second, TO_Z[1])
        plane = [move(a1, TO_Y), move(b1, TO_X), move(a1, TO_X), move(b1, TO_Y)]
        first = [a1, b1]
        cores = to_core(first)
        plane, cores = tied(plane, cores)
        last = [move(plane[0], TO_X), move(plane[1], TO_Y)]
        more = to_core(plane)
        last, more, [near, second] = tied(last, more, [near, second])
        w1 = [*first, *plane, *last, *cores, *more, *to_core(last)]
        far = [move(second, TO_Z[k]) for k in (2, 3)]
        a2 = jnp.concatenate([second, near], 0)
        ya2, xa2 = move(a2, TO_Y), move(a2, TO_X)
        place = gather_places(((0, 0, 0), (2, 0, 0), (0, 0, 1), (2, 1, 0), (0, 1, 0), (2, 0, 1), (0, 1, 1), (2, 1, 1)))
        place2 = gather_places(((0, 0, 0), (0, 0, 1), (0, 1, 0), (2, 0, 0), (2, 1, 0), (2, 0, 1), (0, 1, 1), (2, 1, 1)))
        here = jnp.stack(place_of()).astype(jnp.int32)
    else:
        w1 = [spread(w_qkv, 3, width)]
        w2 = [spread(w_attn_out, 1, width), spread(w_ffn_in, nblk, width), spread(w_ffn_out, 4, width)]
        w2 = [jnp.concatenate(w2, 1)]
        place = place2 = jnp.arange(width // SUB, dtype=jnp.int32)
        here = jnp.zeros((4,), jnp.int32)
    core = here[3:]

    if not regular():
        rows = lax.all_gather(jnp.concatenate(small), "shard", axis=0).astype(F32)
    b_qv, bao, gain1, shift1, b_in, bout, gain2, shift2 = [
        rows[:, e - s : e].reshape(-1) for s, e in zip(sizes, ends)
    ]
    bias3 = jnp.concatenate([b_qv[:width], jnp.zeros((width,), F32), b_qv[width:]]).reshape(1, -1)
    zero = jnp.zeros((width,), F32)
    vecs = jnp.stack([bao, gain1, shift1, bout, gain2, shift2, zero, zero])

    qkv = qkv_call(x, place, w1, bias3)
    parts = 4
    fwd = lambda i, state: attn_fwd_call(qkv, lengths, i, parts, state)
    state = fwd(0, None)
    if regular():
        far, [ya2, xa2], state = tied(far, [ya2, xa2], state)
        b2 = jnp.concatenate(far, 0)
        xb2, yb2 = move(b2, TO_X), move(b2, TO_Y)
        cores = to_core([a2, ya2, xa2])
        state = fwd(1, state)
        cores, state = tied(cores, state)
        state = fwd(2, state)
        [xb2, yb2], state = tied([xb2, yb2], state)
        last = [move(ya2, TO_X), move(xb2, TO_Y)]
        more = to_core([b2, xb2, yb2])
        more, state = tied(more, state)
        state = fwd(3, state)
        last, state = tied(last, state)
        w2 = [a2, ya2, xa2, b2, xb2, yb2, *last, *cores, *more, *to_core(last)]
    else:
        for i in range(1, parts):
            state = fwd(i, state)
    ctx, qa0, qa1 = state
    out, act, low, gf, gp, ga, gc, sums, sbin = row_call(
        x, ctx, cot, place2, w2, vecs, b_in.reshape(nblk, width), lengths
    )
    def small_rows(sq, sv):
        vs = [jnp.concatenate([sq[0], sv[0]]), sums[5], sums[3], sums[4], sbin, sums[2], sums[0], sums[1]]
        return jnp.concatenate([v.reshape(count, -1) for v in vs], 1)

    p_wout = wgrad_call("wgrad_out", core, act, gf, True)
    p_win = wgrad_call("wgrad_in", core, low, gp, False)
    state = None
    bwd = lambda i, state, g: attn_bwd_call(qa0, qa1, qkv, ctx, g, lengths, i, parts, state)
    if regular():
        swap = lambda p: (p[0], move(p[1], TO_CORE))
        r_out = sum_core(here, [swap(p_wout)])
        p_wao = wgrad_call("wgrad_ao", core, ctx, after(ga, r_out[0][0]), False)
        r_in = sum_core(here, [swap(p_win), swap(p_wao)])
        def hold(r, state):
            (k0, g0), second = r
            return (after(k0, state[3]), g0), second

        gc = after(gc, r_in[0][0])
        state = bwd(0, None, gc)
        r_out = sum_plane(here, *hold(r_out, state))
        gc = after(gc, r_out[0][0])
        state = bwd(1, state, gc)
        r_in = sum_plane(here, *hold(r_in, state))
        gc = after(gc, r_in[0][0])
        state = bwd(2, state, gc)
        r_out = sum_z(here, *hold(r_out, state))
        gc = after(gc, r_out[0])
        state = bwd(3, state, gc)
        r_in = sum_z(here, *hold(r_in, state))
        dq, dk, dv, sq, sv = state
        own = small_sum(small_rows(sq, sv))
        p_wqkv = wgrad3(core, after(x, r_in[0]), dq, dk, dv)
        r_qkv = sum_core(here, [swap(p_wqkv)])
        g_tok = tok_call(after(ga, r_qkv[0][0], *r_out[1:]), dq, dk, dv, place, w1)
        (k0, g0), second = r_qkv
        r_qkv = sum_plane(here, (after(k0, g_tok, *r_in[1:]), g0), second)
        r_rest = copies_of([after(r_out[0], r_qkv[0][0]), *r_out[1:]], r_in)
        (k0, g0), second = r_qkv
        r_qkv = sum_z(here, (after(k0, r_rest[0], own), g0), second)
        g_wout, g_win, g_wao = final_call(here, r_rest, [(4, True), (nblk, False), (1, False)])
        (g_wqkv,) = final_call(here, copies_of(r_qkv), [(3, False)])
    else:
        p_wao = wgrad_call("wgrad_ao", core, ctx, ga, False)
        for i in range(parts):
            state = bwd(i, state, gc)
        dq, dk, dv, sq, sv = state
        own = small_sum(small_rows(sq, sv))
        p_wqkv = wgrad3(core, x, dq, dk, dv)
        g_tok = tok_call(ga, dq, dk, dv, place, w1)
        g_wout = reduce_any(*p_wout, True)
        g_win, g_wao, g_wqkv = [reduce_any(*p, False) for p in (p_win, p_wao, p_wqkv)]

    g_bqv, g_bao, g_g1, g_s1, g_bin, g_bout, g_g2, g_s2 = [own[e - s : e] for s, e in zip(sizes, ends)]
    return (
        out[None], g_tok[None], g_wqkv, g_bqv, g_wao, g_bao, g_g1, g_s1,
        g_win, g_bin, g_wout, g_bout, g_g2, g_s2,
    )


def solution(mesh):
    rows = P(("replica", "shard"), None, None)
    mat, vec = P("shard", None), P("shard")
    return jax.shard_map(
        shards,
        mesh=mesh,
        in_specs=(rows, P(("replica", "shard")), rows, mat, vec, mat, vec, vec, vec, mat, vec, mat, vec, vec, vec),
        out_specs=(rows, rows, mat, vec, mat, vec, vec, vec, mat, vec, mat, vec, vec, vec),
        check_vma=False,
    )
```

time: 907 us -> 530 us (0.58)
  waiting for transfers between devices: 517 us -> 86.2 us
  starting transfers between devices: 0.33 us -> 97.6 us
  blocking collectives: 85.7 us -> 0 us
  Pallas kernels: 228 us -> 308 us
  local copies, waits for them, and re-layouts: 48.1 us -> 26.2 us
  between operations: 15.5 us -> 2.29 us
    reduce_scatter x4 -> x0, waiting for transfers between devices: 392 us -> none  [the longest x2 228 us: collect_rows(): lax.psum_scatter(grad.reshape(devices, m // devices, wide), BOTH, scatter...]
    all_gather x4 -> x0, waiting for transfers between devices: 125 us -> none  [the longest x2 107 us: spread(): full = lax.all_gather(packed, BOTH, axis=0)]
    ppermute x0 -> x75, starting transfers between devices: none -> 97.6 us  [move(): return lax.ppermute(v, AXES, pairs)]
    ppermute x0 -> x75, waiting for transfers between devices: none -> 86.2 us  [move(): return lax.ppermute(v, AXES, pairs)]
    pallas_call x9 -> x30, Pallas kernels: 228 us -> 308 us  [the longest x1 60.7 us: row_call(): pl.pallas_call(functools.partial(row_body, len(w2)), name='row_local', gr...]
    all_gather x3 -> x0, blocking collectives: 47.9 us -> none  [the longest x1 33.1 us: shards(): table = lax.all_gather(jnp.concatenate(small), 'shard', axis=0).astype(F32)]
    psum x1 -> x0, blocking collectives: 37.8 us -> none  [shards(): table = lax.psum(table, BOTH)]
    all_gather x1 -> x0, local copies, waits for them, and re-layouts: 18.7 us -> none  [spread(): full = lax.all_gather(packed, BOTH, axis=0)]
  transfers between devices with their start and end apart: 8 -> 75, of which waited for: 8 -> 28; matrix products, arithmetic and copies ran while one was open for 2% -> 3% of each run, Pallas kernels for 16% -> 39%
where the time goes in v2:
time: 530 us; the launch traced here: 525 us
  Pallas kernels  308 us (58%)
  starting transfers between devices  97.6 us (18%)
  waiting for transfers between devices  86.2 us (16%)
  local copies, waits for them, and re-layouts  26.2 us (5%)
    ppermute x75, starting transfers between devices, move(): return lax.ppermute(v, AXES, pairs)  97.6 us
    ppermute x75, waiting for transfers between devices, move(): return lax.ppermute(v, AXES, pairs)  86.2 us
    pallas_call x1, Pallas kernels, row_call(): pl.pallas_call(functools.partial(row_body, len(w2)), name='row_local', gr...  60.7 us
    pallas_call x4, Pallas kernels, attn_bwd_call(): pl.pallas_call(functools.partial(attn_bwd_body, rows), name=f'attn_bwd{pa...  57.8 us
    pallas_call x3, Pallas kernels, wgrad_call(): pl.pallas_call(functools.partial(wgrad_body, group), name=name, grid_spec...  46.7 us
    pallas_call x4, Pallas kernels, attn_fwd_call(): pl.pallas_call(functools.partial(attn_fwd_body, rows), name=f'attn_fwd{pa...  43.5 us
    pallas_call x3, Pallas kernels, add1(): pl.pallas_call(functools.partial(add1_body, len(pairs)), name='add_core',...  19.6 us
    unnamed x106, local copies, waits for them, and re-layouts  17 us
  transfers between devices with their start and end apart: 75, of which 28 were waited for; matrix products, arithmetic and copies ran while one was open for 3% of the time, Pallas kernels for 39%

profile of v2, /device:TPU:0, one launch (start us, length us, event | category | flops | bytes accessed | tf_op | source)
XLA Modules:
  0.0 525.2 jit_solution(912504794027307375)
XLA Ops:
  4.8 4.0 collective-permute-start.2
  12.4 7.5 %collective-permute-done.2 = bf16[1,3,32,1024]{3,2,1,0:T(8,128)(2,1)S(1)} collective-permute-done((bf16[1,3,32,1024]{3,2,1,0:T(8,128)(2,1)}, bf16[1,3,32,1024]{3,2,1,0:T(8,128)(2,1)S(1)}, u32[]{:S(2)}, u32[]{:S(2)}) %collective-permute-start.2) | collective-permute-done | bytes 196640 | tf_op jit(solution)/shard_map/ppermute | solution.py:691
  25.4 6.8 %collective-permute-start.16 = (bf16[2,1536]{1,0:T(2,128)(2,1)S(1)}, bf16[2,1536]{1,0:T(2,128)(2,1)S(1)}, u32[]{:S(2)}, u32[]{:S(2)}) collective-permute-start(bf16[2,1536]{1,0:T(2,128)(2,1)S(1)} %pad_maximum_fusion.1), channel_id=1, source_target_pairs={{0,2},{1,3},{2,4},{3,5},{4,6},{5,7},{6,0},{7,1},{8,10},{9,11},{10,... | collective-permute-start | bytes 18440 | tf_op jit(solution)/shard_map/ppermute | solution.py:691
  39.7 8.5 %collective-permute-done.1.rest_2_ = bf16[2,3,32,1024]{3,2,1,0:T(8,128)(2,1)S(1)} collective-permute-done((bf16[2,3,32,1024]{3,2,1,0:T(8,128)(2,1)S(1)}, bf16[2,3,32,1024]{3,2,1,0:T(8,128)(2,1)S(1)}, u32[]{:S(2)}, u32[]{:S(2)}) %collective-permute-start.1) | collective-permute-done | bytes 393248 | tf_op jit(solution)/shard_map/ppermute | solution.py:691
  51.1 4.6 collective-permute-done.19
  55.8 3.3 collective-permute-done.10.rest_7_
  70.1 13.3 %qkv.1.q_ref.k_ref.v_ref = bf16[1024,3072]{1,0:T(8,128)(2,1)} custom-call(s32[32]{0:T(128)} %stack.224.place, bf16[1024,1024]{1,0:T(8,128)(2,1)} %bitcast.186, f32[1,3072]{1,0:T(1,128)} %bitcast.176, bf16[2,3,32,1024]{3,2,1,0:T(8,128)(2,1)} %copy-done.27, bf16[2,3,32,1024]{3,2,1,0:T(8,128)(2,1)} %copy-done.28, bf16[2,3,32,1024]{3,2,1,0:T(8,128)(2,1)} %copy-done.42, ...), custom_call_target="tpu_custom_call" | custom-call | flops 6442450944 | bytes 14680064 | tf_op jit(solution)/shard_map/qkv/pallas_call | solution.py:80
  83.4 10.9 %attn_fwd0.1 = (bf16[1024,1024]{1,0:T(8,128)(2,1)}, bf16[1024,1024]{1,0:T(8,128)(2,1)}, bf16[1024,1024]{1,0:T(8,128)(2,1)}) custom-call(s32[1]{0:T(128)S(6)} %copy.99.len_ref, bf16[1024,3072]{1,0:T(8,128)(2,1)} %qkv.1.q_ref.k_ref.v_ref, bf16[1024,3072]{1,0:T(8,128)(2,1)} %qkv.1.q_ref.k_ref.v_ref, bf16[1024,3072]{1,0:T(8,128)(2,1)} %qkv.1.q_ref.k_ref.v_ref), custom_call_target="tpu_custom_call" | custom-call | flops 4294967296 | bytes 3145728 | tf_op jit(solution)/shard_map/attn_fwd0/pallas_call | solution.py:157
  98.9 10.8 %attn_fwd1.1 = (bf16[1024,1024]{1,0:T(8,128)(2,1)}, bf16[1024,1024]{1,0:T(8,128)(2,1)}, bf16[1024,1024]{1,0:T(8,128)(2,1)}) custom-call(s32[1]{0:T(128)S(6)} %copy.99.len_ref, bf16[1024,3072]{1,0:T(8,128)(2,1)} %qkv.1.q_ref.k_ref.v_ref, bf16[1024,3072]{1,0:T(8,128)(2,1)} %qkv.1.q_ref.k_ref.v_ref, ...), custom_call_target="tpu_custom_call", output_to_operand_aliasing={{0}: (4, {}), {1}: (5, {}), {2}: (6, {})} | custom-call | flops 4294967296 | bytes 3145728 | tf_op jit(solution)/shard_map/attn_fwd1/pallas_call | solution.py:157
  109.8 11.0 %attn_fwd2.1 = (bf16[1024,1024]{1,0:T(8,128)(2,1)}, bf16[1024,1024]{1,0:T(8,128)(2,1)}, bf16[1024,1024]{1,0:T(8,128)(2,1)}) custom-call(s32[1]{0:T(128)S(6)} %copy.99.len_ref, bf16[1024,3072]{1,0:T(8,128)(2,1)} %qkv.1.q_ref.k_ref.v_ref, bf16[1024,3072]{1,0:T(8,128)(2,1)} %qkv.1.q_ref.k_ref.v_ref, ...), custom_call_target="tpu_custom_call", output_to_operand_aliasing={{0}: (4, {}), {1}: (5, {}), {2}: (6, {})} | custom-call | flops 4294967296 | bytes 3145728 | tf_op jit(solution)/shard_map/attn_fwd2/pallas_call | solution.py:157
  120.9 3.9 collective-permute-done.27.rest_4_
  130.9 10.8 %attn_fwd3.1 = (bf16[1024,1024]{1,0:T(8,128)(2,1)}, bf16[1024,1024]{1,0:T(8,128)(2,1)}, bf16[1024,1024]{1,0:T(8,128)(2,1)}) custom-call(s32[1]{0:T(128)S(6)} %copy.99.len_ref, bf16[1024,3072]{1,0:T(8,128)(2,1)} %qkv.1.q_ref.k_ref.v_ref, bf16[1024,3072]{1,0:T(8,128)(2,1)} %qkv.1.q_ref.k_ref.v_ref, ...), custom_call_target="tpu_custom_call", output_to_operand_aliasing={{0}: (4, {}), {1}: (5, {}), {2}: (6, {})} | custom-call | flops 4294967296 | bytes 3145728 | tf_op jit(solution)/shard_map/attn_fwd3/pallas_call | solution.py:157
  141.7 12.8 %collective-permute-done.26.rest_6_ = bf16[2,9,32,1024]{3,2,1,0:T(8,128)(2,1)} collective-permute-done((bf16[2,9,32,1024]{3,2,1,0:T(8,128)(2,1)S(1)}, bf16[2,9,32,1024]{3,2,1,0:T(8,128)(2,1)}, u32[]{:S(2)}, u32[]{:S(2)}) %collective-permute-start.26) | collective-permute-done | bytes 1179680 | tf_op jit(solution)/shard_map/ppermute | solution.py:691
  160.7 60.7 %row_local.1 = (bf16[1024,1024]{1,0:T(8,128)(2,1)}, bf16[1024,4096]{1,0:T(8,128)(2,1)}, bf16[1024,1024]{1,0:T(8,128)(2,1)}, bf16[1024,1024]{1,0:T(8,128)(2,1)}, ...) custom-call(s32[1]{0:T(128)S(6)} %copy.99.len_ref, ...), custom_call_target="tpu_custom_call" | custom-call | flops 38654705664 | bytes 60817408 | tf_op jit(solution)/shard_map/row_local/pallas_call | solution.py:350
  221.4 19.1 %wgrad_out.1 = (bf16[16,4,32,1024]{3,2,1,0:T(8,128)(2,1)}, bf16[16,4,32,1024]{3,2,1,0:T(8,128)(2,1)}) custom-call(s32[1]{0:T(128)} %bitcast.60.core, bf16[1024,4096]{1,0:T(8,128)(2,1)} %get-tuple-element.228.a_ref, bf16[1024,1024]{1,0:T(8,128)(2,1)} %get-tuple-element.229.b_ref), custom_call_target="tpu_custom_call" | custom-call | flops 8589934592 | bytes 18874368 | tf_op jit(solution)/shard_map/wgrad_out/pallas_call | solution.py:410
  240.7 21.3 %wgrad_in.1 = (bf16[16,4,32,1024]{3,2,1,0:T(8,128)(2,1)}, bf16[16,4,32,1024]{3,2,1,0:T(8,128)(2,1)}) custom-call(s32[1]{0:T(128)} %bitcast.60.core, bf16[1024,1024]{1,0:T(8,128)(2,1)} %get-tuple-element.224.a_ref, bf16[1024,4096]{1,0:T(8,128)(2,1)} %get-tuple-element.225.b_ref), custom_call_target="tpu_custom_call" | custom-call | flops 8589934592 | bytes 18874368 | tf_op jit(solution)/shard_map/wgrad_in/pallas_call | solution.py:410
  263.0 6.5 %add_core.3 = (bf16[4,4,32,1024]{3,2,1,0:T(8,128)(2,1)}, bf16[4,4,32,1024]{3,2,1,0:T(8,128)(2,1)}, bf16[4,4,32,1024]{3,2,1,0:T(8,128)(2,1)}, bf16[4,4,32,1024]{3,2,1,0:T(8,128)(2,1)}) custom-call(s32[4]{0:T(128)} %pad_add_fusion.here, bf16[4,2,2,4,32,1024]{5,4,3,2,1,0:T(8,128)(2,1)} %bitcast.115, ...), custom_call_target="tpu_custom_call" | custom-call | flops 2097152 | bytes 12582912 | tf_op jit(solution)/shard_map/add_core/pallas_call | solution.py:528
  269.5 6.3 %wgrad_ao.1 = (bf16[16,1,32,1024]{3,2,1,0:T(8,128)(2,1)}, bf16[16,1,32,1024]{3,2,1,0:T(8,128)(2,1)}) custom-call(s32[1]{0:T(128)} %bitcast.60.core, bf16[1024,1024]{1,0:T(8,128)(2,1)} %get-tuple-element.213.ctx_ref.a_ref, bf16[1024,1024]{1,0:T(8,128)(2,1)} %get-tuple-element.290.b_ref.g_ref), custom_call_target="tpu_custom_call" | custom-call | flops 2147483648 | bytes 6291456 | tf_op jit(solution)/shard_map/wgrad_ao/pallas_call | solution.py:410
  279.7 7.3 %add_core.4 = (bf16[4,5,32,1024]{3,2,1,0:T(8,128)(2,1)}, bf16[4,5,32,1024]{3,2,1,0:T(8,128)(2,1)}, bf16[4,5,32,1024]{3,2,1,0:T(8,128)(2,1)}, bf16[4,5,32,1024]{3,2,1,0:T(8,128)(2,1)}) custom-call(s32[4]{0:T(128)} %pad_add_fusion.here, bf16[4,2,2,4,32,1024]{5,4,3,2,1,0:T(8,128)(2,1)} %bitcast.119, ...), custom_call_target="tpu_custom_call" | custom-call | flops 2621440 | bytes 15728640 | tf_op jit(solution)/shard_map/add_core/pallas_call | solution.py:528
  289.3 14.3 %attn_bwd0.1 = (bf16[1024,1024]{1,0:T(8,128)(2,1)}, bf16[1024,1024]{1,0:T(8,128)(2,1)}, bf16[1024,1024]{1,0:T(8,128)(2,1)}, f32[1,1024]{1,0:T(1,128)}, f32[1,1024]{1,0:T(1,128)}) custom-call(s32[1]{0:T(128)S(6)} %copy.99.len_ref, bf16[1024,1024]{1,0:T(8,128)(2,1)} %get-tuple-element.237.qa0_ref, bf16[1024,1024]{1,0:T(8,128)(2,1)} %get-tuple-element.238.qa1_ref, ...), custom_call_target="tpu_custom_call" | custom-call | flops 10737418240 | bytes 4718592 | tf_op jit(solution)/shard_map/attn_bwd0/pallas_call | solution.py:233
  304.6 4.0 add_plane.3
  308.6 14.6 %attn_bwd1.1 = (bf16[1024,1024]{1,0:T(8,128)(2,1)}, bf16[1024,1024]{1,0:T(8,128)(2,1)}, bf16[1024,1024]{1,0:T(8,128)(2,1)}, f32[1,1024]{1,0:T(1,128)}, f32[1,1024]{1,0:T(1,128)}) custom-call(s32[1]{0:T(128)S(6)} %copy.99.len_ref, ...), custom_call_target="tpu_custom_call", output_to_operand_aliasing={{0}: (7, {}), {1}: (8, {}), {2}: (9, {}), {3}: (10, {}), {4... | custom-call | flops 10737418240 | bytes 4718592 | tf_op jit(solution)/shard_map/attn_bwd1/pallas_call | solution.py:233
  325.2 5.1 collective-permute-done.43
  332.8 4.5 add_plane.4
  337.3 14.4 %attn_bwd2.1 = (bf16[1024,1024]{1,0:T(8,128)(2,1)}, bf16[1024,1024]{1,0:T(8,128)(2,1)}, bf16[1024,1024]{1,0:T(8,128)(2,1)}, f32[1,1024]{1,0:T(1,128)}, f32[1,1024]{1,0:T(1,128)}) custom-call(s32[1]{0:T(128)S(6)} %copy.99.len_ref, ...), custom_call_target="tpu_custom_call", output_to_operand_aliasing={{0}: (7, {}), {1}: (8, {}), {2}: (9, {}), {3}: (10, {}), {4... | custom-call | flops 10737418240 | bytes 4718592 | tf_op jit(solution)/shard_map/attn_bwd2/pallas_call | solution.py:233
  352.7 3.4 add_z.3
  357.3 14.5 %attn_bwd3.1 = (bf16[1024,1024]{1,0:T(8,128)(2,1)}, bf16[1024,1024]{1,0:T(8,128)(2,1)}, bf16[1024,1024]{1,0:T(8,128)(2,1)}, f32[1,1024]{1,0:T(1,128)}, f32[1,1024]{1,0:T(1,128)}) custom-call(s32[1]{0:T(128)S(6)} %copy.99.len_ref, ...), custom_call_target="tpu_custom_call", output_to_operand_aliasing={{0}: (7, {}), {1}: (8, {}), {2}: (9, {}), {3}: (10, {}), {4... | custom-call | flops 10737418240 | bytes 4718592 | tf_op jit(solution)/shard_map/attn_bwd3/pallas_call | solution.py:233
  372.9 3.7 add_z.4
  376.7 13.8 %wgrad_qkv.1 = (bf16[16,3,32,1024]{3,2,1,0:T(8,128)(2,1)}, bf16[16,3,32,1024]{3,2,1,0:T(8,128)(2,1)}) custom-call(s32[1]{0:T(128)} %bitcast.60.core, bf16[1024,1024]{1,0:T(8,128)(2,1)} %bitcast.188, bf16[1024,1024]{1,0:T(8,128)(2,1)} %get-tuple-element.281.q_ref.dq_ref, bf16[1024,1024]{1,0:T(8,128)(2,1)} %get-tuple-element.282.k_ref.dk_ref, ...), custom_call_target="tpu_custom_call" | custom-call | flops 6442450944 | bytes 14680064 | tf_op jit(solution)/shard_map/wgrad_qkv/pallas_call | solution.py:439
  390.5 12.7 %collective-permute-start.50 = (bf16[1,4,32,1024]{3,2,1,0:T(8,128)(2,1)}, bf16[1,4,32,1024]{3,2,1,0:T(8,128)(2,1)}, u32[]{:S(2)}, u32[]{:S(2)}) collective-permute-start(bf16[1,4,32,1024]{3,2,1,0:T(8,128)(2,1)} %get-tuple-element.287), channel_id=1, source_target_pairs={{0,2},{1,3},{2,4},{3,5},{4,6},{5,7},{6,0},{7,1},{8,10},{9,11},{10,... | collective-permute-start | bytes 786440 | tf_op jit(solution)/shard_map/ppermute | solution.py:691
  411.3 3.7 collective-permute-start.52
  419.0 5.8 %add_core.5 = (bf16[4,3,32,1024]{3,2,1,0:T(8,128)(2,1)}, bf16[4,3,32,1024]{3,2,1,0:T(8,128)(2,1)}, bf16[4,3,32,1024]{3,2,1,0:T(8,128)(2,1)}, bf16[4,3,32,1024]{3,2,1,0:T(8,128)(2,1)}) custom-call(s32[4]{0:T(128)} %pad_add_fusion.here, bf16[4,2,2,3,32,1024]{5,4,3,2,1,0:T(8,128)(2,1)} %bitcast.123, bf16[4,2,2,3,32,1024]{5,4,3,2,1,0:T(8,128)(2,1)} %bitcast.127, ...), custom_call_target="tpu_custom_call" | custom-call | flops 1572864 | bytes 9437184 | tf_op jit(solution)/shard_map/add_core/pallas_call | solution.py:528
  427.6 2.7 collective-permute-done.51.refs_2_
  431.7 3.7 collective-permute-start.54
  435.4 3.4 collective-permute-start.55
  438.8 13.8 %grad_tok.1 = bf16[1024,1024]{1,0:T(8,128)(2,1)} custom-call(s32[32]{0:T(128)} %stack.224.place, bf16[1024,1024]{1,0:T(8,128)(2,1)} %get-tuple-element.290.b_ref.g_ref, bf16[1024,1024]{1,0:T(8,128)(2,1)} %get-tuple-element.281.q_ref.dq_ref, bf16[1024,1024]{1,0:T(8,128)(2,1)} %get-tuple-element.282.k_ref.dk_ref, ...), custom_call_target="tpu_custom_call" | custom-call | flops 6442450944 | bytes 16777216 | tf_op jit(solution)/shard_map/grad_tok/pallas_call | solution.py:475
  454.0 3.6 add_plane.5
  460.5 2.7 add_last.2.own
  463.2 5.2 collective-permute-done.58.ag
  470.2 3.1 add_z.5
  473.3 6.2 %collective-permute-start.60 = (bf16[1,3,32,1024]{3,2,1,0:T(8,128)(2,1)}, bf16[1,3,32,1024]{3,2,1,0:T(8,128)(2,1)S(1)}, u32[]{:S(2)}, u32[]{:S(2)}) collective-permute-start(bf16[1,3,32,1024]{3,2,1,0:T(8,128)(2,1)} %get-tuple-element.305), channel_id=1, source_target_pairs={{0,2},{1,3},{2,4},{3,5},{4,6},{5,7},{6,0},{7,1},{8,10},{9,11},{10,... | collective-permute-start | bytes 589832 | tf_op jit(solution)/shard_map/ppermute | solution.py:691
  479.6 3.3 collective-permute-start.70
  482.9 2.8 collective-permute-start.71
  488.2 3.1 collective-permute-start.62
  492.4 8.7 %collective-permute-done.61.refs_2_ = bf16[1,3,32,1024]{3,2,1,0:T(8,128)(2,1)S(1)} collective-permute-done((bf16[1,3,32,1024]{3,2,1,0:T(8,128)(2,1)}, bf16[1,3,32,1024]{3,2,1,0:T(8,128)(2,1)S(1)}, u32[]{:S(2)}, u32[]{:S(2)}) %collective-permute-start.61) | collective-permute-done | bytes 196640 | tf_op jit(solution)/shard_map/ppermute | solution.py:691
  506.3 8.5 %collective-permute-done.74.both = bf16[1,9,32,1024]{3,2,1,0:T(8,128)(2,1)S(1)} collective-permute-done((bf16[1,9,32,1024]{3,2,1,0:T(8,128)(2,1)}, bf16[1,9,32,1024]{3,2,1,0:T(8,128)(2,1)S(1)}, u32[]{:S(2)}, u32[]{:S(2)}) %collective-permute-start.74) | collective-permute-done | bytes 589856 | tf_op jit(solution)/shard_map/ppermute | solution.py:691
  515.7 4.7 final.3
  521.8 3.1 final.2
  (276 shorter events, 99.8 us)
Async XLA Ops:
  4.8 15.1 %collective-permute-start.2 = (bf16[1,3,32,1024]{3,2,1,0:T(8,128)(2,1)}, bf16[1,3,32,1024]{3,2,1,0:T(8,128)(2,1)S(1)}, u32[]{:S(2)}, u32[]{:S(2)}) collective-permute-start(bf16[1,3,32,1024]{3,2,1,0:T(8,128)(2,1)} %get-tuple-element.164), channel_id=1, source_target_pairs={{0,4},{1,5},{2,6},{3,7},{4,0},{5,1},{6,2},{7,3},{8,12},{9,13},{10,... | collective-permute-start | bytes 589832 | tf_op jit(solution)/shard_map/ppermute | solution.py:691
  10.2 15.1 %collective-permute-start = (bf16[1,3,32,1024]{3,2,1,0:T(8,128)(2,1)}, bf16[1,3,32,1024]{3,2,1,0:T(8,128)(2,1)S(1)}, u32[]{:S(2)}, u32[]{:S(2)}) collective-permute-start(bf16[1,3,32,1024]{3,2,1,0:T(8,128)(2,1)} %get-tuple-element.164), channel_id=1, source_target_pairs={{0,2},{1,3},{2,4},{3,5},{4,6},{5,7},{6,0},{7,1},{8,10},{9,11},{10,... | collective-permute-start | bytes 589832 | tf_op jit(solution)/shard_map/ppermute | solution.py:691
  10.9 13.7 %collective-permute-start.15 = (bf16[1,1536]{1,0:T(2,128)(2,1)}, bf16[1,1536]{1,0:T(2,128)(2,1)S(1)}, u32[]{:S(2)}, u32[]{:S(2)}) collective-permute-start(bf16[1,1536]{1,0:T(2,128)(2,1)} %get-tuple-element.170), channel_id=1, source_target_pairs={{0,1},{1,0},{2,3},{3,2},{4,5},{5,4},{6,7},{7,6},{8,9},{9,8},{10,11... | collective-permute-start | bytes 9224 | tf_op jit(solution)/shard_map/ppermute | solution.py:691
  20.0 17.8 %collective-permute-start.4 = (bf16[2,3,32,1024]{3,2,1,0:T(8,128)(2,1)S(1)}, bf16[2,3,32,1024]{3,2,1,0:T(8,128)(2,1)S(1)}, u32[]{:S(2)}, u32[]{:S(2)}) collective-permute-start(bf16[2,3,32,1024]{3,2,1,0:T(8,128)(2,1)S(1)} %constant_dynamic-update-slice_fusion.2.rest_1_), channel_id=1, source_target_pairs={{0,16},{1,17},{2,18},{3,19},{4,20},{5,21},{6,22},{7,23},{8,24},{9,... | collective-permute-start | bytes 1179656 | tf_op jit(solution)/shard_map/ppermute | solution.py:691
  23.0 14.9 %collective-permute-start.6 = (bf16[2,3,32,1024]{3,2,1,0:T(8,128)(2,1)S(1)}, bf16[2,3,32,1024]{3,2,1,0:T(8,128)(2,1)S(1)}, u32[]{:S(2)}, u32[]{:S(2)}) collective-permute-start(bf16[2,3,32,1024]{3,2,1,0:T(8,128)(2,1)S(1)} %constant_dynamic-update-slice_fusion.2.rest_1_), channel_id=1, source_target_pairs={{0,1},{1,0},{2,3},{3,2},{4,5},{5,4},{6,7},{7,6},{8,9},{9,8},{10,11... | collective-permute-start | bytes 1179656 | tf_op jit(solution)/shard_map/ppermute | solution.py:691
  36.7 11.5 %collective-permute-start.1 = (bf16[2,3,32,1024]{3,2,1,0:T(8,128)(2,1)S(1)}, bf16[2,3,32,1024]{3,2,1,0:T(8,128)(2,1)S(1)}, u32[]{:S(2)}, u32[]{:S(2)}) collective-permute-start(bf16[2,3,32,1024]{3,2,1,0:T(8,128)(2,1)S(1)} %constant_dynamic-update-slice_fusion.rest_0_), channel_id=1, source_target_pairs={{0,1},{1,0},{2,3},{3,2},{4,5},{5,4},{6,7},{7,6},{8,9},{9,8},{10,11... | collective-permute-start | bytes 1179656 | tf_op jit(solution)/shard_map/ppermute | solution.py:691
  38.0 17.8 %collective-permute-start.19 = (bf16[1,9,32,1024]{3,2,1,0:T(8,128)(2,1)}, bf16[1,9,32,1024]{3,2,1,0:T(8,128)(2,1)S(1)}, u32[]{:S(2)}, u32[]{:S(2)}) collective-permute-start(bf16[1,9,32,1024]{3,2,1,0:T(8,128)(2,1)} %get-tuple-element.173), channel_id=1, source_target_pairs={{0,2},{1,3},{2,4},{3,5},{4,6},{5,7},{6,0},{7,1},{8,10},{9,11},{10,... | collective-permute-start | bytes 1769480 | tf_op jit(solution)/shard_map/ppermute | solution.py:691
  65.0 30.9 %collective-permute-start.22 = (bf16[2,9,32,1024]{3,2,1,0:T(8,128)(2,1)}, bf16[2,9,32,1024]{3,2,1,0:T(8,128)(2,1)S(1)}, u32[]{:S(2)}, u32[]{:S(2)}) collective-permute-start(bf16[2,9,32,1024]{3,2,1,0:T(8,128)(2,1)} %constant_dynamic-update-slice_fusion.4.rest_0_), channel_id=1, source_target_pairs={{0,1},{1,0},{2,3},{3,2},{4,5},{5,4},{6,7},{7,6},{8,9},{9,8},{10,11... | collective-permute-start | bytes 3538952 | tf_op jit(solution)/shard_map/ppermute | solution.py:691
  66.3 29.6 %collective-permute-start.23 = (bf16[2,9,32,1024]{3,2,1,0:T(8,128)(2,1)}, bf16[2,9,32,1024]{3,2,1,0:T(8,128)(2,1)}, u32[]{:S(2)}, u32[]{:S(2)}) collective-permute-start(bf16[2,9,32,1024]{3,2,1,0:T(8,128)(2,1)} %constant_dynamic-update-slice_fusion.4.rest_0_), channel_id=1, source_target_pairs={{0,16},{1,17},{2,18},{3,19},{4,20},{5,21},{6,22},{7,23},{8,24},{9,... | collective-permute-start | bytes 3538952 | tf_op jit(solution)/shard_map/ppermute | solution.py:691
  67.5 27.8 %collective-permute-start.20 = (bf16[1,9,32,1024]{3,2,1,0:T(8,128)(2,1)S(1)}, bf16[1,9,32,1024]{3,2,1,0:T(8,128)(2,1)S(1)}, u32[]{:S(2)}, u32[]{:S(2)}) collective-permute-start(bf16[1,9,32,1024]{3,2,1,0:T(8,128)(2,1)S(1)} %copy-done.12), channel_id=1, source_target_pairs={{0,4},{1,5},{2,6},{3,7},{4,0},{5,1},{6,2},{7,3},{8,12},{9,13},{10,... | collective-permute-start | bytes 1769480 | tf_op jit(solution)/shard_map/ppermute | solution.py:691
  68.0 28.0 %collective-permute-start.21 = (bf16[1,9,32,1024]{3,2,1,0:T(8,128)(2,1)S(1)}, bf16[1,9,32,1024]{3,2,1,0:T(8,128)(2,1)S(1)}, u32[]{:S(2)}, u32[]{:S(2)}) collective-permute-start(bf16[1,9,32,1024]{3,2,1,0:T(8,128)(2,1)S(1)} %copy-done.12), channel_id=1, source_target_pairs={{0,6},{1,7},{2,0},{3,1},{4,2},{5,3},{6,4},{7,5},{8,14},{9,15},{10,... | collective-permute-start | bytes 1769480 | tf_op jit(solution)/shard_map/ppermute | solution.py:691
  70.1 39.7 %collective-permute-start.29 = (bf16[2,9,32,1024]{3,2,1,0:T(8,128)(2,1)}, bf16[2,9,32,1024]{3,2,1,0:T(8,128)(2,1)}, u32[]{:S(2)}, u32[]{:S(2)}) collective-permute-start(bf16[2,9,32,1024]{3,2,1,0:T(8,128)(2,1)} %constant_dynamic-update-slice_fusion.4.rest_0_), channel_id=1, source_target_pairs={{0,8},{1,9},{2,10},{3,11},{4,12},{5,13},{6,14},{7,15},{8,0},{9,1},... | collective-permute-start | bytes 3538952 | tf_op jit(solution)/shard_map/ppermute | solution.py:691
  96.0 13.8 %collective-permute-start.30 = (bf16[2,9,32,1024]{3,2,1,0:T(8,128)(2,1)S(1)}, bf16[2,9,32,1024]{3,2,1,0:T(8,128)(2,1)}, u32[]{:S(2)}, u32[]{:S(2)}) collective-permute-start(bf16[2,9,32,1024]{3,2,1,0:T(8,128)(2,1)S(1)} %collective-permute-done.22.rest_1_), channel_id=1, source_target_pairs={{0,8},{1,9},{2,10},{3,11},{4,12},{5,13},{6,14},{7,15},{8,0},{9,1},... | collective-permute-start | bytes 3538952 | tf_op jit(solution)/shard_map/ppermute | solution.py:691
  96.0 13.8 %collective-permute-start.31 = (bf16[2,9,32,1024]{3,2,1,0:T(8,128)(2,1)}, bf16[2,9,32,1024]{3,2,1,0:T(8,128)(2,1)}, u32[]{:S(2)}, u32[]{:S(2)}) collective-permute-start(bf16[2,9,32,1024]{3,2,1,0:T(8,128)(2,1)} %collective-permute-done.23.rest_2_), channel_id=1, source_target_pairs={{0,8},{1,9},{2,10},{3,11},{4,12},{5,13},{6,14},{7,15},{8,0},{9,1},... | collective-permute-start | bytes 3538952 | tf_op jit(solution)/shard_map/ppermute | solution.py:691
  96.6 28.1 %collective-permute-start.27 = (bf16[2,9,32,1024]{3,2,1,0:T(8,128)(2,1)S(1)}, bf16[2,9,32,1024]{3,2,1,0:T(8,128)(2,1)}, u32[]{:S(2)}, u32[]{:S(2)}) collective-permute-start(bf16[2,9,32,1024]{3,2,1,0:T(8,128)(2,1)S(1)} %constant_dynamic-update-slice_fusion.6.rest_3_), channel_id=1, source_target_pairs={{0,16},{1,17},{2,18},{3,19},{4,20},{5,21},{6,22},{7,23},{8,24},{9,... | collective-permute-start | bytes 3538952 | tf_op jit(solution)/shard_map/ppermute | solution.py:691
  98.2 27.8 %collective-permute-start.28 = (bf16[2,9,32,1024]{3,2,1,0:T(8,128)(2,1)S(1)}, bf16[2,9,32,1024]{3,2,1,0:T(8,128)(2,1)}, u32[]{:S(2)}, u32[]{:S(2)}) collective-permute-start(bf16[2,9,32,1024]{3,2,1,0:T(8,128)(2,1)S(1)} %constant_dynamic-update-slice_fusion.6.rest_3_), channel_id=1, source_target_pairs={{0,1},{1,0},{2,3},{3,2},{4,5},{5,4},{6,7},{7,6},{8,9},{9,8},{10,11... | collective-permute-start | bytes 3538952 | tf_op jit(solution)/shard_map/ppermute | solution.py:691
  109.7 18.0 %collective-permute-start.33 = (bf16[2,9,32,1024]{3,2,1,0:T(8,128)(2,1)S(1)}, bf16[2,9,32,1024]{3,2,1,0:T(8,128)(2,1)}, u32[]{:S(2)}, u32[]{:S(2)}) collective-permute-start(bf16[2,9,32,1024]{3,2,1,0:T(8,128)(2,1)S(1)} %constant_dynamic-update-slice_fusion.6.rest_3_), channel_id=1, source_target_pairs={{0,8},{1,9},{2,10},{3,11},{4,12},{5,13},{6,14},{7,15},{8,0},{9,1},... | collective-permute-start | bytes 3538952 | tf_op jit(solution)/shard_map/ppermute | solution.py:691
  126.5 28.0 %collective-permute-start.26 = (bf16[2,9,32,1024]{3,2,1,0:T(8,128)(2,1)S(1)}, bf16[2,9,32,1024]{3,2,1,0:T(8,128)(2,1)}, u32[]{:S(2)}, u32[]{:S(2)}) collective-permute-start(bf16[2,9,32,1024]{3,2,1,0:T(8,128)(2,1)S(1)} %collective-permute-done.22.rest_1_), channel_id=1, source_target_pairs={{0,16},{1,17},{2,18},{3,19},{4,20},{5,21},{6,22},{7,23},{8,24},{9,... | collective-permute-start | bytes 3538952 | tf_op jit(solution)/shard_map/ppermute | solution.py:691
  127.0 27.9 %collective-permute-start.32 = (bf16[2,9,32,1024]{3,2,1,0:T(8,128)(2,1)}, bf16[2,9,32,1024]{3,2,1,0:T(8,128)(2,1)}, u32[]{:S(2)}, u32[]{:S(2)}) collective-permute-start(bf16[2,9,32,1024]{3,2,1,0:T(8,128)(2,1)} %collective-permute-done.27.rest_4_), channel_id=1, source_target_pairs={{0,1},{1,0},{2,3},{3,2},{4,5},{5,4},{6,7},{7,6},{8,9},{9,8},{10,11... | collective-permute-start | bytes 3538952 | tf_op jit(solution)/shard_map/ppermute | solution.py:691
  240.6 22.4 %collective-permute-start.39 = (bf16[16,4,32,1024]{3,2,1,0:T(8,128)(2,1)}, bf16[16,4,32,1024]{3,2,1,0:T(8,128)(2,1)}, u32[]{:S(2)}, u32[]{:S(2)}) collective-permute-start(bf16[16,4,32,1024]{3,2,1,0:T(8,128)(2,1)} %get-tuple-element.231), channel_id=1, source_target_pairs={{0,8},{1,9},{2,10},{3,11},{4,12},{5,13},{6,14},{7,15},{8,0},{9,1},... | collective-permute-start | bytes 12582920 | tf_op jit(solution)/shard_map/ppermute | solution.py:691
  262.0 16.1 %collective-permute-start.38 = (bf16[16,4,32,1024]{3,2,1,0:T(8,128)(2,1)}, bf16[16,4,32,1024]{3,2,1,0:T(8,128)(2,1)}, u32[]{:S(2)}, u32[]{:S(2)}) collective-permute-start(bf16[16,4,32,1024]{3,2,1,0:T(8,128)(2,1)} %get-tuple-element.227), channel_id=1, source_target_pairs={{0,8},{1,9},{2,10},{3,11},{4,12},{5,13},{6,14},{7,15},{8,0},{9,1},... | collective-permute-start | bytes 12582920 | tf_op jit(solution)/shard_map/ppermute | solution.py:691
  275.9 27.7 %collective-permute-start.41 = (bf16[4,4,32,1024]{3,2,1,0:T(8,128)(2,1)}, bf16[4,4,32,1024]{3,2,1,0:T(8,128)(2,1)S(1)}, u32[]{:S(2)}, u32[]{:S(2)}) collective-permute-start(bf16[4,4,32,1024]{3,2,1,0:T(8,128)(2,1)} %get-tuple-element.243), channel_id=1, source_target_pairs={{0,16},{1,17},{2,18},{3,19},{4,20},{5,21},{6,22},{7,23},{8,24},{9,... | collective-permute-start | bytes 3145736 | tf_op jit(solution)/shard_map/ppermute | solution.py:691
  277.4 26.3 %collective-permute-start.42 = (bf16[4,4,32,1024]{3,2,1,0:T(8,128)(2,1)}, bf16[4,4,32,1024]{3,2,1,0:T(8,128)(2,1)}, u32[]{:S(2)}, u32[]{:S(2)}) collective-permute-start(bf16[4,4,32,1024]{3,2,1,0:T(8,128)(2,1)} %get-tuple-element.245), channel_id=1, source_target_pairs={{0,1},{1,0},{2,3},{3,2},{4,5},{5,4},{6,7},{7,6},{8,9},{9,8},{10,11... | collective-permute-start | bytes 3145736 | tf_op jit(solution)/shard_map/ppermute | solution.py:691
  287.0 43.2 %collective-permute-start.43 = (bf16[4,5,32,1024]{3,2,1,0:T(8,128)(2,1)}, bf16[4,5,32,1024]{3,2,1,0:T(8,128)(2,1)S(1)}, u32[]{:S(2)}, u32[]{:S(2)}) collective-permute-start(bf16[4,5,32,1024]{3,2,1,0:T(8,128)(2,1)} %get-tuple-element.254), channel_id=1, source_target_pairs={{0,16},{1,17},{2,18},{3,19},{4,20},{5,21},{6,22},{7,23},{8,24},{9,... | collective-permute-start | bytes 3932168 | tf_op jit(solution)/shard_map/ppermute | solution.py:691
  288.6 43.2 %collective-permute-start.44 = (bf16[4,5,32,1024]{3,2,1,0:T(8,128)(2,1)}, bf16[4,5,32,1024]{3,2,1,0:T(8,128)(2,1)S(1)}, u32[]{:S(2)}, u32[]{:S(2)}) collective-permute-start(bf16[4,5,32,1024]{3,2,1,0:T(8,128)(2,1)} %get-tuple-element.256), channel_id=1, source_target_pairs={{0,1},{1,0},{2,3},{3,2},{4,5},{5,4},{6,7},{7,6},{8,9},{9,8},{10,11... | collective-permute-start | bytes 3932168 | tf_op jit(solution)/shard_map/ppermute | solution.py:691
  323.2 28.5 %collective-permute-start.45 = (bf16[2,4,32,1024]{3,2,1,0:T(8,128)(2,1)}, bf16[2,4,32,1024]{3,2,1,0:T(8,128)(2,1)S(1)}, u32[]{:S(2)}, u32[]{:S(2)}) collective-permute-start(bf16[2,4,32,1024]{3,2,1,0:T(8,128)(2,1)} %get-tuple-element.265), channel_id=1, source_target_pairs={{0,1},{1,0},{2,3},{3,2},{4,5},{5,4},{6,7},{7,6},{8,9},{9,8},{10,11... | collective-permute-start | bytes 1572872 | tf_op jit(solution)/shard_map/ppermute | solution.py:691
  324.6 27.2 %collective-permute-start.46 = (bf16[2,4,32,1024]{3,2,1,0:T(8,128)(2,1)}, bf16[2,4,32,1024]{3,2,1,0:T(8,128)(2,1)S(1)}, u32[]{:S(2)}, u32[]{:S(2)}) collective-permute-start(bf16[2,4,32,1024]{3,2,1,0:T(8,128)(2,1)} %get-tuple-element.267), channel_id=1, source_target_pairs={{0,16},{1,17},{2,18},{3,19},{4,20},{5,21},{6,22},{7,23},{8,24},{9,... | collective-permute-start | bytes 1572872 | tf_op jit(solution)/shard_map/ppermute | solution.py:691
  356.2 15.7 %collective-permute-start.47 = (bf16[2,5,32,1024]{3,2,1,0:T(8,128)(2,1)S(1)}, bf16[2,5,32,1024]{3,2,1,0:T(8,128)(2,1)S(1)}, u32[]{:S(2)}, u32[]{:S(2)}) collective-permute-start(bf16[2,5,32,1024]{3,2,1,0:T(8,128)(2,1)S(1)} %copy-done.38), channel_id=1, source_target_pairs={{0,1},{1,0},{2,3},{3,2},{4,5},{5,4},{6,7},{7,6},{8,9},{9,8},{10,11... | collective-permute-start | bytes 1966088 | tf_op jit(solution)/shard_map/ppermute | solution.py:691
  356.8 15.0 %collective-permute-start.48 = (bf16[2,5,32,1024]{3,2,1,0:T(8,128)(2,1)S(1)}, bf16[2,5,32,1024]{3,2,1,0:T(8,128)(2,1)S(1)}, u32[]{:S(2)}, u32[]{:S(2)}) collective-permute-start(bf16[2,5,32,1024]{3,2,1,0:T(8,128)(2,1)S(1)} %copy-done.37), channel_id=1, source_target_pairs={{0,16},{1,17},{2,18},{3,19},{4,20},{5,21},{6,22},{7,23},{8,24},{9,... | collective-permute-start | bytes 1966088 | tf_op jit(solution)/shard_map/ppermute | solution.py:691
  390.5 26.8 %collective-permute-start.49 = (bf16[16,3,32,1024]{3,2,1,0:T(8,128)(2,1)}, bf16[16,3,32,1024]{3,2,1,0:T(8,128)(2,1)S(1)}, u32[]{:S(2)}, u32[]{:S(2)}) collective-permute-start(bf16[16,3,32,1024]{3,2,1,0:T(8,128)(2,1)} %get-tuple-element.285), channel_id=1, source_target_pairs={{0,8},{1,9},{2,10},{3,11},{4,12},{5,13},{6,14},{7,15},{8,0},{9,1},... | collective-permute-start | bytes 9437192 | tf_op jit(solution)/shard_map/ppermute | solution.py:691
  390.5 35.7 %collective-permute-start.50 = (bf16[1,4,32,1024]{3,2,1,0:T(8,128)(2,1)}, bf16[1,4,32,1024]{3,2,1,0:T(8,128)(2,1)}, u32[]{:S(2)}, u32[]{:S(2)}) collective-permute-start(bf16[1,4,32,1024]{3,2,1,0:T(8,128)(2,1)} %get-tuple-element.287), channel_id=1, source_target_pairs={{0,2},{1,3},{2,4},{3,5},{4,6},{5,7},{6,0},{7,1},{8,10},{9,11},{10,... | collective-permute-start | bytes 786440 | tf_op jit(solution)/shard_map/ppermute | solution.py:691
  405.6 29.8 %collective-permute-start.53 = (bf16[1,5,32,1024]{3,2,1,0:T(8,128)(2,1)}, bf16[1,5,32,1024]{3,2,1,0:T(8,128)(2,1)S(1)}, u32[]{:S(2)}, u32[]{:S(2)}) collective-permute-start(bf16[1,5,32,1024]{3,2,1,0:T(8,128)(2,1)} %get-tuple-element.291), channel_id=1, source_target_pairs={{0,2},{1,3},{2,4},{3,5},{4,6},{5,7},{6,0},{7,1},{8,10},{9,11},{10,... | collective-permute-start | bytes 983048 | tf_op jit(solution)/shard_map/ppermute | solution.py:691
  408.0 22.4 %collective-permute-start.51 = (bf16[1,4,32,1024]{3,2,1,0:T(8,128)(2,1)}, bf16[1,4,32,1024]{3,2,1,0:T(8,128)(2,1)}, u32[]{:S(2)}, u32[]{:S(2)}) collective-permute-start(bf16[1,4,32,1024]{3,2,1,0:T(8,128)(2,1)} %get-tuple-element.288), channel_id=1, source_target_pairs={{0,4},{1,5},{2,6},{3,7},{4,0},{5,1},{6,2},{7,3},{8,12},{9,13},{10,... | collective-permute-start | bytes 786440 | tf_op jit(solution)/shard_map/ppermute | solution.py:691
  411.3 20.3 %collective-permute-start.52 = (bf16[1,4,32,1024]{3,2,1,0:T(8,128)(2,1)}, bf16[1,4,32,1024]{3,2,1,0:T(8,128)(2,1)}, u32[]{:S(2)}, u32[]{:S(2)}) collective-permute-start(bf16[1,4,32,1024]{3,2,1,0:T(8,128)(2,1)} %get-tuple-element.289), channel_id=1, source_target_pairs={{0,6},{1,7},{2,0},{3,1},{4,2},{5,3},{6,4},{7,5},{8,14},{9,15},{10,... | collective-permute-start | bytes 786440 | tf_op jit(solution)/shard_map/ppermute | solution.py:691
  424.8 27.9 %collective-permute-start.56 = (bf16[4,3,32,1024]{3,2,1,0:T(8,128)(2,1)}, bf16[4,3,32,1024]{3,2,1,0:T(8,128)(2,1)S(1)}, u32[]{:S(2)}, u32[]{:S(2)}) collective-permute-start(bf16[4,3,32,1024]{3,2,1,0:T(8,128)(2,1)} %get-tuple-element.295), channel_id=1, source_target_pairs={{0,16},{1,17},{2,18},{3,19},{4,20},{5,21},{6,22},{7,23},{8,24},{9,... | collective-permute-start | bytes 2359304 | tf_op jit(solution)/shard_map/ppermute | solution.py:691
  426.3 26.4 %collective-permute-start.57 = (bf16[4,3,32,1024]{3,2,1,0:T(8,128)(2,1)}, bf16[4,3,32,1024]{3,2,1,0:T(8,128)(2,1)S(1)}, u32[]{:S(2)}, u32[]{:S(2)}) collective-permute-start(bf16[4,3,32,1024]{3,2,1,0:T(8,128)(2,1)} %get-tuple-element.297), channel_id=1, source_target_pairs={{0,1},{1,0},{2,3},{3,2},{4,5},{5,4},{6,7},{7,6},{8,9},{9,8},{10,11... | collective-permute-start | bytes 2359304 | tf_op jit(solution)/shard_map/ppermute | solution.py:691
  430.3 30.1 %collective-permute-start.68 = (f32[4,1536]{1,0:T(4,128)S(1)}, f32[4,1536]{1,0:T(4,128)S(1)}, u32[]{:S(2)}, u32[]{:S(2)}) collective-permute-start(f32[4,1536]{1,0:T(4,128)S(1)} %bitcast.161), channel_id=1, source_target_pairs={{0,1},{1,0},{2,3},{3,2},{4,5},{5,4},{6,7},{7,6},{8,9},{9,8},{10,11... | collective-permute-start | bytes 73736 | tf_op jit(solution)/shard_map/ppermute | solution.py:691
  431.7 21.0 %collective-permute-start.54 = (bf16[1,5,32,1024]{3,2,1,0:T(8,128)(2,1)}, bf16[1,5,32,1024]{3,2,1,0:T(8,128)(2,1)S(1)}, u32[]{:S(2)}, u32[]{:S(2)}) collective-permute-start(bf16[1,5,32,1024]{3,2,1,0:T(8,128)(2,1)} %get-tuple-element.292), channel_id=1, source_target_pairs={{0,4},{1,5},{2,6},{3,7},{4,0},{5,1},{6,2},{7,3},{8,12},{9,13},{10,... | collective-permute-start | bytes 983048 | tf_op jit(solution)/shard_map/ppermute | solution.py:691
  435.4 17.2 %collective-permute-start.55 = (bf16[1,5,32,1024]{3,2,1,0:T(8,128)(2,1)}, bf16[1,5,32,1024]{3,2,1,0:T(8,128)(2,1)S(1)}, u32[]{:S(2)}, u32[]{:S(2)}) collective-permute-start(bf16[1,5,32,1024]{3,2,1,0:T(8,128)(2,1)} %get-tuple-element.293), channel_id=1, source_target_pairs={{0,6},{1,7},{2,0},{3,1},{4,2},{5,3},{6,4},{7,5},{8,14},{9,15},{10,... | collective-permute-start | bytes 983048 | tf_op jit(solution)/shard_map/ppermute | solution.py:691
  463.2 41.3 %collective-permute-start.72 = (bf16[1,9,32,1024]{3,2,1,0:T(8,128)(2,1)}, bf16[1,9,32,1024]{3,2,1,0:T(8,128)(2,1)S(1)}, u32[]{:S(2)}, u32[]{:S(2)}) collective-permute-start(bf16[1,9,32,1024]{3,2,1,0:T(8,128)(2,1)} %add_last.2.own), channel_id=1, source_target_pairs={{0,8},{1,9},{2,10},{3,11},{4,12},{5,13},{6,14},{7,15},{8,0},{9,1},... | collective-permute-start | bytes 1769480 | tf_op jit(solution)/shard_map/ppermute | solution.py:691
  473.3 14.9 %collective-permute-start.60 = (bf16[1,3,32,1024]{3,2,1,0:T(8,128)(2,1)}, bf16[1,3,32,1024]{3,2,1,0:T(8,128)(2,1)S(1)}, u32[]{:S(2)}, u32[]{:S(2)}) collective-permute-start(bf16[1,3,32,1024]{3,2,1,0:T(8,128)(2,1)} %get-tuple-element.305), channel_id=1, source_target_pairs={{0,2},{1,3},{2,4},{3,5},{4,6},{5,7},{6,0},{7,1},{8,10},{9,11},{10,... | collective-permute-start | bytes 589832 | tf_op jit(solution)/shard_map/ppermute | solution.py:691
  486.7 19.6 %collective-permute-start.73 = (bf16[1,9,32,1024]{3,2,1,0:T(8,128)(2,1)}, bf16[1,9,32,1024]{3,2,1,0:T(8,128)(2,1)S(1)}, u32[]{:S(2)}, u32[]{:S(2)}) collective-permute-start(bf16[1,9,32,1024]{3,2,1,0:T(8,128)(2,1)} %add_last.2.own), channel_id=1, source_target_pairs={{0,16},{1,17},{2,18},{3,19},{4,20},{5,21},{6,22},{7,23},{8,24},{9,... | collective-permute-start | bytes 1769480 | tf_op jit(solution)/shard_map/ppermute | solution.py:691
  488.1 26.7 %collective-permute-start.74 = (bf16[1,9,32,1024]{3,2,1,0:T(8,128)(2,1)}, bf16[1,9,32,1024]{3,2,1,0:T(8,128)(2,1)S(1)}, u32[]{:S(2)}, u32[]{:S(2)}) collective-permute-start(bf16[1,9,32,1024]{3,2,1,0:T(8,128)(2,1)} %add_last.2.own), channel_id=1, source_target_pairs={{0,24},{1,25},{2,26},{3,27},{4,28},{5,29},{6,30},{7,31},{8,16},{9,... | collective-permute-start | bytes 1769480 | tf_op jit(solution)/shard_map/ppermute | solution.py:691
  488.1 13.1 %collective-permute-start.61 = (bf16[1,3,32,1024]{3,2,1,0:T(8,128)(2,1)}, bf16[1,3,32,1024]{3,2,1,0:T(8,128)(2,1)S(1)}, u32[]{:S(2)}, u32[]{:S(2)}) collective-permute-start(bf16[1,3,32,1024]{3,2,1,0:T(8,128)(2,1)} %get-tuple-element.306), channel_id=1, source_target_pairs={{0,4},{1,5},{2,6},{3,7},{4,0},{5,1},{6,2},{7,3},{8,12},{9,13},{10,... | collective-permute-start | bytes 589832 | tf_op jit(solution)/shard_map/ppermute | solution.py:691
  488.2 13.0 %collective-permute-start.62 = (bf16[1,3,32,1024]{3,2,1,0:T(8,128)(2,1)}, bf16[1,3,32,1024]{3,2,1,0:T(8,128)(2,1)S(1)}, u32[]{:S(2)}, u32[]{:S(2)}) collective-permute-start(bf16[1,3,32,1024]{3,2,1,0:T(8,128)(2,1)} %get-tuple-element.307), channel_id=1, source_target_pairs={{0,6},{1,7},{2,0},{3,1},{4,2},{5,3},{6,4},{7,5},{8,14},{9,15},{10,... | collective-permute-start | bytes 589832 | tf_op jit(solution)/shard_map/ppermute | solution.py:691
  503.9 16.5 %collective-permute-start.63 = (bf16[1,3,32,1024]{3,2,1,0:T(8,128)(2,1)}, bf16[1,3,32,1024]{3,2,1,0:T(8,128)(2,1)S(1)}, u32[]{:S(2)}, u32[]{:S(2)}) collective-permute-start(bf16[1,3,32,1024]{3,2,1,0:T(8,128)(2,1)} %add_last.3.own), channel_id=1, source_target_pairs={{0,8},{1,9},{2,10},{3,11},{4,12},{5,13},{6,14},{7,15},{8,0},{9,1},... | collective-permute-start | bytes 589832 | tf_op jit(solution)/shard_map/ppermute | solution.py:691
  503.9 16.5 %collective-permute-start.64 = (bf16[1,3,32,1024]{3,2,1,0:T(8,128)(2,1)}, bf16[1,3,32,1024]{3,2,1,0:T(8,128)(2,1)S(1)}, u32[]{:S(2)}, u32[]{:S(2)}) collective-permute-start(bf16[1,3,32,1024]{3,2,1,0:T(8,128)(2,1)} %add_last.3.own), channel_id=1, source_target_pairs={{0,16},{1,17},{2,18},{3,19},{4,20},{5,21},{6,22},{7,23},{8,24},{9,... | collective-permute-start | bytes 589832 | tf_op jit(solution)/shard_map/ppermute | solution.py:691
  504.5 15.9 %collective-permute-start.65 = (bf16[1,3,32,1024]{3,2,1,0:T(8,128)(2,1)}, bf16[1,3,32,1024]{3,2,1,0:T(8,128)(2,1)S(1)}, u32[]{:S(2)}, u32[]{:S(2)}) collective-permute-start(bf16[1,3,32,1024]{3,2,1,0:T(8,128)(2,1)} %add_last.3.own), channel_id=1, source_target_pairs={{0,24},{1,25},{2,26},{3,27},{4,28},{5,29},{6,30},{7,31},{8,16},{9,... | collective-permute-start | bytes 589832 | tf_op jit(solution)/shard_map/ppermute | solution.py:691
  (73 other events, 627.6 us)

commit v3 on v2

--- a/solution.py
+++ b/solution.py
@@ -121,29 +121,35 @@
         own = (lane // HD) == h
         spare = (1 - h) * HD
         k_aug.append(jnp.where(own, k, jnp.where(lane == spare, bias, 0.0)).astype(BF))
-    v = v_ref[...]
+    v_aug = [jnp.where((lane // HD) == h, v_ref[...].astype(F32), 1.0).astype(BF) for h in range(2)]
     lane_q = lanes(rows)
 
-    for blk in range(slots // rows):
+    def scores(item):
+        blk, h = item
+        q = q_ref[blk * rows : (blk + 1) * rows, :].astype(F32) * 0.125
+        qh = jnp.where((lane_q // HD) == h, q, jnp.where(lane_q == (1 - h) * HD, 1.0, 0.0))
+        return qh, dot_nt(qh.astype(BF), k_aug[h])
+
+    items = [(blk, h) for blk in range(slots // rows) for h in range(2)]
+    held = scores(items[0])
+    outs = []
+    for i, (blk, h) in enumerate(items):
         sl = slice(blk * rows, (blk + 1) * rows)
-        q = q_ref[sl, :].astype(F32) * 0.125
-        outs = []
-        for h, qa_ref in enumerate((qa0_ref, qa1_ref)):
-            own = (lane_q // HD) == h
-            spare = (1 - h) * HD
-            qh = jnp.where(own, q, jnp.where(lane_q == spare, 1.0, 0.0))
-            s = dot_nt(qh.astype(BF), k_aug[h])
-            top = jnp.max(s, axis=-1, keepdims=True)
-            e = jnp.exp(s - top)
-            total = jnp.sum(e, axis=-1, keepdims=True)
-            o = dot_nn(e.astype(BF), v) / total
-            outs.append(o)
-            hi, mid, lo = split3(-(top + jnp.log(total)))
-            qh = jnp.where(lane_q == spare + 1, hi, qh)
-            qh = jnp.where(lane_q == spare + 2, mid, qh)
-            qh = jnp.where(lane_q == spare + 3, lo, qh)
-            qa_ref[sl, :] = qh.astype(BF)
-        ctx_ref[sl, :] = jnp.where(lane_q < HD, outs[0], outs[1]).astype(BF)
+        qh, s = held
+        if i + 1 < len(items):
+            held = scores(items[i + 1])
+        spare = (1 - h) * HD
+        top = jnp.max(s, axis=-1, keepdims=True)
+        o = dot_nn(jnp.exp(s - top).astype(BF), v_aug[h])
+        norm = o[:, spare : spare + 1]
+        outs.append(o / norm)
+        hi, mid, lo = split3(-(top + jnp.log(norm)))
+        qh = jnp.where(lane_q == spare + 1, hi, qh)
+        qh = jnp.where(lane_q == spare + 2, mid, qh)
+        qh = jnp.where(lane_q == spare + 3, lo, qh)
+        (qa0_ref, qa1_ref)[h][sl, :] = qh.astype(BF)
+        if h == 1:
+            ctx_ref[sl, :] = jnp.where(lane_q < HD, outs[-2], outs[-1]).astype(BF)
 
 
 def attn_fwd_call(qkv, lengths, part, parts, before, rows=256):
@@ -190,30 +196,38 @@
         k_aug.append(jnp.where(own, k, jnp.where(lane == spare, bias, ones)).astype(BF))
         v_aug.append(jnp.where(own, v, ones).astype(BF))
     lane_q = lanes(rows)
+    items = [(blk, h) for blk in range(slots // rows) for h in range(2)]
+
+    def products(item):
+        blk, h = item
+        sl = slice(blk * rows, (blk + 1) * rows)
+        own = (lane_q // HD) == h
+        spare = (1 - h) * HD
+        g = g_ref[sl, :].astype(F32)
+        delta = jnp.sum(jnp.where(own, g * ctx_ref[sl, :].astype(F32), 0.0), axis=-1, keepdims=True)
+        hi, mid, lo = split3(-delta)
+        ga = jnp.where(own, g, 0.0)
+        ga = jnp.where(lane_q == spare + 1, hi, ga)
+        ga = jnp.where(lane_q == spare + 2, mid, ga)
+        ga = jnp.where(lane_q == spare + 3, lo, ga).astype(BF)
+        return dot_nt(k_aug[h], (qa0_ref, qa1_ref)[h][sl, :]), dot_nt(v_aug[h], ga)
+
+    held = products(items[0])
     dk = [jnp.zeros((slots, 2 * HD), F32)] * 2
     dv = [jnp.zeros((slots, 2 * HD), F32)] * 2
-    for blk in range(slots // rows):
+    dqs = []
+    for i, (blk, h) in enumerate(items):
         sl = slice(blk * rows, (blk + 1) * rows)
-        g_low = g_ref[sl, :]
-        g = g_low.astype(F32)
-        prod = g * ctx_ref[sl, :].astype(F32)
-        dqs = []
-        for h, qa_ref in enumerate((qa0_ref, qa1_ref)):
-            own = (lane_q // HD) == h
-            spare = (1 - h) * HD
-            delta = jnp.sum(jnp.where(own, prod, 0.0), axis=-1, keepdims=True)
-            hi, mid, lo = split3(-delta)
-            ga = jnp.where(own, g, 0.0)
-            ga = jnp.where(lane_q == spare + 1, hi, ga)
-            ga = jnp.where(lane_q == spare + 2, mid, ga)
-            ga = jnp.where(lane_q == spare + 3, lo, ga).astype(BF)
-            qa = qa_ref[sl, :]
-            p = jnp.exp(dot_nt(k_aug[h], qa))
-            ds = (p * dot_nt(v_aug[h], ga)).astype(BF)
-            dv[h] = dv[h] + dot_nn(p.astype(BF), g_low)
-            dk[h] = dk[h] + dot_nn(ds, qa)
-            dqs.append(dot_tn(ds, k_low))
-        dq_ref[sl, :] = (jnp.where(lane_q < HD, dqs[0], dqs[1]) * 0.125).astype(BF)
+        s, gs = held
+        if i + 1 < len(items):
+            held = products(items[i + 1])
+        p = jnp.exp(s)
+        ds = (p * gs).astype(BF)
+        dv[h] = dv[h] + dot_nn(p.astype(BF), g_ref[sl, :])
+        dk[h] = dk[h] + dot_nn(ds, (qa0_ref, qa1_ref)[h][sl, :])
+        dqs.append(dot_tn(ds, k_low))
+        if h == 1:
+            dq_ref[sl, :] = (jnp.where(lane_q < HD, dqs[-2], dqs[-1]) * 0.125).astype(BF)
     dk_ref[...] = jnp.where(lane < HD, dk[0], dk[1]).astype(BF)
     dv_low = jnp.where(lane < HD, dv[0], dv[1]).astype(BF)
     dv_ref[...] = dv_low
@@ -304,7 +318,7 @@
     for n in range(nblk):
         pre = dot_nn(low, wi[n].reshape(width, width)) + bin_ref[n : n + 1, :]
         phi = 0.5 + 0.5 * lax.erf(pre * SQRT_HALF)
-        slope[n] = phi + pre * (INV_ROOT_TAU * jnp.exp(-0.5 * pre * pre))
+        slope[n] = (phi + pre * (INV_ROOT_TAU * jnp.exp(-0.5 * pre * pre))).astype(slope.dtype)
         act = (pre * phi).astype(BF)
         act_ref[:, n * width : (n + 1) * width] = act
         if n == 0:
@@ -325,7 +339,7 @@
     acc = g_resid2
     for n in range(nblk):
         g_act = dot_nt(gf, wo[n * per : (n + 1) * per].reshape(width, width))
-        gp = (g_act * slope[n]).astype(BF)
+        gp = (g_act * slope[n].astype(F32)).astype(BF)
         gp_ref[:, n * width : (n + 1) * width] = gp
         sbin_ref[n : n + 1, :] += colsum(gp.astype(F32))
         acc = acc + dot_nt(gp, wi[n].reshape(width, width))
@@ -343,7 +357,7 @@
     nblk = b_in.shape[0]
     ff = nblk * width
     blk = pl.BlockSpec((rows, width), lambda i, ln, p: (i, 0))
-    big = pl.BlockSpec((rows, ff), lambda i, ln, p: (i, 0))
+    big = pl.BlockSpec((rows, ff), lambda i, ln, p: (i, 0), pipeline_mode=pl.Buffered(1 if rows > 256 else 2))
     const = lambda r: pl.BlockSpec((r, width), lambda i, ln, p: (0, 0))
     o = jax.ShapeDtypeStruct((slots, width), BF)
     ob = jax.ShapeDtypeStruct((slots, ff), BF)
@@ -359,7 +373,7 @@
                 pltpu.VMEM((pieces, sub, width), BF),
                 pltpu.VMEM((nblk, pieces, sub, width), BF),
                 pltpu.VMEM((pieces, 4, sub, width), BF),
-                pltpu.VMEM((nblk, rows, width), F32),
+                pltpu.VMEM((nblk, rows, width), BF),
                 pltpu.SemaphoreType.DMA((3, pieces)),
             ],
         ),
@@ -373,42 +387,56 @@
     )(lengths, place, x, ctx, cot, vecs, b_in, *w2)
 
 
-def halves(core, value, group, keep_ref, send_ref):
-    value = value.reshape(-1, 2, group, SUB, value.shape[-1])
+def halves(core, value, keep_ref, send_ref):
+    count, rows, width = keep_ref.shape
+    value = value.reshape(count, 2, rows, width)
     even, odd = value[:, 0], value[:, 1]
-    shape = keep_ref.shape
 
     @pl.when(core == 0)
     def _():
-        keep_ref[...] = even.reshape(shape)
-        send_ref[...] = odd.reshape(shape)
+        keep_ref[...] = even
+        send_ref[...] = odd
 
     @pl.when(core != 0)
     def _():
-        keep_ref[...] = odd.reshape(shape)
-        send_ref[...] = even.reshape(shape)
-
-
-def wgrad_body(group, core, a_ref, b_ref, keep_ref, send_ref):
-    halves(core[0], dot_tn(a_ref[...], b_ref[...]).astype(BF), group, keep_ref, send_ref)
-
-
-def wgrad_call(name, core, a, b, by_rows, tile=256):
+        keep_ref[...] = odd
+        send_ref[...] = even
+
+
+LINES = 16
+
+
+def lines_of(*lines):
+    width, segments = lines[0][0], [line[1:] for line in lines]
+    row = lax.broadcasted_iota(jnp.int32, (LINES, width), 0)
+    value = jnp.zeros((LINES, width), F32)
+    for i, segs in enumerate(segments):
+        used = sum(v.shape[1] for v in segs)
+        line = jnp.concatenate([*segs, jnp.zeros((1, width - used), F32)], 1)
+        value = jnp.where(row == i, line, value)
+    return value.astype(BF)
+
+
+def wgrad_body(core, a_ref, b_ref, keep_ref, send_ref):
+    halves(core[0], dot_tn(a_ref[...], b_ref[...]).astype(BF), keep_ref, send_ref)
+
+
+def wgrad_call(name, core, a, b, by_rows, tile=1024):
     slots, m = a.shape
     width = a.shape[1] if not by_rows else b.shape[1]
     blocks = m // width if by_rows else b.shape[1] // m
     pieces = width // SUB
     if by_rows:
-        group, grid = blocks, (1, m // tile)
-        block = (tile // (2 * SUB * blocks), blocks, SUB, width)
-        where = lambda j, i, c: (i, 0, 0, 0)
+        grid = (1, m // tile)
+        block = (tile // (2 * SUB * blocks), blocks * SUB, width)
+        where = lambda j, i, c: (i, 0, 0)
     else:
-        group, grid = 1, (blocks, m // tile)
-        block = (tile // (2 * SUB), 1, SUB, width)
-        where = lambda j, i, c: (i, j, 0, 0)
-    out = jax.ShapeDtypeStruct((pieces // 2, blocks, SUB, width), BF)
-    return pl.pallas_call(
-        functools.partial(wgrad_body, group),
+        grid = (blocks, m // tile)
+        block = (tile // (2 * SUB), SUB, width)
+        where = lambda j, i, c: (i, j, 0)
+    out = jax.ShapeDtypeStruct((pieces // 2, blocks * SUB, width), BF)
+    return pl.pallas_call(
+        wgrad_body,
         name=name,
         grid_spec=pltpu.PrefetchScalarGridSpec(
             num_scalar_prefetch=1,
@@ -425,30 +453,75 @@
     )(core, a, b)
 
 
-def wgrad3_body(core, a_ref, q_ref, k_ref, v_ref, keep_ref, send_ref):
+def wgrad_ao_body(core, a_ref, b_ref, sums_ref, sbin_ref, keep_ref, send_ref):
+    value = dot_tn(a_ref[...], b_ref[...]).astype(BF)
+    halves(core[0], value, keep_ref.at[:, pl.ds(0, SUB)], send_ref.at[:, pl.ds(0, SUB)])
+    count, _, width = keep_ref.shape
+    owners = count // 2
+    part, four = width // owners, sbin_ref.shape[0] * width // owners
+    for s in range(owners):
+        segs = [sums_ref[v : v + 1, s * part : (s + 1) * part] for v in (5, 3, 4, 2, 0, 1)]
+        row, col = s * four // width, s * four % width
+        value = lines_of([width, *segs], [width, sbin_ref[row : row + 1, col : col + four]])
+        for ref in (keep_ref, send_ref):
+            for x in (0, 1):
+                ref[2 * s + x, SUB : SUB + LINES] = value
+
+
+def wgrad_ao(core, a, b, sums, sbin):
+    slots, m = a.shape
+    full = lambda v: pl.BlockSpec(v.shape, lambda t, c: (0, 0))
+    shape = (m // SUB // 2, SUB + LINES, m)
+    return pl.pallas_call(
+        wgrad_ao_body,
+        name="wgrad_ao",
+        grid_spec=pltpu.PrefetchScalarGridSpec(
+            num_scalar_prefetch=1,
+            grid=(1,),
+            in_specs=[full(v) for v in (a, b, sums, sbin)],
+            out_specs=[pl.BlockSpec(shape, lambda t, c: (0, 0, 0))] * 2,
+        ),
+        out_shape=[jax.ShapeDtypeStruct(shape, BF)] * 2,
+        compiler_params=params(),
+        cost_estimate=cost(2 * slots * m * m, 4 * slots * m + 2 * m * m),
+    )(core, a, b, sums, sbin)
+
+
+def wgrad3_body(core, a_ref, q_ref, k_ref, v_ref, sq_ref, sv_ref, keep_ref, send_ref):
     for n, ref in enumerate((q_ref, k_ref, v_ref)):
         value = dot_tn(a_ref[...], ref[...]).astype(BF)
-        halves(core[0], value, 1, keep_ref.at[:, pl.ds(n, 1)], send_ref.at[:, pl.ds(n, 1)])
-
-
-def wgrad3(core, a, dq, dk, dv, tile=256):
+        rows = pl.ds(n * SUB, SUB)
+        halves(core[0], value, keep_ref.at[:, rows], send_ref.at[:, rows])
+    count, _, width = keep_ref.shape
+    line = jnp.where(pl.program_id(0) == 0, sq_ref[...], sv_ref[...])
+    part = 2 * width // count
+    for s in range(count // 2):
+        value = lines_of([width, line[:, s * part : (s + 1) * part]])
+        for ref in (keep_ref, send_ref):
+            for x in (0, 1):
+                ref[2 * s + x, 3 * SUB : 3 * SUB + LINES] = value
+
+
+def wgrad3(core, a, dq, dk, dv, sq, sv):
     slots, m = a.shape
+    tile = m // 2
     full = pl.BlockSpec((slots, m), lambda i, c: (0, 0))
-    block = pl.BlockSpec((tile // (2 * SUB), 3, SUB, m), lambda i, c: (i, 0, 0, 0))
-    out = jax.ShapeDtypeStruct((m // SUB // 2, 3, SUB, m), BF)
+    vec = pl.BlockSpec((1, m), lambda i, c: (0, 0))
+    block = pl.BlockSpec((tile // (2 * SUB), 3 * SUB + LINES, m), lambda i, c: (i, 0, 0))
+    out = jax.ShapeDtypeStruct((m // SUB // 2, 3 * SUB + LINES, m), BF)
     return pl.pallas_call(
         wgrad3_body,
         name="wgrad_qkv",
         grid_spec=pltpu.PrefetchScalarGridSpec(
             num_scalar_prefetch=1,
-            grid=(m // tile,),
-            in_specs=[pl.BlockSpec((slots, tile), lambda i, c: (0, i)), full, full, full],
+            grid=(2,),
+            in_specs=[pl.BlockSpec((slots, tile), lambda i, c: (0, i)), full, full, full, vec, vec],
             out_specs=[block, block],
         ),
         out_shape=[out, out],
         compiler_params=params(),
         cost_estimate=cost(6 * slots * m * m, 14 * slots * m),
-    )(core, a, dq, dk, dv)
+    )(core, a, dq, dk, dv, sq, sv)
 
 
 def tok_body(count, place, g_ref, dq_ref, dk_ref, dv_ref, *rest):
@@ -513,18 +586,18 @@
         def where(t, h, half=half, own=own):
             z, j = 2 * half + t // 2, t % 2
             if half == 0:
-                return (z, j, h[0] if own else 1 - h[0], 0, 0, 0)
-            return (z, h[1] if own else 1 - h[1], j, 0, 0, 0)
+                return (z, j, h[0] if own else 1 - h[0], 0, 0)
+            return (z, h[1] if own else 1 - h[1], j, 0, 0)
         views.append(where)
-    specs, args, blocks = [], [], 0
+    specs, args, rows = [], [], 0
     for keep, got in pairs:
         n = keep.shape[1]
-        blocks += n
+        rows += n
         for where in views:
             for arr in (keep, got):
-                specs.append(pl.BlockSpec((1, 1, 1, n, SUB, width), where))
-                args.append(arr.reshape(4, 2, 2, n, SUB, width))
-    out = jax.ShapeDtypeStruct((4, blocks, SUB, width), BF)
+                specs.append(pl.BlockSpec((1, 1, 1, n, width), where))
+                args.append(arr.reshape(4, 2, 2, n, width))
+    out = jax.ShapeDtypeStruct((4, rows, width), BF)
     return pl.pallas_call(
         functools.partial(add1_body, len(pairs)),
         name="add_core",
@@ -532,32 +605,32 @@
             num_scalar_prefetch=1,
             grid=(4,),
             in_specs=specs,
-            out_specs=[pl.BlockSpec((1, blocks, SUB, width), lambda t, h: (t, 0, 0, 0))] * 4,
+            out_specs=[pl.BlockSpec((1, rows, width), lambda t, h: (t, 0, 0))] * 4,
         ),
         out_shape=[out] * 4,
         compiler_params=params(),
-        cost_estimate=cost(16 * blocks * SUB * width, 96 * blocks * SUB * width),
+        cost_estimate=cost(16 * rows * width, 96 * rows * width),
     )(here, *args)
 
 
 def add2_body(here, *refs):
-    ins, outs = refs[:8], refs[-4:]
+    ins, outs = refs[:8], refs[8:]
     for view in range(4):
         outs[view][0] = total(ins[2 * view][0, 0], ins[2 * view + 1][0, 0])
 
 
 def add2(here, first, second):
-    _, blocks, _, width = first[0].shape
+    _, rows, width = first[0].shape
     specs, args = [], []
     for axis, pair in ((1, first), (0, second)):
         for own in (0, 1):
             for arr in pair:
                 specs.append(pl.BlockSpec(
-                    (1, 1, blocks, SUB, width),
-                    lambda t, h, axis=axis, own=own: (t, h[axis] if own else 1 - h[axis], 0, 0, 0),
+                    (1, 1, rows, width),
+                    lambda t, h, axis=axis, own=own: (t, h[axis] if own else 1 - h[axis], 0, 0),
                 ))
-                args.append(arr.reshape(2, 2, blocks, SUB, width))
-    out = jax.ShapeDtypeStruct((2, blocks, SUB, width), BF)
+                args.append(arr.reshape(2, 2, rows, width))
+    out = jax.ShapeDtypeStruct((2, rows, width), BF)
     return pl.pallas_call(
         add2_body,
         name="add_plane",
@@ -565,11 +638,11 @@
             num_scalar_prefetch=1,
             grid=(2,),
             in_specs=specs,
-            out_specs=[pl.BlockSpec((1, blocks, SUB, width), lambda t, h: (t, 0, 0, 0))] * 4,
+            out_specs=[pl.BlockSpec((1, rows, width), lambda t, h: (t, 0, 0))] * 4,
         ),
         out_shape=[out] * 4,
         compiler_params=params(),
-        cost_estimate=cost(8 * blocks * SUB * width, 48 * blocks * SUB * width),
+        cost_estimate=cost(8 * rows * width, 48 * rows * width),
     )(here, *args)
 
 
@@ -588,18 +661,18 @@
 
 
 def add3(here, first, second):
-    _, blocks, _, width = first[0].shape
-    full = pl.BlockSpec((2, blocks, SUB, width), lambda t, h: (0, 0, 0, 0))
-    one = pl.BlockSpec((1, blocks, SUB, width), lambda t, h: (0, 0, 0, 0))
+    _, rows, width = first[0].shape
+    full = pl.BlockSpec((2, rows, width), lambda t, h: (0, 0, 0))
+    one = pl.BlockSpec((1, rows, width), lambda t, h: (0, 0, 0))
     return pl.pallas_call(
         add3_body,
         name="add_z",
         grid_spec=pltpu.PrefetchScalarGridSpec(
             num_scalar_prefetch=1, grid=(1,), in_specs=[full] * 4, out_specs=[one] * 4,
         ),
-        out_shape=[jax.ShapeDtypeStruct((1, blocks, SUB, width), BF)] * 4,
-        compiler_params=params(),
-        cost_estimate=cost(4 * blocks * SUB * width, 24 * blocks * SUB * width),
+        out_shape=[jax.ShapeDtypeStruct((1, rows, width), BF)] * 4,
+        compiler_params=params(),
+        cost_estimate=cost(4 * rows * width, 24 * rows * width),
     )(here, *first, *second)
 
 
@@ -614,10 +687,10 @@
 
 def add4(*groups):
     spec = lambda shape: pl.BlockSpec(shape, lambda t: (0,) * len(shape))
-    _, _, sub, width = groups[0][0].shape
-    shape = (1, sum(g[0].shape[1] for g in groups), sub, width)
+    width = groups[0][0].shape[-1]
+    shape = (1, sum(g[0].shape[1] for g in groups), width)
     parts = [v for g in groups for v in g]
-    size = shape[1] * sub * width
+    size = shape[1] * width
     return pl.pallas_call(
         add4_body,
         name="add_last",
@@ -630,35 +703,42 @@
     )(*parts)
 
 
-def final_body(kinds, here, own, core, over_x, both, *outs):
+def final_body(kinds, vectors, here, own, core, over_x, both, *outs):
     mine_at = 2 * here[0] + here[3]
+    mats, vecs = outs[: len(kinds)], outs[len(kinds) :]
     for flip, ref in enumerate((own, core, over_x, both)):
         share = jnp.bitwise_xor(mine_at, flip)
         n0 = 0
-        for (blocks, by_rows), out in zip(kinds, outs):
+        for (blocks, by_rows), out in zip(kinds, mats):
             width = ref.shape[-1]
             for n in range(blocks):
-                value = ref[0, n0 + n].astype(F32)
+                value = ref[0, n0 : n0 + SUB].astype(F32)
+                n0 += SUB
                 if by_rows:
                     out[pl.ds(pl.multiple_of(share * blocks * SUB, SUB) + n * SUB, SUB), :] = value
                 else:
                     out[pl.ds(pl.multiple_of(share * SUB, SUB), SUB), n * width : (n + 1) * width] = value
-            n0 += blocks
-
-
-def final_call(here, parts, kinds):
+
+        @pl.when(share == 0)
+        def _():
+            lines = ref[0, n0 : n0 + LINES].astype(F32)
+            for (row, lane, size), out in zip(vectors, vecs):
+                out[...] = lines[row : row + 1, lane : lane + size]
+
+
+def final_call(here, parts, kinds, vectors):
     shape = parts[0].shape
     width = shape[-1]
     shapes = [
         (4 * blocks * SUB, width) if by_rows else (4 * SUB, blocks * width) for blocks, by_rows in kinds
-    ]
-    return pl.pallas_call(
-        functools.partial(final_body, kinds),
+    ] + [(1, size) for _, _, size in vectors]
+    return pl.pallas_call(
+        functools.partial(final_body, kinds, vectors),
         name="final",
         grid_spec=pltpu.PrefetchScalarGridSpec(
             num_scalar_prefetch=1,
             grid=(1,),
-            in_specs=[pl.BlockSpec(shape, lambda t, h: (0, 0, 0, 0))] * 4,
+            in_specs=[pl.BlockSpec(shape, lambda t, h: (0, 0, 0))] * 4,
             out_specs=[pl.BlockSpec(sh, lambda t, h: (0, 0)) for sh in shapes],
         ),
         out_shape=[jax.ShapeDtypeStruct(sh, F32) for sh in shapes],
@@ -798,11 +878,6 @@
     return [own] + [move(v, TO_Z[k + 1]) for k, v in enumerate(sends)]
 
 
-def copies_of(*groups):
-    own = add4(*groups)
-    return own, move(own, TO_CORE), move(own, TO_X), move(own, TO_XCORE)
-
-
 def small_gather(plane):
     x, y, z, c = place_of()
     rows = jnp.concatenate([plane] + [move(plane, TO_Z[k]) for k in (1, 2, 3)], 0)
@@ -812,25 +887,13 @@
 
 
 def small_sum(rows):
-    s = lax.axis_index("shard")
-    if not regular():
-        return lax.dynamic_index_in_dim(lax.psum(rows, BOTH), s, 0, keepdims=False)
-    x, y, z, c = place_of()
-    rows = rows + move(rows, TO_CORE)
-    rows = rows + move(rows, TO_X)
-    rows = rows.reshape(4, 2, -1)
-    pick = lambda v, i, axis: lax.dynamic_index_in_dim(v, i, axis, keepdims=False)
-    rows = pick(rows, y, 1) + move(pick(rows, 1 - y, 1), TO_Y)
-    own = pick(rows, z, 0)
-    for k in (1, 2, 3):
-        own = own + move(pick(rows, (z + k) % 4, 0)[None], TO_Z[k])[0]
-    return own
+    return lax.dynamic_index_in_dim(lax.psum(rows, BOTH), lax.axis_index("shard"), 0, keepdims=False)
 
 
 def reduce_any(keep, send, by_rows):
-    half, blocks, _, wide = keep.shape
-    full = jnp.stack([keep, send], 1).reshape(2 * half, blocks, SUB, wide)
-    full = full.reshape(-1, wide) if by_rows else full.transpose(0, 2, 1, 3).reshape(-1, blocks * wide)
+    half, rows, wide = keep.shape
+    full = jnp.stack([keep, send], 1).reshape(2 * half, rows // SUB, SUB, wide)
+    full = full.reshape(-1, wide) if by_rows else full.transpose(0, 2, 1, 3).reshape(2 * half * SUB, -1)
     part = lax.psum_scatter(full, "shard", scatter_dimension=0, tiled=True)
     return lax.psum(part, "replica").astype(F32)
 
@@ -856,16 +919,15 @@
         rows = small_gather(after(plane, a1, b1))
         second, _ = pack(share, [w_attn_out, w_ffn_in, w_ffn_out], [b_qv], width)
         second = after(second, a1, b1, rows)
-        near = move(second, TO_Z[1])
+        near, *far = [move(second, TO_Z[k]) for k in (1, 2, 3)]
         plane = [move(a1, TO_Y), move(b1, TO_X), move(a1, TO_X), move(b1, TO_Y)]
         first = [a1, b1]
         cores = to_core(first)
         plane, cores = tied(plane, cores)
         last = [move(plane[0], TO_X), move(plane[1], TO_Y)]
         more = to_core(plane)
-        last, more, [near, second] = tied(last, more, [near, second])
+        _, [near, far[1]] = tied(last, [near, far[1]])
         w1 = [*first, *plane, *last, *cores, *more, *to_core(last)]
-        far = [move(second, TO_Z[k]) for k in (2, 3)]
         a2 = jnp.concatenate([second, near], 0)
         ya2, xa2 = move(a2, TO_Y), move(a2, TO_X)
         place = gather_places(((0, 0, 0), (2, 0, 0), (0, 0, 1), (2, 1, 0), (0, 1, 0), (2, 0, 1), (0, 1, 1), (2, 1, 1)))
@@ -914,10 +976,6 @@
     out, act, low, gf, gp, ga, gc, sums, sbin = row_call(
         x, ctx, cot, place2, w2, vecs, b_in.reshape(nblk, width), lengths
     )
-    def small_rows(sq, sv):
-        vs = [jnp.concatenate([sq[0], sv[0]]), sums[5], sums[3], sums[4], sbin, sums[2], sums[0], sums[1]]
-        return jnp.concatenate([v.reshape(count, -1) for v in vs], 1)
-
     p_wout = wgrad_call("wgrad_out", core, act, gf, True)
     p_win = wgrad_call("wgrad_in", core, low, gp, False)
     state = None
@@ -925,7 +983,7 @@
     if regular():
         swap = lambda p: (p[0], move(p[1], TO_CORE))
         r_out = sum_core(here, [swap(p_wout)])
-        p_wao = wgrad_call("wgrad_ao", core, ctx, after(ga, r_out[0][0]), False)
+        p_wao = wgrad_ao(core, ctx, after(ga, r_out[0][0]), sums, sbin)
         r_in = sum_core(here, [swap(p_win), swap(p_wao)])
         def hold(r, state):
             (k0, g0), second = r
@@ -944,29 +1002,42 @@
         state = bwd(3, state, gc)
         r_in = sum_z(here, *hold(r_in, state))
         dq, dk, dv, sq, sv = state
-        own = small_sum(small_rows(sq, sv))
-        p_wqkv = wgrad3(core, after(x, r_in[0]), dq, dk, dv)
-        r_qkv = sum_core(here, [swap(p_wqkv)])
-        g_tok = tok_call(after(ga, r_qkv[0][0], *r_out[1:]), dq, dk, dv, place, w1)
+        p_wqkv = wgrad3(core, after(x, r_in[0], *r_out[1:]), dq, dk, dv, sq, sv)
+        keep, send = p_wqkv
+        r_qkv = sum_core(here, [swap((keep, after(send, r_in[1], r_in[3])))])
+        g_tok = tok_call(after(ga, r_qkv[0][0]), dq, dk, dv, place, w1)
         (k0, g0), second = r_qkv
-        r_qkv = sum_plane(here, (after(k0, g_tok, *r_in[1:]), g0), second)
-        r_rest = copies_of([after(r_out[0], r_qkv[0][0]), *r_out[1:]], r_in)
-        (k0, g0), second = r_qkv
-        r_qkv = sum_z(here, (after(k0, r_rest[0], own), g0), second)
-        g_wout, g_win, g_wao = final_call(here, r_rest, [(4, True), (nblk, False), (1, False)])
-        (g_wqkv,) = final_call(here, copies_of(r_qkv), [(3, False)])
+        r_qkv = sum_plane(here, (after(k0, g_tok, r_in[2]), g0), second)
+        rest = add4(r_out, [after(r_in[0], r_qkv[0][0]), *r_in[1:]])
+        own, *far = sum_z(here, *r_qkv)
+        over_x = move(after(rest, own), TO_X)
+        own = add4([own, *far])
+        [rest, over_x], [own] = tied([rest, over_x], [own])
+        vectors = [(0, 128 * i, 128) for i in range(6)] + [(1, 0, nblk * 128)]
+        g_wout, g_win, g_wao, g_bao, g_g1, g_s1, g_bout, g_g2, g_s2, g_bin = final_call(
+            here,
+            (rest, move(rest, TO_CORE), over_x, move(over_x, TO_CORE)),
+            [(4, True), (nblk, False), (1, False)],
+            vectors,
+        )
+        over_x = move(own, TO_X)
+        over_x, g_wout = lax.optimization_barrier((over_x, g_wout))
+        shares = (own, move(own, TO_CORE), over_x, move(over_x, TO_CORE))
+        g_wqkv, g_bqv = final_call(here, shares, [(3, False)], [(0, 0, 256)])
+        vecs = [v.reshape(-1) for v in (g_bqv, g_bao, g_g1, g_s1, g_bin, g_bout, g_g2, g_s2)]
     else:
         p_wao = wgrad_call("wgrad_ao", core, ctx, ga, False)
         for i in range(parts):
             state = bwd(i, state, gc)
         dq, dk, dv, sq, sv = state
-        own = small_sum(small_rows(sq, sv))
-        p_wqkv = wgrad3(core, x, dq, dk, dv)
+        p_wqkv = [v[:, : 3 * SUB] for v in wgrad3(core, x, dq, dk, dv, sq, sv)]
         g_tok = tok_call(ga, dq, dk, dv, place, w1)
         g_wout = reduce_any(*p_wout, True)
         g_win, g_wao, g_wqkv = [reduce_any(*p, False) for p in (p_win, p_wao, p_wqkv)]
-
-    g_bqv, g_bao, g_g1, g_s1, g_bin, g_bout, g_g2, g_s2 = [own[e - s : e] for s, e in zip(sizes, ends)]
+        vecs = [jnp.concatenate([sq[0], sv[0]]), sums[5], sums[3], sums[4], sbin, sums[2], sums[0], sums[1]]
+        own = small_sum(jnp.concatenate([v.reshape(count, -1) for v in vecs], 1))
+        vecs = [own[e - s : e] for s, e in zip(sizes, ends)]
+    g_bqv, g_bao, g_g1, g_s1, g_bin, g_bout, g_g2, g_s2 = vecs
     return (
         out[None], g_tok[None], g_wqkv, g_bqv, g_wao, g_bao, g_g1, g_s1,
         g_win, g_bin, g_wout, g_bout, g_g2, g_s2,

time: 530 us -> 497 us (0.938)
  starting transfers between devices: 97.6 us -> 61.9 us
  waiting for transfers between devices: 86.2 us -> 117 us
  Pallas kernels: 308 us -> 286 us
    ppermute x75 -> x69, starting transfers between devices: 97.6 us -> 61.9 us  [move(): return lax.ppermute(v, AXES, pairs)]
    ppermute x75 -> x69, waiting for transfers between devices: 86.2 us -> 117 us  [move(): return lax.ppermute(v, AXES, pairs)]
    pallas_call x5, Pallas kernels: 54.6 us -> 42.8 us  [the longest x2 28.2 us: wgrad_call(): pl.pallas_call(wgrad_body, name=name, grid_spec=pltpu.PrefetchScalarGridS...]
    pallas_call x4, Pallas kernels: 43.5 us -> 32.3 us  [attn_fwd_call(): pl.pallas_call(functools.partial(attn_fwd_body, rows), name=f'attn_fwd{pa...]
    unnamed x106 -> x89, local copies, waits for them, and re-layouts: 17 us -> 17.3 us
  transfers between devices with their start and end apart: 75 -> 69, of which waited for: 28 -> 31; matrix products, arithmetic and copies ran while one was open for 3% -> 2% of each run, Pallas kernels for 39% -> 38%
where the time goes in v3:
time: 497 us; the launch traced here: 492 us
  Pallas kernels  286 us (58%)
  waiting for transfers between devices  117 us (24%)
  starting transfers between devices  61.9 us (12%)
  local copies, waits for them, and re-layouts  23.5 us (5%)
    ppermute x69, waiting for transfers between devices, move(): return lax.ppermute(v, AXES, pairs)  117 us
    ppermute x69, starting transfers between devices, move(): return lax.ppermute(v, AXES, pairs)  61.9 us
    pallas_call x1, Pallas kernels, row_call(): pl.pallas_call(functools.partial(row_body, len(w2)), name='row_local', gr...  60.7 us
    pallas_call x4, Pallas kernels, attn_bwd_call(): pl.pallas_call(functools.partial(attn_bwd_body, rows), name=f'attn_bwd{pa...  56.8 us
    pallas_call x4, Pallas kernels, attn_fwd_call(): pl.pallas_call(functools.partial(attn_fwd_body, rows), name=f'attn_fwd{pa...  32.3 us
    pallas_call x2, Pallas kernels, wgrad_call(): pl.pallas_call(wgrad_body, name=name, grid_spec=pltpu.PrefetchScalarGridS...  28.2 us
    pallas_call x3, Pallas kernels, add1(): pl.pallas_call(functools.partial(add1_body, len(pairs)), name='add_core',...  20.8 us
    unnamed x89, local copies, waits for them, and re-layouts  17.3 us
  transfers between devices with their start and end apart: 69, of which 31 were waited for; matrix products, arithmetic and copies ran while one was open for 2% of the time, Pallas kernels for 38%

profile of v3, /device:TPU:0, one launch (start us, length us, event | category | flops | bytes accessed | tf_op | source)
XLA Modules:
  0.0 492.5 jit_solution(2913184555193336005)
XLA Ops:
  4.8 5.0 %collective-permute-start.2 = (bf16[1,3,32,1024]{3,2,1,0:T(8,128)(2,1)}, bf16[1,3,32,1024]{3,2,1,0:T(8,128)(2,1)S(1)}, u32[]{:S(2)}, u32[]{:S(2)}) collective-permute-start(bf16[1,3,32,1024]{3,2,1,0:T(8,128)(2,1)} %get-tuple-element.174), channel_id=1, source_target_pairs={{0,6},{1,7},{2,0},{3,1},{4,2},{5,3},{6,4},{7,5},{8,14},{9,15},{10,... | collective-permute-start | bytes 589832 | tf_op jit(solution)/shard_map/ppermute | solution.py:771
  15.4 8.2 %collective-permute-done = bf16[1,3,32,1024]{3,2,1,0:T(8,128)(2,1)S(1)} collective-permute-done((bf16[1,3,32,1024]{3,2,1,0:T(8,128)(2,1)}, bf16[1,3,32,1024]{3,2,1,0:T(8,128)(2,1)S(1)}, u32[]{:S(2)}, u32[]{:S(2)}) %collective-permute-start) | collective-permute-done | bytes 196640 | tf_op jit(solution)/shard_map/ppermute | solution.py:771
  27.3 5.7 %collective-permute-start.5 = (bf16[2,1536]{1,0:T(2,128)(2,1)S(1)}, bf16[2,1536]{1,0:T(2,128)(2,1)S(1)}, u32[]{:S(2)}, u32[]{:S(2)}) collective-permute-start(bf16[2,1536]{1,0:T(2,128)(2,1)S(1)} %pad_maximum_fusion.1), channel_id=1, source_target_pairs={{0,4},{1,5},{2,6},{3,7},{4,0},{5,1},{6,2},{7,3},{8,12},{9,13},{10,... | collective-permute-start | bytes 18440 | tf_op jit(solution)/shard_map/ppermute | solution.py:771
  33.0 2.1 collective-permute-start.4
  42.3 9.9 %collective-permute-done.11.rest_5_ = bf16[2,3,32,1024]{3,2,1,0:T(8,128)(2,1)} collective-permute-done((bf16[2,3,32,1024]{3,2,1,0:T(8,128)(2,1)S(1)}, bf16[2,3,32,1024]{3,2,1,0:T(8,128)(2,1)}, u32[]{:S(2)}, u32[]{:S(2)}) %collective-permute-start.11) | collective-permute-done | bytes 393248 | tf_op jit(solution)/shard_map/ppermute | solution.py:771
  55.0 11.2 %collective-permute-done.16 = bf16[1,9,32,1024]{3,2,1,0:T(8,128)(2,1)S(1)} collective-permute-done((bf16[1,9,32,1024]{3,2,1,0:T(8,128)(2,1)}, bf16[1,9,32,1024]{3,2,1,0:T(8,128)(2,1)S(1)}, u32[]{:S(2)}, u32[]{:S(2)}) %collective-permute-start.16) | collective-permute-done | bytes 589856 | tf_op jit(solution)/shard_map/ppermute | solution.py:771
  72.8 13.5 %qkv.1.q_ref.k_ref.v_ref = bf16[1024,3072]{1,0:T(8,128)(2,1)} custom-call(s32[32]{0:T(128)} %stack.224.place, bf16[1024,1024]{1,0:T(8,128)(2,1)} %bitcast.158, f32[1,3072]{1,0:T(1,128)} %bitcast.150, bf16[2,3,32,1024]{3,2,1,0:T(8,128)(2,1)} %copy-done.31, bf16[2,3,32,1024]{3,2,1,0:T(8,128)(2,1)} %copy-done.32, ...), custom_call_target="tpu_custom_call" | custom-call | flops 6442450944 | bytes 14680064 | tf_op jit(solution)/shard_map/qkv/pallas_call | solution.py:80
  86.3 8.0 %attn_fwd0.1 = (bf16[1024,1024]{1,0:T(8,128)(2,1)}, bf16[1024,1024]{1,0:T(8,128)(2,1)}, bf16[1024,1024]{1,0:T(8,128)(2,1)}) custom-call(s32[1]{0:T(128)S(6)} %copy.83.len_ref, bf16[1024,3072]{1,0:T(8,128)(2,1)} %qkv.1.q_ref.k_ref.v_ref, bf16[1024,3072]{1,0:T(8,128)(2,1)} %qkv.1.q_ref.k_ref.v_ref, bf16[1024,3072]{1,0:T(8,128)(2,1)} %qkv.1.q_ref.k_ref.v_ref), custom_call_target="tpu_custom_call" | custom-call | flops 4294967296 | bytes 3145728 | tf_op jit(solution)/shard_map/attn_fwd0/pallas_call | solution.py:163
  94.3 5.4 %collective-permute-done.7 = bf16[1,9,32,1024]{3,2,1,0:T(8,128)(2,1)S(1)} collective-permute-done((bf16[1,9,32,1024]{3,2,1,0:T(8,128)(2,1)S(1)}, bf16[1,9,32,1024]{3,2,1,0:T(8,128)(2,1)S(1)}, u32[]{:S(2)}, u32[]{:S(2)}) %collective-permute-start.7) | collective-permute-done | bytes 589856 | tf_op jit(solution)/shard_map/ppermute | solution.py:771
  104.9 8.0 %attn_fwd1.1 = (bf16[1024,1024]{1,0:T(8,128)(2,1)}, bf16[1024,1024]{1,0:T(8,128)(2,1)}, bf16[1024,1024]{1,0:T(8,128)(2,1)}) custom-call(s32[1]{0:T(128)S(6)} %copy.83.len_ref, bf16[1024,3072]{1,0:T(8,128)(2,1)} %qkv.1.q_ref.k_ref.v_ref, bf16[1024,3072]{1,0:T(8,128)(2,1)} %qkv.1.q_ref.k_ref.v_ref, ...), custom_call_target="tpu_custom_call", output_to_operand_aliasing={{0}: (4, {}), {1}: (5, {}), {2}: (6, {})} | custom-call | flops 4294967296 | bytes 3145728 | tf_op jit(solution)/shard_map/attn_fwd1/pallas_call | solution.py:163
  113.0 8.0 %attn_fwd2.1 = (bf16[1024,1024]{1,0:T(8,128)(2,1)}, bf16[1024,1024]{1,0:T(8,128)(2,1)}, bf16[1024,1024]{1,0:T(8,128)(2,1)}) custom-call(s32[1]{0:T(128)S(6)} %copy.83.len_ref, bf16[1024,3072]{1,0:T(8,128)(2,1)} %qkv.1.q_ref.k_ref.v_ref, bf16[1024,3072]{1,0:T(8,128)(2,1)} %qkv.1.q_ref.k_ref.v_ref, ...), custom_call_target="tpu_custom_call", output_to_operand_aliasing={{0}: (4, {}), {1}: (5, {}), {2}: (6, {})} | custom-call | flops 4294967296 | bytes 3145728 | tf_op jit(solution)/shard_map/attn_fwd2/pallas_call | solution.py:163
  121.0 9.1 %collective-permute-done.28.rest_5_ = bf16[2,9,32,1024]{3,2,1,0:T(8,128)(2,1)S(1)} collective-permute-done((bf16[2,9,32,1024]{3,2,1,0:T(8,128)(2,1)}, bf16[2,9,32,1024]{3,2,1,0:T(8,128)(2,1)S(1)}, u32[]{:S(2)}, u32[]{:S(2)}) %collective-permute-start.28) | collective-permute-done | bytes 1179680 | tf_op jit(solution)/shard_map/ppermute | solution.py:771
  136.9 8.2 %attn_fwd3.1 = (bf16[1024,1024]{1,0:T(8,128)(2,1)}, bf16[1024,1024]{1,0:T(8,128)(2,1)}, bf16[1024,1024]{1,0:T(8,128)(2,1)}) custom-call(s32[1]{0:T(128)S(6)} %copy.83.len_ref, bf16[1024,3072]{1,0:T(8,128)(2,1)} %qkv.1.q_ref.k_ref.v_ref, bf16[1024,3072]{1,0:T(8,128)(2,1)} %qkv.1.q_ref.k_ref.v_ref, ...), custom_call_target="tpu_custom_call", output_to_operand_aliasing={{0}: (4, {}), {1}: (5, {}), {2}: (6, {})} | custom-call | flops 4294967296 | bytes 3145728 | tf_op jit(solution)/shard_map/attn_fwd3/pallas_call | solution.py:163
  145.1 15.0 %collective-permute-done.26.rest_6_ = bf16[2,9,32,1024]{3,2,1,0:T(8,128)(2,1)} collective-permute-done((bf16[2,9,32,1024]{3,2,1,0:T(8,128)(2,1)}, bf16[2,9,32,1024]{3,2,1,0:T(8,128)(2,1)}, u32[]{:S(2)}, u32[]{:S(2)}) %collective-permute-start.26) | collective-permute-done | bytes 1179680 | tf_op jit(solution)/shard_map/ppermute | solution.py:771
  167.1 60.7 %row_local.1 = (bf16[1024,1024]{1,0:T(8,128)(2,1)}, bf16[1024,4096]{1,0:T(8,128)(2,1)}, bf16[1024,1024]{1,0:T(8,128)(2,1)}, bf16[1024,1024]{1,0:T(8,128)(2,1)}, ...) custom-call(s32[1]{0:T(128)S(6)} %copy.83.len_ref, ...), custom_call_target="tpu_custom_call" | custom-call | flops 38654705664 | bytes 60817408 | tf_op jit(solution)/shard_map/row_local/pallas_call | solution.py:364
  227.8 14.3 %wgrad_out.1 = (bf16[16,128,1024]{2,1,0:T(8,128)(2,1)}, bf16[16,128,1024]{2,1,0:T(8,128)(2,1)}) custom-call(s32[1]{0:T(128)} %bitcast.60.core, bf16[1024,4096]{1,0:T(8,128)(2,1)} %get-tuple-element.231.a_ref, bf16[1024,1024]{1,0:T(8,128)(2,1)} %get-tuple-element.232.b_ref), custom_call_target="tpu_custom_call" | custom-call | flops 8589934592 | bytes 18874368 | tf_op jit(solution)/shard_map/wgrad_out/pallas_call | solution.py:438
  242.3 13.9 %wgrad_in.1 = (bf16[16,128,1024]{2,1,0:T(8,128)(2,1)}, bf16[16,128,1024]{2,1,0:T(8,128)(2,1)}) custom-call(s32[1]{0:T(128)} %bitcast.60.core, bf16[1024,1024]{1,0:T(8,128)(2,1)} %get-tuple-element.227.a_ref, bf16[1024,4096]{1,0:T(8,128)(2,1)} %get-tuple-element.228.b_ref), custom_call_target="tpu_custom_call" | custom-call | flops 8589934592 | bytes 18874368 | tf_op jit(solution)/shard_map/wgrad_in/pallas_call | solution.py:438
  257.2 6.5 %add_core.3 = (bf16[4,128,1024]{2,1,0:T(8,128)(2,1)}, bf16[4,128,1024]{2,1,0:T(8,128)(2,1)}, bf16[4,128,1024]{2,1,0:T(8,128)(2,1)}, bf16[4,128,1024]{2,1,0:T(8,128)(2,1)}) custom-call(s32[4]{0:T(128)} %pad_add_fusion.here, bf16[4,2,2,128,1024]{4,3,2,1,0:T(8,128)(2,1)} %bitcast.100, bf16[4,2,2,128,1024]{4,3,2,1,0:T(8,128)(2,1)} %bitcast.64.refs_1_.refs_3_.refs_5_.refs_7_, ...), custom_call_target="tpu_custom_call" | custom-call | flops 2097152 | bytes 12582912 | tf_op jit(solution)/shard_map/add_core/pallas_call | solution.py:601
  263.7 6.5 %wgrad_ao.1 = (bf16[16,48,1024]{2,1,0:T(8,128)(2,1)}, bf16[16,48,1024]{2,1,0:T(8,128)(2,1)}) custom-call(s32[1]{0:T(128)} %bitcast.60.core, bf16[1024,1024]{1,0:T(8,128)(2,1)} %get-tuple-element.216.ctx_ref.a_ref, bf16[1024,1024]{1,0:T(8,128)(2,1)} %get-tuple-element.299.b_ref.g_ref, f32[8,1024]{1,0:T(8,128)} %get-tuple-element.237.sums_ref, ...), custom_call_target="tpu_custom_call" | custom-call | flops 2147483648 | bytes 6291456 | tf_op jit(solution)/shard_map/wgrad_ao/pallas_call | solution.py:475
  271.5 2.4 collective-permute-done.40
  275.1 8.1 %add_core.4 = (bf16[4,176,1024]{2,1,0:T(8,128)(2,1)}, bf16[4,176,1024]{2,1,0:T(8,128)(2,1)}, bf16[4,176,1024]{2,1,0:T(8,128)(2,1)}, bf16[4,176,1024]{2,1,0:T(8,128)(2,1)}) custom-call(s32[4]{0:T(128)} %pad_add_fusion.here, bf16[4,2,2,128,1024]{4,3,2,1,0:T(8,128)(2,1)} %bitcast.96, bf16[4,2,2,128,1024]{4,3,2,1,0:T(8,128)(2,1)} %bitcast.62.refs_1_.refs_3_.refs_5_.refs_7_, ...), custom_call_target="tpu_custom_call" | custom-call | flops 2883584 | bytes 17301504 | tf_op jit(solution)/shard_map/add_core/pallas_call | solution.py:601
  284.3 14.0 %attn_bwd0.1 = (bf16[1024,1024]{1,0:T(8,128)(2,1)}, bf16[1024,1024]{1,0:T(8,128)(2,1)}, bf16[1024,1024]{1,0:T(8,128)(2,1)}, f32[1,1024]{1,0:T(1,128)}, f32[1,1024]{1,0:T(1,128)}) custom-call(s32[1]{0:T(128)S(6)} %copy.83.len_ref, bf16[1024,1024]{1,0:T(8,128)(2,1)} %get-tuple-element.242.qa0_ref, bf16[1024,1024]{1,0:T(8,128)(2,1)} %get-tuple-element.243.qa1_ref, ...), custom_call_target="tpu_custom_call" | custom-call | flops 10737418240 | bytes 4718592 | tf_op jit(solution)/shard_map/attn_bwd0/pallas_call | solution.py:247
  299.3 4.0 add_plane.3
  303.2 14.2 %attn_bwd1.1 = (bf16[1024,1024]{1,0:T(8,128)(2,1)}, bf16[1024,1024]{1,0:T(8,128)(2,1)}, bf16[1024,1024]{1,0:T(8,128)(2,1)}, f32[1,1024]{1,0:T(1,128)}, f32[1,1024]{1,0:T(1,128)}) custom-call(s32[1]{0:T(128)S(6)} %copy.83.len_ref, ...), custom_call_target="tpu_custom_call", output_to_operand_aliasing={{0}: (7, {}), {1}: (8, {}), {2}: (9, {}), {3}: (10, {}), {4... | custom-call | flops 10737418240 | bytes 4718592 | tf_op jit(solution)/shard_map/attn_bwd1/pallas_call | solution.py:247
  320.5 7.0 %collective-permute-done.43 = bf16[4,176,1024]{2,1,0:T(8,128)(2,1)S(1)} collective-permute-done((bf16[4,176,1024]{2,1,0:T(8,128)(2,1)}, bf16[4,176,1024]{2,1,0:T(8,128)(2,1)S(1)}, u32[]{:S(2)}, u32[]{:S(2)}) %collective-permute-start.43) | collective-permute-done | bytes 1441824 | tf_op jit(solution)/shard_map/ppermute | solution.py:771
  329.1 4.7 add_plane.4
  333.8 14.2 %attn_bwd2.1 = (bf16[1024,1024]{1,0:T(8,128)(2,1)}, bf16[1024,1024]{1,0:T(8,128)(2,1)}, bf16[1024,1024]{1,0:T(8,128)(2,1)}, f32[1,1024]{1,0:T(1,128)}, f32[1,1024]{1,0:T(1,128)}) custom-call(s32[1]{0:T(128)S(6)} %copy.83.len_ref, ...), custom_call_target="tpu_custom_call", output_to_operand_aliasing={{0}: (7, {}), {1}: (8, {}), {2}: (9, {}), {3}: (10, {}), {4... | custom-call | flops 10737418240 | bytes 4718592 | tf_op jit(solution)/shard_map/attn_bwd2/pallas_call | solution.py:247
  349.0 3.4 add_z.3
  352.5 2.7 collective-permute-start.50
  358.4 14.3 %attn_bwd3.1 = (bf16[1024,1024]{1,0:T(8,128)(2,1)}, bf16[1024,1024]{1,0:T(8,128)(2,1)}, bf16[1024,1024]{1,0:T(8,128)(2,1)}, f32[1,1024]{1,0:T(1,128)}, f32[1,1024]{1,0:T(1,128)}) custom-call(s32[1]{0:T(128)S(6)} %copy.83.len_ref, ...), custom_call_target="tpu_custom_call", output_to_operand_aliasing={{0}: (7, {}), {1}: (8, {}), {2}: (9, {}), {3}: (10, {}), {4... | custom-call | flops 10737418240 | bytes 4718592 | tf_op jit(solution)/shard_map/attn_bwd3/pallas_call | solution.py:247
  374.1 3.9 add_z.4
  378.7 3.2 collective-permute-start.53
  381.9 14.0 %wgrad_qkv.1 = (bf16[16,112,1024]{2,1,0:T(8,128)(2,1)}, bf16[16,112,1024]{2,1,0:T(8,128)(2,1)}) custom-call(s32[1]{0:T(128)} %bitcast.60.core, bf16[1024,1024]{1,0:T(8,128)(2,1)} %bitcast.160, bf16[1024,1024]{1,0:T(8,128)(2,1)} %get-tuple-element.289.q_ref.dq_ref, bf16[1024,1024]{1,0:T(8,128)(2,1)} %get-tuple-element.290.k_ref.dk_ref, ...), custom_call_target="tpu_custom_call" | custom-call | flops 6442450944 | bytes 14680064 | tf_op jit(solution)/shard_map/wgrad_qkv/pallas_call | solution.py:512
  396.7 6.6 %collective-permute-done.54 = bf16[16,112,1024]{2,1,0:T(8,128)(2,1)S(1)} collective-permute-done((bf16[16,112,1024]{2,1,0:T(8,128)(2,1)}, bf16[16,112,1024]{2,1,0:T(8,128)(2,1)S(1)}, u32[]{:S(2)}, u32[]{:S(2)}) %collective-permute-start.54) | collective-permute-done | bytes 3670048 | tf_op jit(solution)/shard_map/ppermute | solution.py:771
  405.2 6.2 %add_core.5 = (bf16[4,112,1024]{2,1,0:T(8,128)(2,1)}, bf16[4,112,1024]{2,1,0:T(8,128)(2,1)}, bf16[4,112,1024]{2,1,0:T(8,128)(2,1)}, bf16[4,112,1024]{2,1,0:T(8,128)(2,1)}) custom-call(s32[4]{0:T(128)} %pad_add_fusion.here, bf16[4,2,2,112,1024]{4,3,2,1,0:T(8,128)(2,1)} %bitcast.104, bf16[4,2,2,112,1024]{4,3,2,1,0:T(8,128)(2,1)} %bitcast.108, ...), custom_call_target="tpu_custom_call" | custom-call | flops 1835008 | bytes 11010048 | tf_op jit(solution)/shard_map/add_core/pallas_call | solution.py:601
  413.9 13.6 %grad_tok.1 = bf16[1024,1024]{1,0:T(8,128)(2,1)} custom-call(s32[32]{0:T(128)} %stack.224.place, bf16[1024,1024]{1,0:T(8,128)(2,1)} %get-tuple-element.299.b_ref.g_ref, bf16[1024,1024]{1,0:T(8,128)(2,1)} %get-tuple-element.289.q_ref.dq_ref, bf16[1024,1024]{1,0:T(8,128)(2,1)} %get-tuple-element.290.k_ref.dk_ref, ...), custom_call_target="tpu_custom_call" | custom-call | flops 6442450944 | bytes 16777216 | tf_op jit(solution)/shard_map/grad_tok/pallas_call | solution.py:548
  427.5 4.0 collective-permute-done.55.refs_6_
  431.6 2.5 collective-permute-done.56
  435.7 3.9 add_plane.5
  442.2 2.8 add_last.2.own
  445.0 6.3 %collective-permute-done.58.ag = bf16[2,112,1024]{2,1,0:T(8,128)(2,1)S(1)} collective-permute-done((bf16[2,112,1024]{2,1,0:T(8,128)(2,1)}, bf16[2,112,1024]{2,1,0:T(8,128)(2,1)S(1)}, u32[]{:S(2)}, u32[]{:S(2)}) %collective-permute-start.58) | collective-permute-done | bytes 458784 | tf_op jit(solution)/shard_map/ppermute | solution.py:771
  453.3 3.3 add_z.5
  458.6 2.9 collective-permute-start.63
  461.5 6.8 %collective-permute-done.61.refs_1_ = bf16[1,112,1024]{2,1,0:T(8,128)(2,1)S(1)} collective-permute-done((bf16[1,112,1024]{2,1,0:T(8,128)(2,1)}, bf16[1,112,1024]{2,1,0:T(8,128)(2,1)S(1)}, u32[]{:S(2)}, u32[]{:S(2)}) %collective-permute-start.61) | collective-permute-done | bytes 229408 | tf_op jit(solution)/shard_map/ppermute | solution.py:771
  468.3 6.5 %collective-permute-done.62.refs_2_ = bf16[1,112,1024]{2,1,0:T(8,128)(2,1)S(1)} collective-permute-done((bf16[1,112,1024]{2,1,0:T(8,128)(2,1)}, bf16[1,112,1024]{2,1,0:T(8,128)(2,1)S(1)}, u32[]{:S(2)}, u32[]{:S(2)}) %collective-permute-start.62) | collective-permute-done | bytes 229408 | tf_op jit(solution)/shard_map/ppermute | solution.py:771
  476.1 2.1 add_last.3.own
  482.0 4.8 final.2
  489.1 3.2 final.3
  (228 shorter events, 85.6 us)
Async XLA Ops:
  4.8 22.1 %collective-permute-start.2 = (bf16[1,3,32,1024]{3,2,1,0:T(8,128)(2,1)}, bf16[1,3,32,1024]{3,2,1,0:T(8,128)(2,1)S(1)}, u32[]{:S(2)}, u32[]{:S(2)}) collective-permute-start(bf16[1,3,32,1024]{3,2,1,0:T(8,128)(2,1)} %get-tuple-element.174), channel_id=1, source_target_pairs={{0,6},{1,7},{2,0},{3,1},{4,2},{5,3},{6,4},{7,5},{8,14},{9,15},{10,... | collective-permute-start | bytes 589832 | tf_op jit(solution)/shard_map/ppermute | solution.py:771
  9.9 17.0 %collective-permute-start.1 = (bf16[1,3,32,1024]{3,2,1,0:T(8,128)(2,1)}, bf16[1,3,32,1024]{3,2,1,0:T(8,128)(2,1)S(1)}, u32[]{:S(2)}, u32[]{:S(2)}) collective-permute-start(bf16[1,3,32,1024]{3,2,1,0:T(8,128)(2,1)} %get-tuple-element.174), channel_id=1, source_target_pairs={{0,4},{1,5},{2,6},{3,7},{4,0},{5,1},{6,2},{7,3},{8,12},{9,13},{10,... | collective-permute-start | bytes 589832 | tf_op jit(solution)/shard_map/ppermute | solution.py:771
  9.9 13.8 %collective-permute-start = (bf16[1,3,32,1024]{3,2,1,0:T(8,128)(2,1)}, bf16[1,3,32,1024]{3,2,1,0:T(8,128)(2,1)S(1)}, u32[]{:S(2)}, u32[]{:S(2)}) collective-permute-start(bf16[1,3,32,1024]{3,2,1,0:T(8,128)(2,1)} %get-tuple-element.174), channel_id=1, source_target_pairs={{0,2},{1,3},{2,4},{3,5},{4,6},{5,7},{6,0},{7,1},{8,10},{9,11},{10,... | collective-permute-start | bytes 589832 | tf_op jit(solution)/shard_map/ppermute | solution.py:771
  23.7 16.9 %collective-permute-start.12 = (bf16[2,3,32,1024]{3,2,1,0:T(8,128)(2,1)S(1)}, bf16[2,3,32,1024]{3,2,1,0:T(8,128)(2,1)S(1)}, u32[]{:S(2)}, u32[]{:S(2)}) collective-permute-start(bf16[2,3,32,1024]{3,2,1,0:T(8,128)(2,1)S(1)} %constant_dynamic-update-slice_fusion.rest_0_), channel_id=1, source_target_pairs={{0,8},{1,9},{2,10},{3,11},{4,12},{5,13},{6,14},{7,15},{8,0},{9,1},... | collective-permute-start | bytes 1179656 | tf_op jit(solution)/shard_map/ppermute | solution.py:771
  23.8 16.8 %collective-permute-start.10 = (bf16[2,3,32,1024]{3,2,1,0:T(8,128)(2,1)S(1)}, bf16[2,3,32,1024]{3,2,1,0:T(8,128)(2,1)}, u32[]{:S(2)}, u32[]{:S(2)}) collective-permute-start(bf16[2,3,32,1024]{3,2,1,0:T(8,128)(2,1)S(1)} %constant_dynamic-update-slice_fusion.rest_0_), channel_id=1, source_target_pairs={{0,16},{1,17},{2,18},{3,19},{4,20},{5,21},{6,22},{7,23},{8,24},{9,... | collective-permute-start | bytes 1179656 | tf_op jit(solution)/shard_map/ppermute | solution.py:771
  25.3 15.8 %collective-permute-start.8 = (bf16[2,3,32,1024]{3,2,1,0:T(8,128)(2,1)S(1)}, bf16[2,3,32,1024]{3,2,1,0:T(8,128)(2,1)}, u32[]{:S(2)}, u32[]{:S(2)}) collective-permute-start(bf16[2,3,32,1024]{3,2,1,0:T(8,128)(2,1)S(1)} %constant_dynamic-update-slice_fusion.rest_0_), channel_id=1, source_target_pairs={{0,1},{1,0},{2,3},{3,2},{4,5},{5,4},{6,7},{7,6},{8,9},{9,8},{10,11... | collective-permute-start | bytes 1179656 | tf_op jit(solution)/shard_map/ppermute | solution.py:771
  38.5 16.0 %collective-permute-start.17 = (bf16[1,9,32,1024]{3,2,1,0:T(8,128)(2,1)}, bf16[1,9,32,1024]{3,2,1,0:T(8,128)(2,1)S(1)}, u32[]{:S(2)}, u32[]{:S(2)}) collective-permute-start(bf16[1,9,32,1024]{3,2,1,0:T(8,128)(2,1)} %get-tuple-element.177), channel_id=1, source_target_pairs={{0,6},{1,7},{2,0},{3,1},{4,2},{5,3},{6,4},{7,5},{8,14},{9,15},{10,... | collective-permute-start | bytes 1769480 | tf_op jit(solution)/shard_map/ppermute | solution.py:771
  39.7 26.5 %collective-permute-start.16 = (bf16[1,9,32,1024]{3,2,1,0:T(8,128)(2,1)}, bf16[1,9,32,1024]{3,2,1,0:T(8,128)(2,1)S(1)}, u32[]{:S(2)}, u32[]{:S(2)}) collective-permute-start(bf16[1,9,32,1024]{3,2,1,0:T(8,128)(2,1)} %get-tuple-element.177), channel_id=1, source_target_pairs={{0,2},{1,3},{2,4},{3,5},{4,6},{5,7},{6,0},{7,1},{8,10},{9,11},{10,... | collective-permute-start | bytes 1769480 | tf_op jit(solution)/shard_map/ppermute | solution.py:771
  40.6 11.6 %collective-permute-start.11 = (bf16[2,3,32,1024]{3,2,1,0:T(8,128)(2,1)S(1)}, bf16[2,3,32,1024]{3,2,1,0:T(8,128)(2,1)}, u32[]{:S(2)}, u32[]{:S(2)}) collective-permute-start(bf16[2,3,32,1024]{3,2,1,0:T(8,128)(2,1)S(1)} %constant_dynamic-update-slice_fusion.2.rest_1_), channel_id=1, source_target_pairs={{0,1},{1,0},{2,3},{3,2},{4,5},{5,4},{6,7},{7,6},{8,9},{9,8},{10,11... | collective-permute-start | bytes 1179656 | tf_op jit(solution)/shard_map/ppermute | solution.py:771
  41.2 11.3 %collective-permute-start.9 = (bf16[2,3,32,1024]{3,2,1,0:T(8,128)(2,1)S(1)}, bf16[2,3,32,1024]{3,2,1,0:T(8,128)(2,1)}, u32[]{:S(2)}, u32[]{:S(2)}) collective-permute-start(bf16[2,3,32,1024]{3,2,1,0:T(8,128)(2,1)S(1)} %constant_dynamic-update-slice_fusion.2.rest_1_), channel_id=1, source_target_pairs={{0,16},{1,17},{2,18},{3,19},{4,20},{5,21},{6,22},{7,23},{8,24},{9,... | collective-permute-start | bytes 1179656 | tf_op jit(solution)/shard_map/ppermute | solution.py:771
  52.5 16.2 %collective-permute-start.14 = (bf16[2,3,32,1024]{3,2,1,0:T(8,128)(2,1)}, bf16[2,3,32,1024]{3,2,1,0:T(8,128)(2,1)}, u32[]{:S(2)}, u32[]{:S(2)}) collective-permute-start(bf16[2,3,32,1024]{3,2,1,0:T(8,128)(2,1)} %collective-permute-done.8.rest_2_), channel_id=1, source_target_pairs={{0,16},{1,17},{2,18},{3,19},{4,20},{5,21},{6,22},{7,23},{8,24},{9,... | collective-permute-start | bytes 1179656 | tf_op jit(solution)/shard_map/ppermute | solution.py:771
  53.0 16.3 %collective-permute-start.15 = (bf16[2,3,32,1024]{3,2,1,0:T(8,128)(2,1)}, bf16[2,3,32,1024]{3,2,1,0:T(8,128)(2,1)}, u32[]{:S(2)}, u32[]{:S(2)}) collective-permute-start(bf16[2,3,32,1024]{3,2,1,0:T(8,128)(2,1)} %collective-permute-done.9.rest_3_), channel_id=1, source_target_pairs={{0,1},{1,0},{2,3},{3,2},{4,5},{5,4},{6,7},{7,6},{8,9},{9,8},{10,11... | collective-permute-start | bytes 1179656 | tf_op jit(solution)/shard_map/ppermute | solution.py:771
  54.5 14.9 %collective-permute-start.22 = (bf16[2,3,32,1024]{3,2,1,0:T(8,128)(2,1)}, bf16[2,3,32,1024]{3,2,1,0:T(8,128)(2,1)}, u32[]{:S(2)}, u32[]{:S(2)}) collective-permute-start(bf16[2,3,32,1024]{3,2,1,0:T(8,128)(2,1)} %collective-permute-done.10.rest_4_), channel_id=1, source_target_pairs={{0,8},{1,9},{2,10},{3,11},{4,12},{5,13},{6,14},{7,15},{8,0},{9,1},... | collective-permute-start | bytes 1179656 | tf_op jit(solution)/shard_map/ppermute | solution.py:771
  54.5 15.3 %collective-permute-start.23 = (bf16[2,3,32,1024]{3,2,1,0:T(8,128)(2,1)}, bf16[2,3,32,1024]{3,2,1,0:T(8,128)(2,1)}, u32[]{:S(2)}, u32[]{:S(2)}) collective-permute-start(bf16[2,3,32,1024]{3,2,1,0:T(8,128)(2,1)} %collective-permute-done.11.rest_5_), channel_id=1, source_target_pairs={{0,8},{1,9},{2,10},{3,11},{4,12},{5,13},{6,14},{7,15},{8,0},{9,1},... | collective-permute-start | bytes 1179656 | tf_op jit(solution)/shard_map/ppermute | solution.py:771
  69.9 29.8 %collective-permute-start.19 = (bf16[2,9,32,1024]{3,2,1,0:T(8,128)(2,1)S(1)}, bf16[2,9,32,1024]{3,2,1,0:T(8,128)(2,1)}, u32[]{:S(2)}, u32[]{:S(2)}) collective-permute-start(bf16[2,9,32,1024]{3,2,1,0:T(8,128)(2,1)S(1)} %constant_dynamic-update-slice_fusion.4.rest_0_), channel_id=1, source_target_pairs={{0,16},{1,17},{2,18},{3,19},{4,20},{5,21},{6,22},{7,23},{8,24},{9,... | collective-permute-start | bytes 3538952 | tf_op jit(solution)/shard_map/ppermute | solution.py:771
  70.5 29.2 %collective-permute-start.18 = (bf16[2,9,32,1024]{3,2,1,0:T(8,128)(2,1)S(1)}, bf16[2,9,32,1024]{3,2,1,0:T(8,128)(2,1)}, u32[]{:S(2)}, u32[]{:S(2)}) collective-permute-start(bf16[2,9,32,1024]{3,2,1,0:T(8,128)(2,1)S(1)} %constant_dynamic-update-slice_fusion.4.rest_0_), channel_id=1, source_target_pairs={{0,1},{1,0},{2,3},{3,2},{4,5},{5,4},{6,7},{7,6},{8,9},{9,8},{10,11... | collective-permute-start | bytes 3538952 | tf_op jit(solution)/shard_map/ppermute | solution.py:771
  71.6 28.0 %collective-permute-start.7 = (bf16[1,9,32,1024]{3,2,1,0:T(8,128)(2,1)S(1)}, bf16[1,9,32,1024]{3,2,1,0:T(8,128)(2,1)S(1)}, u32[]{:S(2)}, u32[]{:S(2)}) collective-permute-start(bf16[1,9,32,1024]{3,2,1,0:T(8,128)(2,1)S(1)} %copy-done.13), channel_id=1, source_target_pairs={{0,4},{1,5},{2,6},{3,7},{4,0},{5,1},{6,2},{7,3},{8,12},{9,13},{10,... | collective-permute-start | bytes 1769480 | tf_op jit(solution)/shard_map/ppermute | solution.py:771
  72.8 40.2 %collective-permute-start.29 = (bf16[2,9,32,1024]{3,2,1,0:T(8,128)(2,1)S(1)}, bf16[2,9,32,1024]{3,2,1,0:T(8,128)(2,1)}, u32[]{:S(2)}, u32[]{:S(2)}) collective-permute-start(bf16[2,9,32,1024]{3,2,1,0:T(8,128)(2,1)S(1)} %constant_dynamic-update-slice_fusion.4.rest_0_), channel_id=1, source_target_pairs={{0,8},{1,9},{2,10},{3,11},{4,12},{5,13},{6,14},{7,15},{8,0},{9,1},... | collective-permute-start | bytes 3538952 | tf_op jit(solution)/shard_map/ppermute | solution.py:771
  99.7 13.3 %collective-permute-start.31 = (bf16[2,9,32,1024]{3,2,1,0:T(8,128)(2,1)}, bf16[2,9,32,1024]{3,2,1,0:T(8,128)(2,1)}, u32[]{:S(2)}, u32[]{:S(2)}) collective-permute-start(bf16[2,9,32,1024]{3,2,1,0:T(8,128)(2,1)} %collective-permute-done.19.rest_2_), channel_id=1, source_target_pairs={{0,8},{1,9},{2,10},{3,11},{4,12},{5,13},{6,14},{7,15},{8,0},{9,1},... | collective-permute-start | bytes 3538952 | tf_op jit(solution)/shard_map/ppermute | solution.py:771
  99.7 13.3 %collective-permute-start.30 = (bf16[2,9,32,1024]{3,2,1,0:T(8,128)(2,1)}, bf16[2,9,32,1024]{3,2,1,0:T(8,128)(2,1)}, u32[]{:S(2)}, u32[]{:S(2)}) collective-permute-start(bf16[2,9,32,1024]{3,2,1,0:T(8,128)(2,1)} %collective-permute-done.18.rest_1_), channel_id=1, source_target_pairs={{0,8},{1,9},{2,10},{3,11},{4,12},{5,13},{6,14},{7,15},{8,0},{9,1},... | collective-permute-start | bytes 3538952 | tf_op jit(solution)/shard_map/ppermute | solution.py:771
  101.9 28.2 %collective-permute-start.28 = (bf16[2,9,32,1024]{3,2,1,0:T(8,128)(2,1)}, bf16[2,9,32,1024]{3,2,1,0:T(8,128)(2,1)S(1)}, u32[]{:S(2)}, u32[]{:S(2)}) collective-permute-start(bf16[2,9,32,1024]{3,2,1,0:T(8,128)(2,1)} %constant_dynamic-update-slice_fusion.6.rest_3_), channel_id=1, source_target_pairs={{0,1},{1,0},{2,3},{3,2},{4,5},{5,4},{6,7},{7,6},{8,9},{9,8},{10,11... | collective-permute-start | bytes 3538952 | tf_op jit(solution)/shard_map/ppermute | solution.py:771
  103.4 28.0 %collective-permute-start.27 = (bf16[2,9,32,1024]{3,2,1,0:T(8,128)(2,1)}, bf16[2,9,32,1024]{3,2,1,0:T(8,128)(2,1)}, u32[]{:S(2)}, u32[]{:S(2)}) collective-permute-start(bf16[2,9,32,1024]{3,2,1,0:T(8,128)(2,1)} %constant_dynamic-update-slice_fusion.6.rest_3_), channel_id=1, source_target_pairs={{0,16},{1,17},{2,18},{3,19},{4,20},{5,21},{6,22},{7,23},{8,24},{9,... | collective-permute-start | bytes 3538952 | tf_op jit(solution)/shard_map/ppermute | solution.py:771
  112.9 21.0 %collective-permute-start.33 = (bf16[2,9,32,1024]{3,2,1,0:T(8,128)(2,1)}, bf16[2,9,32,1024]{3,2,1,0:T(8,128)(2,1)S(1)}, u32[]{:S(2)}, u32[]{:S(2)}) collective-permute-start(bf16[2,9,32,1024]{3,2,1,0:T(8,128)(2,1)} %constant_dynamic-update-slice_fusion.6.rest_3_), channel_id=1, source_target_pairs={{0,8},{1,9},{2,10},{3,11},{4,12},{5,13},{6,14},{7,15},{8,0},{9,1},... | collective-permute-start | bytes 3538952 | tf_op jit(solution)/shard_map/ppermute | solution.py:771
  131.9 28.2 %collective-permute-start.26 = (bf16[2,9,32,1024]{3,2,1,0:T(8,128)(2,1)}, bf16[2,9,32,1024]{3,2,1,0:T(8,128)(2,1)}, u32[]{:S(2)}, u32[]{:S(2)}) collective-permute-start(bf16[2,9,32,1024]{3,2,1,0:T(8,128)(2,1)} %collective-permute-done.18.rest_1_), channel_id=1, source_target_pairs={{0,16},{1,17},{2,18},{3,19},{4,20},{5,21},{6,22},{7,23},{8,24},{9,... | collective-permute-start | bytes 3538952 | tf_op jit(solution)/shard_map/ppermute | solution.py:771
  133.4 27.9 %collective-permute-start.32 = (bf16[2,9,32,1024]{3,2,1,0:T(8,128)(2,1)}, bf16[2,9,32,1024]{3,2,1,0:T(8,128)(2,1)}, u32[]{:S(2)}, u32[]{:S(2)}) collective-permute-start(bf16[2,9,32,1024]{3,2,1,0:T(8,128)(2,1)} %collective-permute-done.27.rest_4_), channel_id=1, source_target_pairs={{0,1},{1,0},{2,3},{3,2},{4,5},{5,4},{6,7},{7,6},{8,9},{9,8},{10,11... | collective-permute-start | bytes 3538952 | tf_op jit(solution)/shard_map/ppermute | solution.py:771
  242.1 15.1 %collective-permute-start.39 = (bf16[16,128,1024]{2,1,0:T(8,128)(2,1)}, bf16[16,128,1024]{2,1,0:T(8,128)(2,1)}, u32[]{:S(2)}, u32[]{:S(2)}) collective-permute-start(bf16[16,128,1024]{2,1,0:T(8,128)(2,1)} %get-tuple-element.234), channel_id=1, source_target_pairs={{0,8},{1,9},{2,10},{3,11},{4,12},{5,13},{6,14},{7,15},{8,0},{9,1},... | collective-permute-start | bytes 12582920 | tf_op jit(solution)/shard_map/ppermute | solution.py:771
  256.2 15.3 %collective-permute-start.38 = (bf16[16,128,1024]{2,1,0:T(8,128)(2,1)}, bf16[16,128,1024]{2,1,0:T(8,128)(2,1)}, u32[]{:S(2)}, u32[]{:S(2)}) collective-permute-start(bf16[16,128,1024]{2,1,0:T(8,128)(2,1)} %get-tuple-element.230), channel_id=1, source_target_pairs={{0,8},{1,9},{2,10},{3,11},{4,12},{5,13},{6,14},{7,15},{8,0},{9,1},... | collective-permute-start | bytes 12582920 | tf_op jit(solution)/shard_map/ppermute | solution.py:771
  270.4 27.9 %collective-permute-start.41 = (bf16[4,128,1024]{2,1,0:T(8,128)(2,1)}, bf16[4,128,1024]{2,1,0:T(8,128)(2,1)S(1)}, u32[]{:S(2)}, u32[]{:S(2)}) collective-permute-start(bf16[4,128,1024]{2,1,0:T(8,128)(2,1)} %get-tuple-element.248), channel_id=1, source_target_pairs={{0,16},{1,17},{2,18},{3,19},{4,20},{5,21},{6,22},{7,23},{8,24},{9,... | collective-permute-start | bytes 3145736 | tf_op jit(solution)/shard_map/ppermute | solution.py:771
  270.9 27.4 %collective-permute-start.42 = (bf16[4,128,1024]{2,1,0:T(8,128)(2,1)}, bf16[4,128,1024]{2,1,0:T(8,128)(2,1)}, u32[]{:S(2)}, u32[]{:S(2)}) collective-permute-start(bf16[4,128,1024]{2,1,0:T(8,128)(2,1)} %get-tuple-element.250), channel_id=1, source_target_pairs={{0,1},{1,0},{2,3},{3,2},{4,5},{5,4},{6,7},{7,6},{8,9},{9,8},{10,11... | collective-permute-start | bytes 3145736 | tf_op jit(solution)/shard_map/ppermute | solution.py:771
  283.2 44.3 %collective-permute-start.43 = (bf16[4,176,1024]{2,1,0:T(8,128)(2,1)}, bf16[4,176,1024]{2,1,0:T(8,128)(2,1)S(1)}, u32[]{:S(2)}, u32[]{:S(2)}) collective-permute-start(bf16[4,176,1024]{2,1,0:T(8,128)(2,1)} %get-tuple-element.259), channel_id=1, source_target_pairs={{0,16},{1,17},{2,18},{3,19},{4,20},{5,21},{6,22},{7,23},{8,24},{9,... | collective-permute-start | bytes 4325384 | tf_op jit(solution)/shard_map/ppermute | solution.py:771
  283.8 44.3 %collective-permute-start.44 = (bf16[4,176,1024]{2,1,0:T(8,128)(2,1)}, bf16[4,176,1024]{2,1,0:T(8,128)(2,1)S(1)}, u32[]{:S(2)}, u32[]{:S(2)}) collective-permute-start(bf16[4,176,1024]{2,1,0:T(8,128)(2,1)} %get-tuple-element.261), channel_id=1, source_target_pairs={{0,1},{1,0},{2,3},{3,2},{4,5},{5,4},{6,7},{7,6},{8,9},{9,8},{10,11... | collective-permute-start | bytes 4325384 | tf_op jit(solution)/shard_map/ppermute | solution.py:771
  317.5 30.6 %collective-permute-start.45 = (bf16[2,128,1024]{2,1,0:T(8,128)(2,1)}, bf16[2,128,1024]{2,1,0:T(8,128)(2,1)S(1)}, u32[]{:S(2)}, u32[]{:S(2)}) collective-permute-start(bf16[2,128,1024]{2,1,0:T(8,128)(2,1)} %get-tuple-element.270), channel_id=1, source_target_pairs={{0,1},{1,0},{2,3},{3,2},{4,5},{5,4},{6,7},{7,6},{8,9},{9,8},{10,11... | collective-permute-start | bytes 1572872 | tf_op jit(solution)/shard_map/ppermute | solution.py:771
  319.1 29.0 %collective-permute-start.46 = (bf16[2,128,1024]{2,1,0:T(8,128)(2,1)}, bf16[2,128,1024]{2,1,0:T(8,128)(2,1)S(1)}, u32[]{:S(2)}, u32[]{:S(2)}) collective-permute-start(bf16[2,128,1024]{2,1,0:T(8,128)(2,1)} %get-tuple-element.272), channel_id=1, source_target_pairs={{0,16},{1,17},{2,18},{3,19},{4,20},{5,21},{6,22},{7,23},{8,24},{9,... | collective-permute-start | bytes 1572872 | tf_op jit(solution)/shard_map/ppermute | solution.py:771
  352.5 25.5 %collective-permute-start.49 = (bf16[1,128,1024]{2,1,0:T(8,128)(2,1)}, bf16[1,128,1024]{2,1,0:T(8,128)(2,1)S(1)}, u32[]{:S(2)}, u32[]{:S(2)}) collective-permute-start(bf16[1,128,1024]{2,1,0:T(8,128)(2,1)} %get-tuple-element.285), channel_id=1, source_target_pairs={{0,2},{1,3},{2,4},{3,5},{4,6},{5,7},{6,0},{7,1},{8,10},{9,11},{10,... | collective-permute-start | bytes 786440 | tf_op jit(solution)/shard_map/ppermute | solution.py:771
  352.5 25.5 %collective-permute-start.50 = (bf16[1,128,1024]{2,1,0:T(8,128)(2,1)}, bf16[1,128,1024]{2,1,0:T(8,128)(2,1)S(1)}, u32[]{:S(2)}, u32[]{:S(2)}) collective-permute-start(bf16[1,128,1024]{2,1,0:T(8,128)(2,1)} %get-tuple-element.286), channel_id=1, source_target_pairs={{0,4},{1,5},{2,6},{3,7},{4,0},{5,1},{6,2},{7,3},{8,12},{9,13},{10,... | collective-permute-start | bytes 786440 | tf_op jit(solution)/shard_map/ppermute | solution.py:771
  355.2 22.8 %collective-permute-start.51 = (bf16[1,128,1024]{2,1,0:T(8,128)(2,1)}, bf16[1,128,1024]{2,1,0:T(8,128)(2,1)S(1)}, u32[]{:S(2)}, u32[]{:S(2)}) collective-permute-start(bf16[1,128,1024]{2,1,0:T(8,128)(2,1)} %get-tuple-element.287), channel_id=1, source_target_pairs={{0,6},{1,7},{2,0},{3,1},{4,2},{5,3},{6,4},{7,5},{8,14},{9,15},{10,... | collective-permute-start | bytes 786440 | tf_op jit(solution)/shard_map/ppermute | solution.py:771
  356.3 16.7 %collective-permute-start.47 = (bf16[2,176,1024]{2,1,0:T(8,128)(2,1)}, bf16[2,176,1024]{2,1,0:T(8,128)(2,1)S(1)}, u32[]{:S(2)}, u32[]{:S(2)}) collective-permute-start(bf16[2,176,1024]{2,1,0:T(8,128)(2,1)} %get-tuple-element.281), channel_id=1, source_target_pairs={{0,1},{1,0},{2,3},{3,2},{4,5},{5,4},{6,7},{7,6},{8,9},{9,8},{10,11... | collective-permute-start | bytes 2162696 | tf_op jit(solution)/shard_map/ppermute | solution.py:771
  356.9 16.3 %collective-permute-start.48 = (bf16[2,176,1024]{2,1,0:T(8,128)(2,1)}, bf16[2,176,1024]{2,1,0:T(8,128)(2,1)S(1)}, u32[]{:S(2)}, u32[]{:S(2)}) collective-permute-start(bf16[2,176,1024]{2,1,0:T(8,128)(2,1)} %get-tuple-element.283), channel_id=1, source_target_pairs={{0,16},{1,17},{2,18},{3,19},{4,20},{5,21},{6,22},{7,23},{8,24},{9,... | collective-permute-start | bytes 2162696 | tf_op jit(solution)/shard_map/ppermute | solution.py:771
  378.0 17.9 %collective-permute-start.52 = (bf16[1,176,1024]{2,1,0:T(8,128)(2,1)}, bf16[1,176,1024]{2,1,0:T(8,128)(2,1)S(1)}, u32[]{:S(2)}, u32[]{:S(2)}) collective-permute-start(bf16[1,176,1024]{2,1,0:T(8,128)(2,1)} %get-tuple-element.295), channel_id=1, source_target_pairs={{0,2},{1,3},{2,4},{3,5},{4,6},{5,7},{6,0},{7,1},{8,10},{9,11},{10,... | collective-permute-start | bytes 1081352 | tf_op jit(solution)/shard_map/ppermute | solution.py:771
  378.7 17.2 %collective-permute-start.53 = (bf16[1,176,1024]{2,1,0:T(8,128)(2,1)}, bf16[1,176,1024]{2,1,0:T(8,128)(2,1)S(1)}, u32[]{:S(2)}, u32[]{:S(2)}) collective-permute-start(bf16[1,176,1024]{2,1,0:T(8,128)(2,1)} %get-tuple-element.296), channel_id=1, source_target_pairs={{0,6},{1,7},{2,0},{3,1},{4,2},{5,3},{6,4},{7,5},{8,14},{9,15},{10,... | collective-permute-start | bytes 1081352 | tf_op jit(solution)/shard_map/ppermute | solution.py:771
  411.4 22.7 %collective-permute-start.56 = (bf16[4,112,1024]{2,1,0:T(8,128)(2,1)}, bf16[4,112,1024]{2,1,0:T(8,128)(2,1)S(1)}, u32[]{:S(2)}, u32[]{:S(2)}) collective-permute-start(bf16[4,112,1024]{2,1,0:T(8,128)(2,1)} %get-tuple-element.302), channel_id=1, source_target_pairs={{0,16},{1,17},{2,18},{3,19},{4,20},{5,21},{6,22},{7,23},{8,24},{9,... | collective-permute-start | bytes 2752520 | tf_op jit(solution)/shard_map/ppermute | solution.py:771
  412.4 22.3 %collective-permute-start.57 = (bf16[4,112,1024]{2,1,0:T(8,128)(2,1)}, bf16[4,112,1024]{2,1,0:T(8,128)(2,1)S(1)}, u32[]{:S(2)}, u32[]{:S(2)}) collective-permute-start(bf16[4,112,1024]{2,1,0:T(8,128)(2,1)} %get-tuple-element.304), channel_id=1, source_target_pairs={{0,1},{1,0},{2,3},{3,2},{4,5},{5,4},{6,7},{7,6},{8,9},{9,8},{10,11... | collective-permute-start | bytes 2752520 | tf_op jit(solution)/shard_map/ppermute | solution.py:771
  413.9 17.6 %collective-permute-start.55 = (bf16[1,176,1024]{2,1,0:T(8,128)(2,1)}, bf16[1,176,1024]{2,1,0:T(8,128)(2,1)S(1)}, u32[]{:S(2)}, u32[]{:S(2)}) collective-permute-start(bf16[1,176,1024]{2,1,0:T(8,128)(2,1)} %get-tuple-element.300), channel_id=1, source_target_pairs={{0,4},{1,5},{2,6},{3,7},{4,0},{5,1},{6,2},{7,3},{8,12},{9,13},{10,... | collective-permute-start | bytes 1081352 | tf_op jit(solution)/shard_map/ppermute | solution.py:771
  439.6 11.7 %collective-permute-start.58 = (bf16[2,112,1024]{2,1,0:T(8,128)(2,1)}, bf16[2,112,1024]{2,1,0:T(8,128)(2,1)S(1)}, u32[]{:S(2)}, u32[]{:S(2)}) collective-permute-start(bf16[2,112,1024]{2,1,0:T(8,128)(2,1)} %get-tuple-element.307), channel_id=1, source_target_pairs={{0,1},{1,0},{2,3},{3,2},{4,5},{5,4},{6,7},{7,6},{8,9},{9,8},{10,11... | collective-permute-start | bytes 1376264 | tf_op jit(solution)/shard_map/ppermute | solution.py:771
  441.2 11.3 %collective-permute-start.59 = (bf16[2,112,1024]{2,1,0:T(8,128)(2,1)}, bf16[2,112,1024]{2,1,0:T(8,128)(2,1)S(1)}, u32[]{:S(2)}, u32[]{:S(2)}) collective-permute-start(bf16[2,112,1024]{2,1,0:T(8,128)(2,1)} %get-tuple-element.309), channel_id=1, source_target_pairs={{0,16},{1,17},{2,18},{3,19},{4,20},{5,21},{6,22},{7,23},{8,24},{9,... | collective-permute-start | bytes 1376264 | tf_op jit(solution)/shard_map/ppermute | solution.py:771
  456.6 21.6 %collective-permute-start.60 = (bf16[1,304,1024]{2,1,0:T(8,128)(2,1)}, bf16[1,304,1024]{2,1,0:T(8,128)(2,1)S(1)}, u32[]{:S(2)}, u32[]{:S(2)}) collective-permute-start(bf16[1,304,1024]{2,1,0:T(8,128)(2,1)} %add_last.2.own), channel_id=1, source_target_pairs={{0,16},{1,17},{2,18},{3,19},{4,20},{5,21},{6,22},{7,23},{8,24},{9,... | collective-permute-start | bytes 1867784 | tf_op jit(solution)/shard_map/ppermute | solution.py:771
  457.6 17.1 %collective-permute-start.62 = (bf16[1,112,1024]{2,1,0:T(8,128)(2,1)}, bf16[1,112,1024]{2,1,0:T(8,128)(2,1)S(1)}, u32[]{:S(2)}, u32[]{:S(2)}) collective-permute-start(bf16[1,112,1024]{2,1,0:T(8,128)(2,1)} %get-tuple-element.313), channel_id=1, source_target_pairs={{0,4},{1,5},{2,6},{3,7},{4,0},{5,1},{6,2},{7,3},{8,12},{9,13},{10,... | collective-permute-start | bytes 688136 | tf_op jit(solution)/shard_map/ppermute | solution.py:771
  458.6 16.2 %collective-permute-start.63 = (bf16[1,112,1024]{2,1,0:T(8,128)(2,1)}, bf16[1,112,1024]{2,1,0:T(8,128)(2,1)S(1)}, u32[]{:S(2)}, u32[]{:S(2)}) collective-permute-start(bf16[1,112,1024]{2,1,0:T(8,128)(2,1)} %get-tuple-element.314), channel_id=1, source_target_pairs={{0,6},{1,7},{2,0},{3,1},{4,2},{5,3},{6,4},{7,5},{8,14},{9,15},{10,... | collective-permute-start | bytes 688136 | tf_op jit(solution)/shard_map/ppermute | solution.py:771
  (62 other events, 462.4 us)

commit v4 on v3

--- a/solution.py
+++ b/solution.py
@@ -412,7 +412,7 @@
     value = jnp.zeros((LINES, width), F32)
     for i, segs in enumerate(segments):
         used = sum(v.shape[1] for v in segs)
-        line = jnp.concatenate([*segs, jnp.zeros((1, width - used), F32)], 1)
+        line = jnp.concatenate(segs + [jnp.zeros((1, width - used), F32)] * (used < width), 1)
         value = jnp.where(row == i, line, value)
     return value.astype(BF)
 
@@ -780,9 +780,8 @@
     return r // 2, s % 2, s // 2, r % 2
 
 
-def pack_body(count, share, *refs):
-    ins, smalls, outs = refs[:count], refs[count:-2], refs[-2:]
-    out, line = outs
+def pack_body(share, *refs):
+    ins, out = refs[:-1], refs[-1]
     width = out.shape[-1]
     n0 = 0
     for ref in ins:
@@ -794,43 +793,57 @@
             for n in range(cols // width):
                 out[0, n0 + n] = ref[:, n * width : (n + 1) * width]
             n0 += cols // width
-    n0 = 0
-    for ref in smalls:
-        line[:, n0 : n0 + ref.shape[1]] = ref[...]
-        n0 += ref.shape[1]
-
-
-def pack(share, mats, smalls, width):
+
+
+def pack(share, mats, width):
     shapes = [(m.shape[0] // 4, m.shape[1]) for m in mats]
     blocks = sum(r * c for r, c in shapes) // (SUB * width)
-    smalls = [v.reshape(1, -1) for v in smalls]
-    line = (1, sum(v.shape[1] for v in smalls))
-    return pl.pallas_call(
-        functools.partial(pack_body, len(mats)),
+    return pl.pallas_call(
+        pack_body,
         name="pack",
         grid_spec=pltpu.PrefetchScalarGridSpec(
             num_scalar_prefetch=1,
             grid=(1,),
-            in_specs=[pl.BlockSpec(sh, lambda t, r: (r[0], 0)) for sh in shapes]
-            + [pl.BlockSpec(v.shape, lambda t, r: (0, 0)) for v in smalls],
-            out_specs=[
-                pl.BlockSpec((1, blocks, SUB, width), lambda t, r: (0, 0, 0, 0)),
-                pl.BlockSpec(line, lambda t, r: (0, 0)),
-            ],
-        ),
-        out_shape=[jax.ShapeDtypeStruct((1, blocks, SUB, width), BF), jax.ShapeDtypeStruct(line, BF)],
+            in_specs=[pl.BlockSpec(sh, lambda t, r: (r[0], 0)) for sh in shapes],
+            out_specs=pl.BlockSpec((1, blocks, SUB, width), lambda t, r: (0, 0, 0, 0)),
+        ),
+        out_shape=jax.ShapeDtypeStruct((1, blocks, SUB, width), BF),
         compiler_params=params(),
         cost_estimate=cost(1, 4 * blocks * SUB * width),
-    )(share, *mats, *smalls)
+    )(share, *mats)
+
+
+def pack_first_body(share, w_ref, *refs):
+    vecs, out = refs[:-1], refs[-1]
+    rows, width = 3 * SUB, out.shape[-1]
+    for n in range(3):
+        out[0, n * SUB : (n + 1) * SUB] = w_ref[:, n * width : (n + 1) * width]
+    segs = [v[...].astype(F32) for v in vecs]
+    out[0, rows : rows + LINES] = lines_of([width, *segs[:-1]], [width, segs[-1]])
+
+
+def pack_first(share, w_qkv, vecs, width):
+    rows = w_qkv.shape[0] // 4
+    vecs = [v.reshape(1, -1) for v in vecs]
+    shape = (1, 3 * rows + LINES, width)
+    return pl.pallas_call(
+        pack_first_body,
+        name="pack_first",
+        grid_spec=pltpu.PrefetchScalarGridSpec(
+            num_scalar_prefetch=1,
+            grid=(1,),
+            in_specs=[pl.BlockSpec((rows, 3 * width), lambda t, r: (r[0], 0))]
+            + [pl.BlockSpec(v.shape, lambda t, r: (0, 0)) for v in vecs],
+            out_specs=pl.BlockSpec(shape, lambda t, r: (0, 0, 0)),
+        ),
+        out_shape=jax.ShapeDtypeStruct(shape, BF),
+        compiler_params=params(),
+        cost_estimate=cost(1, 12 * rows * width),
+    )(share, w_qkv, *vecs)
 
 
 def after(v, *deps):
     return lax.optimization_barrier((v,) + deps)[0]
-
-
-def gather_z(own):
-    near = [move(own, TO_Z[k]) for k in (1, 2, 3)]
-    return jnp.concatenate([own, near[0]], 0), jnp.concatenate([near[1], near[2]], 0)
 
 
 def to_core(bufs):
@@ -850,10 +863,20 @@
     x, y, z, c = place_of()
     spots = []
     for fc in (0, 1):
-        for k0, fx, fy in order:
-            for k in (k0, k0 + 1):
-                spots.append((((z - k) % 4) * 2 + (y ^ fy)) * 4 + (x ^ fx) * 2 + (c ^ fc))
+        for k, fx, fy in order:
+            spots.append((((z - k) % 4) * 2 + (y ^ fy)) * 4 + (x ^ fx) * 2 + (c ^ fc))
     return jnp.stack(spots).astype(jnp.int32)
+
+
+FIRST = [
+    (k0 + k, fx, fy)
+    for k0, fx, fy in ((0, 0, 0), (2, 0, 0), (0, 0, 1), (2, 1, 0), (0, 1, 0), (2, 0, 1), (0, 1, 1), (2, 1, 1))
+    for k in (0, 1)
+]
+SECOND = [
+    (0, 0, 0), (0, 1, 0), (1, 0, 0), (3, 0, 0), (2, 0, 0), (0, 0, 1), (1, 1, 0), (3, 1, 0),
+    (1, 0, 1), (3, 0, 1), (2, 1, 0), (0, 1, 1), (2, 0, 1), (3, 1, 1), (1, 1, 1), (2, 1, 1),
+]
 
 
 def spread(w, blocks, wide):
@@ -878,10 +901,10 @@
     return [own] + [move(v, TO_Z[k + 1]) for k, v in enumerate(sends)]
 
 
-def small_gather(plane):
+def small_gather(lines):
     x, y, z, c = place_of()
-    rows = jnp.concatenate([plane] + [move(plane, TO_Z[k]) for k in (1, 2, 3)], 0)
-    spots = jnp.stack([((z - k) % 4) * 2 + (y ^ f) for k in range(4) for f in (0, 1)])
+    rows = jnp.concatenate([lines, move(lines, TO_Y)], 0)
+    spots = jnp.stack([((z - k) % 4) * 2 + (y ^ f) for f in (0, 1) for k in range(4)])
     pick = (jnp.arange(8)[:, None] == spots[None, :]).astype(BF)
     return dot_nn(pick, rows)
 
@@ -907,18 +930,24 @@
     count = lax.axis_size("shard")
     x = tokens.reshape(slots, width)
     cot = cotangent.reshape(slots, width)
-    small = [b_qv, b_attn_out, ln1_gain, ln1_bias, b_ffn_in, b_ffn_out, ln2_gain, ln2_bias]
+    small = [b_qv, b_attn_out, ln1_gain, ln1_bias, b_ffn_out, ln2_gain, ln2_bias, b_ffn_in]
     sizes = [v.shape[0] for v in small]
     ends = [sum(sizes[: i + 1]) for i in range(len(sizes))]
 
     if regular():
         share = lax.axis_index("replica").reshape(1).astype(jnp.int32)
-        first, line = pack(share, [w_qkv], small, width)
-        plane = jnp.concatenate([line, move(line, TO_Y)], 0)
-        a1, b1 = gather_z(first)
-        rows = small_gather(after(plane, a1, b1))
-        second, _ = pack(share, [w_attn_out, w_ffn_in, w_ffn_out], [b_qv], width)
-        second = after(second, a1, b1, rows)
+        first = pack_first(share, w_qkv, small, width)
+        second = pack(share, [after(w_attn_out, first), w_ffn_in, w_ffn_out], width)
+        xo, yo = move(second, TO_X), move(second, TO_Y)
+        along = [first] + [move(first, TO_Z[k]) for k in (1, 2, 3)]
+        *along, xo, yo = lax.optimization_barrier((*along, xo, yo))
+        a1, b1 = [
+            jnp.concatenate([v[:, : 3 * SUB] for v in pair], 0).reshape(2, 3, SUB, width)
+            for pair in (along[:2], along[2:])
+        ]
+        lines = jnp.concatenate([v[:, 3 * SUB : 3 * SUB + 2] for v in along], 0)
+        rows = small_gather(lines.reshape(4, 2 * width)[:, : ends[-1]])
+        second = after(second, along[3])
         near, *far = [move(second, TO_Z[k]) for k in (1, 2, 3)]
         plane = [move(a1, TO_Y), move(b1, TO_X), move(a1, TO_X), move(b1, TO_Y)]
         first = [a1, b1]
@@ -928,10 +957,9 @@
         more = to_core(plane)
         _, [near, far[1]] = tied(last, [near, far[1]])
         w1 = [*first, *plane, *last, *cores, *more, *to_core(last)]
-        a2 = jnp.concatenate([second, near], 0)
-        ya2, xa2 = move(a2, TO_Y), move(a2, TO_X)
-        place = gather_places(((0, 0, 0), (2, 0, 0), (0, 0, 1), (2, 1, 0), (0, 1, 0), (2, 0, 1), (0, 1, 1), (2, 1, 1)))
-        place2 = gather_places(((0, 0, 0), (0, 0, 1), (0, 1, 0), (2, 0, 0), (2, 1, 0), (2, 0, 1), (0, 1, 1), (2, 1, 1)))
+        r13 = jnp.concatenate([near, far[1]], 0)
+        x1, y1 = move(r13, TO_X), move(r13, TO_Y)
+        place, place2 = gather_places(FIRST), gather_places(SECOND)
         here = jnp.stack(place_of()).astype(jnp.int32)
     else:
         w1 = [spread(w_qkv, 3, width)]
@@ -943,7 +971,7 @@
 
     if not regular():
         rows = lax.all_gather(jnp.concatenate(small), "shard", axis=0).astype(F32)
-    b_qv, bao, gain1, shift1, b_in, bout, gain2, shift2 = [
+    b_qv, bao, gain1, shift1, bout, gain2, shift2, b_in = [
         rows[:, e - s : e].reshape(-1) for s, e in zip(sizes, ends)
     ]
     bias3 = jnp.concatenate([b_qv[:width], jnp.zeros((width,), F32), b_qv[width:]]).reshape(1, -1)
@@ -955,20 +983,21 @@
     fwd = lambda i, state: attn_fwd_call(qkv, lengths, i, parts, state)
     state = fwd(0, None)
     if regular():
-        far, [ya2, xa2], state = tied(far, [ya2, xa2], state)
-        b2 = jnp.concatenate(far, 0)
-        xb2, yb2 = move(b2, TO_X), move(b2, TO_Y)
-        cores = to_core([a2, ya2, xa2])
+        [r2], [x1, y1], state = tied([far[0]], [x1, y1], state)
+        c2 = jnp.concatenate([r2, yo], 0)
+        x2, y2 = move(c2, TO_X), move(jnp.concatenate([r2, x1[1:]], 0), TO_Y)
+        cores = to_core([second, xo, r13, x1, y1])
         state = fwd(1, state)
         cores, state = tied(cores, state)
         state = fwd(2, state)
-        [xb2, yb2], state = tied([xb2, yb2], state)
-        last = [move(ya2, TO_X), move(xb2, TO_Y)]
-        more = to_core([b2, xb2, yb2])
+        [x2, y2], state = tied([x2, y2], state)
+        x3, y3 = move(y1[:1], TO_X), move(x2[:1], TO_Y)
+        more = to_core([c2, x2, y2])
         more, state = tied(more, state)
         state = fwd(3, state)
-        last, state = tied(last, state)
-        w2 = [a2, ya2, xa2, b2, xb2, yb2, *last, *cores, *more, *to_core(last)]
+        last, state = tied([x3, y3], state)
+        w2 = [second, xo, r13, c2, x1, y1, x2, y2, *last]
+        w2 += [*cores[:3], more[0], *cores[3:], *more[1:], *to_core(last)]
     else:
         for i in range(1, parts):
             state = fwd(i, state)
@@ -1034,9 +1063,10 @@
         g_tok = tok_call(ga, dq, dk, dv, place, w1)
         g_wout = reduce_any(*p_wout, True)
         g_win, g_wao, g_wqkv = [reduce_any(*p, False) for p in (p_win, p_wao, p_wqkv)]
-        vecs = [jnp.concatenate([sq[0], sv[0]]), sums[5], sums[3], sums[4], sbin, sums[2], sums[0], sums[1]]
+        vecs = [jnp.concatenate([sq[0], sv[0]]), sums[5], sums[3], sums[4], sums[2], sums[0], sums[1], sbin]
         own = small_sum(jnp.concatenate([v.reshape(count, -1) for v in vecs], 1))
         vecs = [own[e - s : e] for s, e in zip(sizes, ends)]
+        vecs.insert(4, vecs.pop())
     g_bqv, g_bao, g_g1, g_s1, g_bin, g_bout, g_g2, g_s2 = vecs
     return (
         out[None], g_tok[None], g_wqkv, g_bqv, g_wao, g_bao, g_g1, g_s1,

time: 497 us -> 488 us (0.982)
  waiting for transfers between devices: 117 us -> 112 us
    ppermute x69 -> x70, waiting for transfers between devices: 117 us -> 112 us  [move(): return lax.ppermute(v, AXES, pairs)]
    ppermute x69 -> x70, starting transfers between devices: 61.9 us -> 57.7 us  [move(): return lax.ppermute(v, AXES, pairs)]
    unnamed x89 -> x100, local copies, waits for them, and re-layouts: 17.3 us -> 14.6 us
  transfers between devices with their start and end apart: 69 -> 70, of which waited for: 31 -> 28; matrix products, arithmetic and copies ran while one was open for 2% -> 2% of each run, Pallas kernels for 38% -> 39%
where the time goes in v4:
time: 488 us; the launch traced here: 483 us
  Pallas kernels  286 us (59%)
  waiting for transfers between devices  112 us (23%)
  starting transfers between devices  57.7 us (12%)
  local copies, waits for them, and re-layouts  22.9 us (5%)
    ppermute x70, waiting for transfers between devices, move(): return lax.ppermute(v, AXES, pairs)  112 us
    pallas_call x1, Pallas kernels, row_call(): pl.pallas_call(functools.partial(row_body, len(w2)), name='row_local', gr...  60.8 us
    ppermute x70, starting transfers between devices, move(): return lax.ppermute(v, AXES, pairs)  57.7 us
    pallas_call x4, Pallas kernels, attn_bwd_call(): pl.pallas_call(functools.partial(attn_bwd_body, rows), name=f'attn_bwd{pa...  56.8 us
    pallas_call x4, Pallas kernels, attn_fwd_call(): pl.pallas_call(functools.partial(attn_fwd_body, rows), name=f'attn_fwd{pa...  32.3 us
    pallas_call x2, Pallas kernels, wgrad_call(): pl.pallas_call(wgrad_body, name=name, grid_spec=pltpu.PrefetchScalarGridS...  28.4 us
    pallas_call x3, Pallas kernels, add1(): pl.pallas_call(functools.partial(add1_body, len(pairs)), name='add_core',...  20.9 us
    unnamed x100, local copies, waits for them, and re-layouts  14.6 us
  transfers between devices with their start and end apart: 70, of which 28 were waited for; matrix products, arithmetic and copies ran while one was open for 2% of the time, Pallas kernels for 39%

profile of v4, /device:TPU:0, one launch (start us, length us, event | category | flops | bytes accessed | tf_op | source)
XLA Modules:
  0.0 483.2 jit_solution(8017405477234884306)
XLA Ops:
  6.8 3.0 collective-permute-start.4
  11.2 3.6 collective-permute-start.2
  15.9 5.1 %collective-permute-done.2 = bf16[1,112,1024]{2,1,0:T(8,128)(2,1)S(1)} collective-permute-done((bf16[1,112,1024]{2,1,0:T(8,128)(2,1)S(1)}, bf16[1,112,1024]{2,1,0:T(8,128)(2,1)S(1)}, u32[]{:S(2)}, u32[]{:S(2)}) %collective-permute-start.2) | collective-permute-done | bytes 229408 | tf_op jit(solution)/shard_map/ppermute | solution.py:771
  21.0 12.8 %collective-permute-done.1 = bf16[1,112,1024]{2,1,0:T(8,128)(2,1)S(1)} collective-permute-done((bf16[1,112,1024]{2,1,0:T(8,128)(2,1)S(1)}, bf16[1,112,1024]{2,1,0:T(8,128)(2,1)S(1)}, u32[]{:S(2)}, u32[]{:S(2)}) %collective-permute-start.1) | collective-permute-done | bytes 229408 | tf_op jit(solution)/shard_map/ppermute | solution.py:771
  37.3 8.2 %collective-permute-done.9.rest_5_ = bf16[2,3,32,1024]{3,2,1,0:T(8,128)(2,1)S(1)} collective-permute-done((bf16[2,3,32,1024]{3,2,1,0:T(8,128)(2,1)S(1)}, bf16[2,3,32,1024]{3,2,1,0:T(8,128)(2,1)S(1)}, u32[]{:S(2)}, u32[]{:S(2)}) %collective-permute-start.9) | collective-permute-done | bytes 393248 | tf_op jit(solution)/shard_map/ppermute | solution.py:771
  47.4 9.0 %collective-permute-done.8.rest_4_ = bf16[2,3,32,1024]{3,2,1,0:T(8,128)(2,1)} collective-permute-done((bf16[2,3,32,1024]{3,2,1,0:T(8,128)(2,1)S(1)}, bf16[2,3,32,1024]{3,2,1,0:T(8,128)(2,1)}, u32[]{:S(2)}, u32[]{:S(2)}) %collective-permute-start.8) | collective-permute-done | bytes 393248 | tf_op jit(solution)/shard_map/ppermute | solution.py:771
  60.4 7.6 %collective-permute-done.18 = bf16[4,1536]{1,0:T(4,128)(2,1)S(1)} collective-permute-done((bf16[4,1536]{1,0:T(4,128)(2,1)S(1)}, bf16[4,1536]{1,0:T(4,128)(2,1)S(1)}, u32[]{:S(2)}, u32[]{:S(2)}) %collective-permute-start.18) | collective-permute-done | bytes 12320 | tf_op jit(solution)/shard_map/ppermute | solution.py:771
  75.1 2.9 collective-permute-start.5
  78.8 13.5 %qkv.1.q_ref.k_ref.v_ref = bf16[1024,3072]{1,0:T(8,128)(2,1)} custom-call(s32[32]{0:T(128)} %stack.215.place, bf16[1024,1024]{1,0:T(8,128)(2,1)} %bitcast.174, f32[1,3072]{1,0:T(1,128)} %bitcast.166, bf16[2,3,32,1024]{3,2,1,0:T(8,128)(2,1)} %bitcast.155, bf16[2,3,32,1024]{3,2,1,0:T(8,128)(2,1)} %bitcast.150, ...), custom_call_target="tpu_custom_call" | custom-call | flops 6442450944 | bytes 14680064 | tf_op jit(solution)/shard_map/qkv/pallas_call | solution.py:80
  92.2 8.0 %attn_fwd0.1 = (bf16[1024,1024]{1,0:T(8,128)(2,1)}, bf16[1024,1024]{1,0:T(8,128)(2,1)}, bf16[1024,1024]{1,0:T(8,128)(2,1)}) custom-call(s32[1]{0:T(128)S(6)} %copy.82.len_ref, bf16[1024,3072]{1,0:T(8,128)(2,1)} %qkv.1.q_ref.k_ref.v_ref, bf16[1024,3072]{1,0:T(8,128)(2,1)} %qkv.1.q_ref.k_ref.v_ref, bf16[1024,3072]{1,0:T(8,128)(2,1)} %qkv.1.q_ref.k_ref.v_ref), custom_call_target="tpu_custom_call" | custom-call | flops 4294967296 | bytes 3145728 | tf_op jit(solution)/shard_map/attn_fwd0/pallas_call | solution.py:163
  100.3 4.3 collective-permute-done.5
  109.0 8.0 %attn_fwd1.1 = (bf16[1024,1024]{1,0:T(8,128)(2,1)}, bf16[1024,1024]{1,0:T(8,128)(2,1)}, bf16[1024,1024]{1,0:T(8,128)(2,1)}) custom-call(s32[1]{0:T(128)S(6)} %copy.82.len_ref, bf16[1024,3072]{1,0:T(8,128)(2,1)} %qkv.1.q_ref.k_ref.v_ref, bf16[1024,3072]{1,0:T(8,128)(2,1)} %qkv.1.q_ref.k_ref.v_ref, ...), custom_call_target="tpu_custom_call", output_to_operand_aliasing={{0}: (4, {}), {1}: (5, {}), {2}: (6, {})} | custom-call | flops 4294967296 | bytes 3145728 | tf_op jit(solution)/shard_map/attn_fwd1/pallas_call | solution.py:163
  117.2 8.2 %attn_fwd2.1 = (bf16[1024,1024]{1,0:T(8,128)(2,1)}, bf16[1024,1024]{1,0:T(8,128)(2,1)}, bf16[1024,1024]{1,0:T(8,128)(2,1)}) custom-call(s32[1]{0:T(128)S(6)} %copy.82.len_ref, bf16[1024,3072]{1,0:T(8,128)(2,1)} %qkv.1.q_ref.k_ref.v_ref, bf16[1024,3072]{1,0:T(8,128)(2,1)} %qkv.1.q_ref.k_ref.v_ref, ...), custom_call_target="tpu_custom_call", output_to_operand_aliasing={{0}: (4, {}), {1}: (5, {}), {2}: (6, {})} | custom-call | flops 4294967296 | bytes 3145728 | tf_op jit(solution)/shard_map/attn_fwd2/pallas_call | solution.py:163
  125.4 9.4 %collective-permute-done.26.rest_6_ = bf16[2,9,32,1024]{3,2,1,0:T(8,128)(2,1)S(1)} collective-permute-done((bf16[2,9,32,1024]{3,2,1,0:T(8,128)(2,1)S(1)}, bf16[2,9,32,1024]{3,2,1,0:T(8,128)(2,1)S(1)}, u32[]{:S(2)}, u32[]{:S(2)}) %collective-permute-start.26) | collective-permute-done | bytes 1179680 | tf_op jit(solution)/shard_map/ppermute | solution.py:771
  140.5 8.0 %attn_fwd3.1 = (bf16[1024,1024]{1,0:T(8,128)(2,1)}, bf16[1024,1024]{1,0:T(8,128)(2,1)}, bf16[1024,1024]{1,0:T(8,128)(2,1)}) custom-call(s32[1]{0:T(128)S(6)} %copy.82.len_ref, bf16[1024,3072]{1,0:T(8,128)(2,1)} %qkv.1.q_ref.k_ref.v_ref, bf16[1024,3072]{1,0:T(8,128)(2,1)} %qkv.1.q_ref.k_ref.v_ref, ...), custom_call_target="tpu_custom_call", output_to_operand_aliasing={{0}: (4, {}), {1}: (5, {}), {2}: (6, {})} | custom-call | flops 4294967296 | bytes 3145728 | tf_op jit(solution)/shard_map/attn_fwd3/pallas_call | solution.py:163
  148.5 4.2 collective-permute-done.25.rest_8_
  157.5 60.8 %row_local.1 = (bf16[1024,1024]{1,0:T(8,128)(2,1)}, bf16[1024,4096]{1,0:T(8,128)(2,1)}, bf16[1024,1024]{1,0:T(8,128)(2,1)}, bf16[1024,1024]{1,0:T(8,128)(2,1)}, ...) custom-call(s32[1]{0:T(128)S(6)} %copy.82.len_ref, ...), custom_call_target="tpu_custom_call" | custom-call | flops 38654705664 | bytes 60817408 | tf_op jit(solution)/shard_map/row_local/pallas_call | solution.py:364
  218.2 14.4 %wgrad_out.1 = (bf16[16,128,1024]{2,1,0:T(8,128)(2,1)}, bf16[16,128,1024]{2,1,0:T(8,128)(2,1)}) custom-call(s32[1]{0:T(128)} %bitcast.62.core, bf16[1024,4096]{1,0:T(8,128)(2,1)} %get-tuple-element.239.a_ref, bf16[1024,1024]{1,0:T(8,128)(2,1)} %get-tuple-element.240.b_ref), custom_call_target="tpu_custom_call" | custom-call | flops 8589934592 | bytes 18874368 | tf_op jit(solution)/shard_map/wgrad_out/pallas_call | solution.py:438
  232.7 14.0 %wgrad_in.1 = (bf16[16,128,1024]{2,1,0:T(8,128)(2,1)}, bf16[16,128,1024]{2,1,0:T(8,128)(2,1)}) custom-call(s32[1]{0:T(128)} %bitcast.62.core, bf16[1024,1024]{1,0:T(8,128)(2,1)} %get-tuple-element.235.a_ref, bf16[1024,4096]{1,0:T(8,128)(2,1)} %get-tuple-element.236.b_ref), custom_call_target="tpu_custom_call" | custom-call | flops 8589934592 | bytes 18874368 | tf_op jit(solution)/shard_map/wgrad_in/pallas_call | solution.py:438
  247.7 6.6 %add_core.3 = (bf16[4,128,1024]{2,1,0:T(8,128)(2,1)}, bf16[4,128,1024]{2,1,0:T(8,128)(2,1)}, bf16[4,128,1024]{2,1,0:T(8,128)(2,1)}, bf16[4,128,1024]{2,1,0:T(8,128)(2,1)}) custom-call(s32[4]{0:T(128)} %pad_add_fusion.here, bf16[4,2,2,128,1024]{4,3,2,1,0:T(8,128)(2,1)} %bitcast.105, bf16[4,2,2,128,1024]{4,3,2,1,0:T(8,128)(2,1)} %bitcast.66.refs_1_.refs_3_.refs_5_.refs_7_, ...), custom_call_target="tpu_custom_call" | custom-call | flops 2097152 | bytes 12582912 | tf_op jit(solution)/shard_map/add_core/pallas_call | solution.py:601
  254.2 6.5 %wgrad_ao.1 = (bf16[16,48,1024]{2,1,0:T(8,128)(2,1)}, bf16[16,48,1024]{2,1,0:T(8,128)(2,1)}) custom-call(s32[1]{0:T(128)} %bitcast.62.core, bf16[1024,1024]{1,0:T(8,128)(2,1)} %get-tuple-element.222.ctx_ref.a_ref, bf16[1024,1024]{1,0:T(8,128)(2,1)} %get-tuple-element.307.b_ref.g_ref, f32[8,1024]{1,0:T(8,128)} %get-tuple-element.245.sums_ref, ...), custom_call_target="tpu_custom_call" | custom-call | flops 2147483648 | bytes 6291456 | tf_op jit(solution)/shard_map/wgrad_ao/pallas_call | solution.py:475
  265.6 8.1 %add_core.4 = (bf16[4,176,1024]{2,1,0:T(8,128)(2,1)}, bf16[4,176,1024]{2,1,0:T(8,128)(2,1)}, bf16[4,176,1024]{2,1,0:T(8,128)(2,1)}, bf16[4,176,1024]{2,1,0:T(8,128)(2,1)}) custom-call(s32[4]{0:T(128)} %pad_add_fusion.here, bf16[4,2,2,128,1024]{4,3,2,1,0:T(8,128)(2,1)} %bitcast.101, bf16[4,2,2,128,1024]{4,3,2,1,0:T(8,128)(2,1)} %bitcast.64.refs_1_.refs_3_.refs_5_.refs_7_, ...), custom_call_target="tpu_custom_call" | custom-call | flops 2883584 | bytes 17301504 | tf_op jit(solution)/shard_map/add_core/pallas_call | solution.py:601
  276.3 14.1 %attn_bwd0.1 = (bf16[1024,1024]{1,0:T(8,128)(2,1)}, bf16[1024,1024]{1,0:T(8,128)(2,1)}, bf16[1024,1024]{1,0:T(8,128)(2,1)}, f32[1,1024]{1,0:T(1,128)}, f32[1,1024]{1,0:T(1,128)}) custom-call(s32[1]{0:T(128)S(6)} %copy.82.len_ref, bf16[1024,1024]{1,0:T(8,128)(2,1)} %get-tuple-element.250.qa0_ref, bf16[1024,1024]{1,0:T(8,128)(2,1)} %get-tuple-element.251.qa1_ref, ...), custom_call_target="tpu_custom_call" | custom-call | flops 10737418240 | bytes 4718592 | tf_op jit(solution)/shard_map/attn_bwd0/pallas_call | solution.py:247
  291.3 4.0 add_plane.3
  295.3 14.2 %attn_bwd1.1 = (bf16[1024,1024]{1,0:T(8,128)(2,1)}, bf16[1024,1024]{1,0:T(8,128)(2,1)}, bf16[1024,1024]{1,0:T(8,128)(2,1)}, f32[1,1024]{1,0:T(1,128)}, f32[1,1024]{1,0:T(1,128)}) custom-call(s32[1]{0:T(128)S(6)} %copy.82.len_ref, ...), custom_call_target="tpu_custom_call", output_to_operand_aliasing={{0}: (7, {}), {1}: (8, {}), {2}: (9, {}), {3}: (10, {}), {4... | custom-call | flops 10737418240 | bytes 4718592 | tf_op jit(solution)/shard_map/attn_bwd1/pallas_call | solution.py:247
  311.1 6.9 %collective-permute-done.44 = bf16[4,176,1024]{2,1,0:T(8,128)(2,1)S(1)} collective-permute-done((bf16[4,176,1024]{2,1,0:T(8,128)(2,1)}, bf16[4,176,1024]{2,1,0:T(8,128)(2,1)S(1)}, u32[]{:S(2)}, u32[]{:S(2)}) %collective-permute-start.44) | collective-permute-done | bytes 1441824 | tf_op jit(solution)/shard_map/ppermute | solution.py:771
  320.1 4.8 add_plane.4
  324.9 14.2 %attn_bwd2.1 = (bf16[1024,1024]{1,0:T(8,128)(2,1)}, bf16[1024,1024]{1,0:T(8,128)(2,1)}, bf16[1024,1024]{1,0:T(8,128)(2,1)}, f32[1,1024]{1,0:T(1,128)}, f32[1,1024]{1,0:T(1,128)}) custom-call(s32[1]{0:T(128)S(6)} %copy.82.len_ref, ...), custom_call_target="tpu_custom_call", output_to_operand_aliasing={{0}: (7, {}), {1}: (8, {}), {2}: (9, {}), {3}: (10, {}), {4... | custom-call | flops 10737418240 | bytes 4718592 | tf_op jit(solution)/shard_map/attn_bwd2/pallas_call | solution.py:247
  340.1 3.5 add_z.3
  344.6 2.8 collective-permute-start.52
  349.6 14.3 %attn_bwd3.1 = (bf16[1024,1024]{1,0:T(8,128)(2,1)}, bf16[1024,1024]{1,0:T(8,128)(2,1)}, bf16[1024,1024]{1,0:T(8,128)(2,1)}, f32[1,1024]{1,0:T(1,128)}, f32[1,1024]{1,0:T(1,128)}) custom-call(s32[1]{0:T(128)S(6)} %copy.82.len_ref, ...), custom_call_target="tpu_custom_call", output_to_operand_aliasing={{0}: (7, {}), {1}: (8, {}), {2}: (9, {}), {3}: (10, {}), {4... | custom-call | flops 10737418240 | bytes 4718592 | tf_op jit(solution)/shard_map/attn_bwd3/pallas_call | solution.py:247
  365.6 3.9 add_z.4
  370.2 3.3 collective-permute-start.54
  373.4 14.0 %wgrad_qkv.1 = (bf16[16,112,1024]{2,1,0:T(8,128)(2,1)}, bf16[16,112,1024]{2,1,0:T(8,128)(2,1)}) custom-call(s32[1]{0:T(128)} %bitcast.62.core, bf16[1024,1024]{1,0:T(8,128)(2,1)} %bitcast.176, bf16[1024,1024]{1,0:T(8,128)(2,1)} %get-tuple-element.297.q_ref.dq_ref, bf16[1024,1024]{1,0:T(8,128)(2,1)} %get-tuple-element.298.k_ref.dk_ref, ...), custom_call_target="tpu_custom_call" | custom-call | flops 6442450944 | bytes 14680064 | tf_op jit(solution)/shard_map/wgrad_qkv/pallas_call | solution.py:512
  388.2 6.6 %collective-permute-done.55 = bf16[16,112,1024]{2,1,0:T(8,128)(2,1)S(1)} collective-permute-done((bf16[16,112,1024]{2,1,0:T(8,128)(2,1)}, bf16[16,112,1024]{2,1,0:T(8,128)(2,1)S(1)}, u32[]{:S(2)}, u32[]{:S(2)}) %collective-permute-start.55) | collective-permute-done | bytes 3670048 | tf_op jit(solution)/shard_map/ppermute | solution.py:771
  396.7 6.2 %add_core.5 = (bf16[4,112,1024]{2,1,0:T(8,128)(2,1)}, bf16[4,112,1024]{2,1,0:T(8,128)(2,1)}, bf16[4,112,1024]{2,1,0:T(8,128)(2,1)}, bf16[4,112,1024]{2,1,0:T(8,128)(2,1)}) custom-call(s32[4]{0:T(128)} %pad_add_fusion.here, bf16[4,2,2,112,1024]{4,3,2,1,0:T(8,128)(2,1)} %bitcast.109, bf16[4,2,2,112,1024]{4,3,2,1,0:T(8,128)(2,1)} %bitcast.113, ...), custom_call_target="tpu_custom_call" | custom-call | flops 1835008 | bytes 11010048 | tf_op jit(solution)/shard_map/add_core/pallas_call | solution.py:601
  404.7 13.6 %grad_tok.1 = bf16[1024,1024]{1,0:T(8,128)(2,1)} custom-call(s32[32]{0:T(128)} %stack.215.place, bf16[1024,1024]{1,0:T(8,128)(2,1)} %get-tuple-element.307.b_ref.g_ref, bf16[1024,1024]{1,0:T(8,128)(2,1)} %get-tuple-element.297.q_ref.dq_ref, bf16[1024,1024]{1,0:T(8,128)(2,1)} %get-tuple-element.298.k_ref.dk_ref, ...), custom_call_target="tpu_custom_call" | custom-call | flops 6442450944 | bytes 16777216 | tf_op jit(solution)/shard_map/grad_tok/pallas_call | solution.py:548
  418.3 4.0 collective-permute-done.56.refs_6_
  422.3 3.2 collective-permute-done.57
  427.3 3.9 add_plane.5
  432.8 2.8 add_last.2.own
  435.6 7.3 %collective-permute-done.59.ag = bf16[2,112,1024]{2,1,0:T(8,128)(2,1)S(1)} collective-permute-done((bf16[2,112,1024]{2,1,0:T(8,128)(2,1)}, bf16[2,112,1024]{2,1,0:T(8,128)(2,1)S(1)}, u32[]{:S(2)}, u32[]{:S(2)}) %collective-permute-start.59) | collective-permute-done | bytes 458784 | tf_op jit(solution)/shard_map/ppermute | solution.py:771
  443.9 3.3 add_z.5
  452.0 6.8 %collective-permute-done.62.refs_1_ = bf16[1,112,1024]{2,1,0:T(8,128)(2,1)S(1)} collective-permute-done((bf16[1,112,1024]{2,1,0:T(8,128)(2,1)}, bf16[1,112,1024]{2,1,0:T(8,128)(2,1)S(1)}, u32[]{:S(2)}, u32[]{:S(2)}) %collective-permute-start.62) | collective-permute-done | bytes 229408 | tf_op jit(solution)/shard_map/ppermute | solution.py:771
  458.8 6.6 %collective-permute-done.63.refs_2_ = bf16[1,112,1024]{2,1,0:T(8,128)(2,1)S(1)} collective-permute-done((bf16[1,112,1024]{2,1,0:T(8,128)(2,1)}, bf16[1,112,1024]{2,1,0:T(8,128)(2,1)S(1)}, u32[]{:S(2)}, u32[]{:S(2)}) %collective-permute-start.63) | collective-permute-done | bytes 229408 | tf_op jit(solution)/shard_map/ppermute | solution.py:771
  466.8 2.1 add_last.3.own
  472.7 4.8 final.2
  479.8 3.2 final.3
  (255 shorter events, 80.5 us)
Async XLA Ops:
  6.8 27.0 %collective-permute-start.4 = (bf16[1,9,32,1024]{3,2,1,0:T(8,128)(2,1)}, bf16[1,9,32,1024]{3,2,1,0:T(8,128)(2,1)S(1)}, u32[]{:S(2)}, u32[]{:S(2)}) collective-permute-start(bf16[1,9,32,1024]{3,2,1,0:T(8,128)(2,1)} %pack.1.rest_0_), channel_id=1, source_target_pairs={{0,1},{1,0},{2,3},{3,2},{4,5},{5,4},{6,7},{7,6},{8,9},{9,8},{10,11... | collective-permute-start | bytes 1769480 | tf_op jit(solution)/shard_map/ppermute | solution.py:771
  9.8 24.0 %collective-permute-start.3 = (bf16[1,9,32,1024]{3,2,1,0:T(8,128)(2,1)}, bf16[1,9,32,1024]{3,2,1,0:T(8,128)(2,1)}, u32[]{:S(2)}, u32[]{:S(2)}) collective-permute-start(bf16[1,9,32,1024]{3,2,1,0:T(8,128)(2,1)} %pack.1.rest_0_), channel_id=1, source_target_pairs={{0,16},{1,17},{2,18},{3,19},{4,20},{5,21},{6,22},{7,23},{8,24},{9,... | collective-permute-start | bytes 1769480 | tf_op jit(solution)/shard_map/ppermute | solution.py:771
  14.8 18.9 %collective-permute-start.1 = (bf16[1,112,1024]{2,1,0:T(8,128)(2,1)S(1)}, bf16[1,112,1024]{2,1,0:T(8,128)(2,1)S(1)}, u32[]{:S(2)}, u32[]{:S(2)}) collective-permute-start(bf16[1,112,1024]{2,1,0:T(8,128)(2,1)S(1)} %copy-done.8), channel_id=1, source_target_pairs={{0,4},{1,5},{2,6},{3,7},{4,0},{5,1},{6,2},{7,3},{8,12},{9,13},{10,... | collective-permute-start | bytes 688136 | tf_op jit(solution)/shard_map/ppermute | solution.py:771
  14.9 18.9 %collective-permute-start = (bf16[1,112,1024]{2,1,0:T(8,128)(2,1)S(1)}, bf16[1,112,1024]{2,1,0:T(8,128)(2,1)S(1)}, u32[]{:S(2)}, u32[]{:S(2)}) collective-permute-start(bf16[1,112,1024]{2,1,0:T(8,128)(2,1)S(1)} %copy-done.8), channel_id=1, source_target_pairs={{0,2},{1,3},{2,4},{3,5},{4,6},{5,7},{6,0},{7,1},{8,10},{9,11},{10,... | collective-permute-start | bytes 688136 | tf_op jit(solution)/shard_map/ppermute | solution.py:771
  34.0 11.5 %collective-permute-start.9 = (bf16[2,3,32,1024]{3,2,1,0:T(8,128)(2,1)S(1)}, bf16[2,3,32,1024]{3,2,1,0:T(8,128)(2,1)S(1)}, u32[]{:S(2)}, u32[]{:S(2)}) collective-permute-start(bf16[2,3,32,1024]{3,2,1,0:T(8,128)(2,1)S(1)} %bitcast.148), channel_id=1, source_target_pairs={{0,1},{1,0},{2,3},{3,2},{4,5},{5,4},{6,7},{7,6},{8,9},{9,8},{10,11... | collective-permute-start | bytes 1179656 | tf_op jit(solution)/shard_map/ppermute | solution.py:771
  34.6 11.5 %collective-permute-start.7 = (bf16[2,3,32,1024]{3,2,1,0:T(8,128)(2,1)S(1)}, bf16[2,3,32,1024]{3,2,1,0:T(8,128)(2,1)}, u32[]{:S(2)}, u32[]{:S(2)}) collective-permute-start(bf16[2,3,32,1024]{3,2,1,0:T(8,128)(2,1)S(1)} %bitcast.149), channel_id=1, source_target_pairs={{0,16},{1,17},{2,18},{3,19},{4,20},{5,21},{6,22},{7,23},{8,24},{9,... | collective-permute-start | bytes 1179656 | tf_op jit(solution)/shard_map/ppermute | solution.py:771
  35.1 34.4 %collective-permute-start.15 = (bf16[1,9,32,1024]{3,2,1,0:T(8,128)(2,1)}, bf16[1,9,32,1024]{3,2,1,0:T(8,128)(2,1)S(1)}, u32[]{:S(2)}, u32[]{:S(2)}) collective-permute-start(bf16[1,9,32,1024]{3,2,1,0:T(8,128)(2,1)} %pack.1.rest_0_), channel_id=1, source_target_pairs={{0,6},{1,7},{2,0},{3,1},{4,2},{5,3},{6,4},{7,5},{8,14},{9,15},{10,... | collective-permute-start | bytes 1769480 | tf_op jit(solution)/shard_map/ppermute | solution.py:771
  35.1 34.7 %collective-permute-start.14 = (bf16[1,9,32,1024]{3,2,1,0:T(8,128)(2,1)}, bf16[1,9,32,1024]{3,2,1,0:T(8,128)(2,1)S(1)}, u32[]{:S(2)}, u32[]{:S(2)}) collective-permute-start(bf16[1,9,32,1024]{3,2,1,0:T(8,128)(2,1)} %pack.1.rest_0_), channel_id=1, source_target_pairs={{0,2},{1,3},{2,4},{3,5},{4,6},{5,7},{6,0},{7,1},{8,10},{9,11},{10,... | collective-permute-start | bytes 1769480 | tf_op jit(solution)/shard_map/ppermute | solution.py:771
  45.5 10.9 %collective-permute-start.8 = (bf16[2,3,32,1024]{3,2,1,0:T(8,128)(2,1)S(1)}, bf16[2,3,32,1024]{3,2,1,0:T(8,128)(2,1)}, u32[]{:S(2)}, u32[]{:S(2)}) collective-permute-start(bf16[2,3,32,1024]{3,2,1,0:T(8,128)(2,1)S(1)} %bitcast.153), channel_id=1, source_target_pairs={{0,16},{1,17},{2,18},{3,19},{4,20},{5,21},{6,22},{7,23},{8,24},{9,... | collective-permute-start | bytes 1179656 | tf_op jit(solution)/shard_map/ppermute | solution.py:771
  46.1 10.6 %collective-permute-start.6 = (bf16[2,3,32,1024]{3,2,1,0:T(8,128)(2,1)S(1)}, bf16[2,3,32,1024]{3,2,1,0:T(8,128)(2,1)}, u32[]{:S(2)}, u32[]{:S(2)}) collective-permute-start(bf16[2,3,32,1024]{3,2,1,0:T(8,128)(2,1)S(1)} %bitcast.154), channel_id=1, source_target_pairs={{0,1},{1,0},{2,3},{3,2},{4,5},{5,4},{6,7},{7,6},{8,9},{9,8},{10,11... | collective-permute-start | bytes 1179656 | tf_op jit(solution)/shard_map/ppermute | solution.py:771
  56.7 13.5 %collective-permute-start.12 = (bf16[2,3,32,1024]{3,2,1,0:T(8,128)(2,1)}, bf16[2,3,32,1024]{3,2,1,0:T(8,128)(2,1)}, u32[]{:S(2)}, u32[]{:S(2)}) collective-permute-start(bf16[2,3,32,1024]{3,2,1,0:T(8,128)(2,1)} %collective-permute-done.6.rest_2_), channel_id=1, source_target_pairs={{0,16},{1,17},{2,18},{3,19},{4,20},{5,21},{6,22},{7,23},{8,24},{9,... | collective-permute-start | bytes 1179656 | tf_op jit(solution)/shard_map/ppermute | solution.py:771
  58.2 12.4 %collective-permute-start.13 = (bf16[2,3,32,1024]{3,2,1,0:T(8,128)(2,1)}, bf16[2,3,32,1024]{3,2,1,0:T(8,128)(2,1)}, u32[]{:S(2)}, u32[]{:S(2)}) collective-permute-start(bf16[2,3,32,1024]{3,2,1,0:T(8,128)(2,1)} %collective-permute-done.7.rest_3_), channel_id=1, source_target_pairs={{0,1},{1,0},{2,3},{3,2},{4,5},{5,4},{6,7},{7,6},{8,9},{9,8},{10,11... | collective-permute-start | bytes 1179656 | tf_op jit(solution)/shard_map/ppermute | solution.py:771
  72.8 31.8 %collective-permute-start.17 = (bf16[2,9,32,1024]{3,2,1,0:T(8,128)(2,1)}, bf16[2,9,32,1024]{3,2,1,0:T(8,128)(2,1)}, u32[]{:S(2)}, u32[]{:S(2)}) collective-permute-start(bf16[2,9,32,1024]{3,2,1,0:T(8,128)(2,1)} %constant_dynamic-update-slice_fusion.rest_2_), channel_id=1, source_target_pairs={{0,1},{1,0},{2,3},{3,2},{4,5},{5,4},{6,7},{7,6},{8,9},{9,8},{10,11... | collective-permute-start | bytes 3538952 | tf_op jit(solution)/shard_map/ppermute | solution.py:771
  73.4 31.2 %collective-permute-start.16 = (bf16[2,9,32,1024]{3,2,1,0:T(8,128)(2,1)}, bf16[2,9,32,1024]{3,2,1,0:T(8,128)(2,1)}, u32[]{:S(2)}, u32[]{:S(2)}) collective-permute-start(bf16[2,9,32,1024]{3,2,1,0:T(8,128)(2,1)} %constant_dynamic-update-slice_fusion.rest_2_), channel_id=1, source_target_pairs={{0,16},{1,17},{2,18},{3,19},{4,20},{5,21},{6,22},{7,23},{8,24},{9,... | collective-permute-start | bytes 3538952 | tf_op jit(solution)/shard_map/ppermute | solution.py:771
  75.0 31.4 %collective-permute-start.28 = (bf16[1,9,32,1024]{3,2,1,0:T(8,128)(2,1)S(1)}, bf16[1,9,32,1024]{3,2,1,0:T(8,128)(2,1)}, u32[]{:S(2)}, u32[]{:S(2)}) collective-permute-start(bf16[1,9,32,1024]{3,2,1,0:T(8,128)(2,1)S(1)} %copy-done.14), channel_id=1, source_target_pairs={{0,8},{1,9},{2,10},{3,11},{4,12},{5,13},{6,14},{7,15},{8,0},{9,1},... | collective-permute-start | bytes 1769480 | tf_op jit(solution)/shard_map/ppermute | solution.py:771
  75.1 29.4 %collective-permute-start.5 = (bf16[1,9,32,1024]{3,2,1,0:T(8,128)(2,1)S(1)}, bf16[1,9,32,1024]{3,2,1,0:T(8,128)(2,1)S(1)}, u32[]{:S(2)}, u32[]{:S(2)}) collective-permute-start(bf16[1,9,32,1024]{3,2,1,0:T(8,128)(2,1)S(1)} %copy-done.14), channel_id=1, source_target_pairs={{0,4},{1,5},{2,6},{3,7},{4,0},{5,1},{6,2},{7,3},{8,12},{9,13},{10,... | collective-permute-start | bytes 1769480 | tf_op jit(solution)/shard_map/ppermute | solution.py:771
  78.0 29.5 %collective-permute-start.29 = (bf16[1,9,32,1024]{3,2,1,0:T(8,128)(2,1)}, bf16[1,9,32,1024]{3,2,1,0:T(8,128)(2,1)}, u32[]{:S(2)}, u32[]{:S(2)}) collective-permute-start(bf16[1,9,32,1024]{3,2,1,0:T(8,128)(2,1)} %collective-permute-done.3.rest_1_), channel_id=1, source_target_pairs={{0,8},{1,9},{2,10},{3,11},{4,12},{5,13},{6,14},{7,15},{8,0},{9,1},... | collective-permute-start | bytes 1769480 | tf_op jit(solution)/shard_map/ppermute | solution.py:771
  104.5 12.5 %collective-permute-start.30 = (bf16[2,9,32,1024]{3,2,1,0:T(8,128)(2,1)}, bf16[2,9,32,1024]{3,2,1,0:T(8,128)(2,1)}, u32[]{:S(2)}, u32[]{:S(2)}) collective-permute-start(bf16[2,9,32,1024]{3,2,1,0:T(8,128)(2,1)} %constant_dynamic-update-slice_fusion.rest_2_), channel_id=1, source_target_pairs={{0,8},{1,9},{2,10},{3,11},{4,12},{5,13},{6,14},{7,15},{8,0},{9,1},... | collective-permute-start | bytes 3538952 | tf_op jit(solution)/shard_map/ppermute | solution.py:771
  104.5 12.6 %collective-permute-start.32 = (bf16[2,9,32,1024]{3,2,1,0:T(8,128)(2,1)}, bf16[2,9,32,1024]{3,2,1,0:T(8,128)(2,1)}, u32[]{:S(2)}, u32[]{:S(2)}) collective-permute-start(bf16[2,9,32,1024]{3,2,1,0:T(8,128)(2,1)} %collective-permute-done.17.rest_5_), channel_id=1, source_target_pairs={{0,8},{1,9},{2,10},{3,11},{4,12},{5,13},{6,14},{7,15},{8,0},{9,1},... | collective-permute-start | bytes 3538952 | tf_op jit(solution)/shard_map/ppermute | solution.py:771
  105.1 12.1 %collective-permute-start.31 = (bf16[2,9,32,1024]{3,2,1,0:T(8,128)(2,1)}, bf16[2,9,32,1024]{3,2,1,0:T(8,128)(2,1)}, u32[]{:S(2)}, u32[]{:S(2)}) collective-permute-start(bf16[2,9,32,1024]{3,2,1,0:T(8,128)(2,1)} %collective-permute-done.16.rest_4_), channel_id=1, source_target_pairs={{0,8},{1,9},{2,10},{3,11},{4,12},{5,13},{6,14},{7,15},{8,0},{9,1},... | collective-permute-start | bytes 3538952 | tf_op jit(solution)/shard_map/ppermute | solution.py:771
  106.5 28.4 %collective-permute-start.26 = (bf16[2,9,32,1024]{3,2,1,0:T(8,128)(2,1)S(1)}, bf16[2,9,32,1024]{3,2,1,0:T(8,128)(2,1)S(1)}, u32[]{:S(2)}, u32[]{:S(2)}) collective-permute-start(bf16[2,9,32,1024]{3,2,1,0:T(8,128)(2,1)S(1)} %constant_dynamic-update-slice_fusion.2.rest_3_), channel_id=1, source_target_pairs={{0,16},{1,17},{2,18},{3,19},{4,20},{5,21},{6,22},{7,23},{8,24},{9,... | collective-permute-start | bytes 3538952 | tf_op jit(solution)/shard_map/ppermute | solution.py:771
  107.5 28.1 %collective-permute-start.27 = (bf16[2,9,32,1024]{3,2,1,0:T(8,128)(2,1)S(1)}, bf16[2,9,32,1024]{3,2,1,0:T(8,128)(2,1)}, u32[]{:S(2)}, u32[]{:S(2)}) collective-permute-start(bf16[2,9,32,1024]{3,2,1,0:T(8,128)(2,1)S(1)} %pad_maximum_fusion), channel_id=1, source_target_pairs={{0,1},{1,0},{2,3},{3,2},{4,5},{5,4},{6,7},{7,6},{8,9},{9,8},{10,11... | collective-permute-start | bytes 3538952 | tf_op jit(solution)/shard_map/ppermute | solution.py:771
  117.1 22.5 %collective-permute-start.34 = (bf16[2,9,32,1024]{3,2,1,0:T(8,128)(2,1)S(1)}, bf16[2,9,32,1024]{3,2,1,0:T(8,128)(2,1)}, u32[]{:S(2)}, u32[]{:S(2)}) collective-permute-start(bf16[2,9,32,1024]{3,2,1,0:T(8,128)(2,1)S(1)} %constant_dynamic-update-slice_fusion.2.rest_3_), channel_id=1, source_target_pairs={{0,8},{1,9},{2,10},{3,11},{4,12},{5,13},{6,14},{7,15},{8,0},{9,1},... | collective-permute-start | bytes 3538952 | tf_op jit(solution)/shard_map/ppermute | solution.py:771
  137.3 15.4 %collective-permute-start.25 = (bf16[1,9,32,1024]{3,2,1,0:T(8,128)(2,1)S(1)}, bf16[1,9,32,1024]{3,2,1,0:T(8,128)(2,1)}, u32[]{:S(2)}, u32[]{:S(2)}) collective-permute-start(bf16[1,9,32,1024]{3,2,1,0:T(8,128)(2,1)S(1)} %slice.85), channel_id=1, source_target_pairs={{0,16},{1,17},{2,18},{3,19},{4,20},{5,21},{6,22},{7,23},{8,24},{9,... | collective-permute-start | bytes 1769480 | tf_op jit(solution)/shard_map/ppermute | solution.py:771
  138.4 15.1 %collective-permute-start.33 = (bf16[1,9,32,1024]{3,2,1,0:T(8,128)(2,1)S(1)}, bf16[1,9,32,1024]{3,2,1,0:T(8,128)(2,1)}, u32[]{:S(2)}, u32[]{:S(2)}) collective-permute-start(bf16[1,9,32,1024]{3,2,1,0:T(8,128)(2,1)S(1)} %slice.87), channel_id=1, source_target_pairs={{0,1},{1,0},{2,3},{3,2},{4,5},{5,4},{6,7},{7,6},{8,9},{9,8},{10,11... | collective-permute-start | bytes 1769480 | tf_op jit(solution)/shard_map/ppermute | solution.py:771
  232.6 15.1 %collective-permute-start.40 = (bf16[16,128,1024]{2,1,0:T(8,128)(2,1)}, bf16[16,128,1024]{2,1,0:T(8,128)(2,1)}, u32[]{:S(2)}, u32[]{:S(2)}) collective-permute-start(bf16[16,128,1024]{2,1,0:T(8,128)(2,1)} %get-tuple-element.242), channel_id=1, source_target_pairs={{0,8},{1,9},{2,10},{3,11},{4,12},{5,13},{6,14},{7,15},{8,0},{9,1},... | collective-permute-start | bytes 12582920 | tf_op jit(solution)/shard_map/ppermute | solution.py:771
  246.7 16.7 %collective-permute-start.39 = (bf16[16,128,1024]{2,1,0:T(8,128)(2,1)}, bf16[16,128,1024]{2,1,0:T(8,128)(2,1)}, u32[]{:S(2)}, u32[]{:S(2)}) collective-permute-start(bf16[16,128,1024]{2,1,0:T(8,128)(2,1)} %get-tuple-element.238), channel_id=1, source_target_pairs={{0,8},{1,9},{2,10},{3,11},{4,12},{5,13},{6,14},{7,15},{8,0},{9,1},... | collective-permute-start | bytes 12582920 | tf_op jit(solution)/shard_map/ppermute | solution.py:771
  260.9 29.4 %collective-permute-start.42 = (bf16[4,128,1024]{2,1,0:T(8,128)(2,1)}, bf16[4,128,1024]{2,1,0:T(8,128)(2,1)S(1)}, u32[]{:S(2)}, u32[]{:S(2)}) collective-permute-start(bf16[4,128,1024]{2,1,0:T(8,128)(2,1)} %get-tuple-element.256), channel_id=1, source_target_pairs={{0,16},{1,17},{2,18},{3,19},{4,20},{5,21},{6,22},{7,23},{8,24},{9,... | collective-permute-start | bytes 3145736 | tf_op jit(solution)/shard_map/ppermute | solution.py:771
  261.9 28.4 %collective-permute-start.43 = (bf16[4,128,1024]{2,1,0:T(8,128)(2,1)}, bf16[4,128,1024]{2,1,0:T(8,128)(2,1)}, u32[]{:S(2)}, u32[]{:S(2)}) collective-permute-start(bf16[4,128,1024]{2,1,0:T(8,128)(2,1)} %get-tuple-element.258), channel_id=1, source_target_pairs={{0,1},{1,0},{2,3},{3,2},{4,5},{5,4},{6,7},{7,6},{8,9},{9,8},{10,11... | collective-permute-start | bytes 3145736 | tf_op jit(solution)/shard_map/ppermute | solution.py:771
  273.7 44.3 %collective-permute-start.44 = (bf16[4,176,1024]{2,1,0:T(8,128)(2,1)}, bf16[4,176,1024]{2,1,0:T(8,128)(2,1)S(1)}, u32[]{:S(2)}, u32[]{:S(2)}) collective-permute-start(bf16[4,176,1024]{2,1,0:T(8,128)(2,1)} %get-tuple-element.267), channel_id=1, source_target_pairs={{0,16},{1,17},{2,18},{3,19},{4,20},{5,21},{6,22},{7,23},{8,24},{9,... | collective-permute-start | bytes 4325384 | tf_op jit(solution)/shard_map/ppermute | solution.py:771
  274.7 44.3 %collective-permute-start.45 = (bf16[4,176,1024]{2,1,0:T(8,128)(2,1)}, bf16[4,176,1024]{2,1,0:T(8,128)(2,1)S(1)}, u32[]{:S(2)}, u32[]{:S(2)}) collective-permute-start(bf16[4,176,1024]{2,1,0:T(8,128)(2,1)} %get-tuple-element.269), channel_id=1, source_target_pairs={{0,1},{1,0},{2,3},{3,2},{4,5},{5,4},{6,7},{7,6},{8,9},{9,8},{10,11... | collective-permute-start | bytes 4325384 | tf_op jit(solution)/shard_map/ppermute | solution.py:771
  309.5 29.6 %collective-permute-start.46 = (bf16[2,128,1024]{2,1,0:T(8,128)(2,1)}, bf16[2,128,1024]{2,1,0:T(8,128)(2,1)S(1)}, u32[]{:S(2)}, u32[]{:S(2)}) collective-permute-start(bf16[2,128,1024]{2,1,0:T(8,128)(2,1)} %get-tuple-element.278), channel_id=1, source_target_pairs={{0,1},{1,0},{2,3},{3,2},{4,5},{5,4},{6,7},{7,6},{8,9},{9,8},{10,11... | collective-permute-start | bytes 1572872 | tf_op jit(solution)/shard_map/ppermute | solution.py:771
  310.1 29.1 %collective-permute-start.47 = (bf16[2,128,1024]{2,1,0:T(8,128)(2,1)}, bf16[2,128,1024]{2,1,0:T(8,128)(2,1)S(1)}, u32[]{:S(2)}, u32[]{:S(2)}) collective-permute-start(bf16[2,128,1024]{2,1,0:T(8,128)(2,1)} %get-tuple-element.280), channel_id=1, source_target_pairs={{0,16},{1,17},{2,18},{3,19},{4,20},{5,21},{6,22},{7,23},{8,24},{9,... | collective-permute-start | bytes 1572872 | tf_op jit(solution)/shard_map/ppermute | solution.py:771
  343.6 25.9 %collective-permute-start.50 = (bf16[1,128,1024]{2,1,0:T(8,128)(2,1)}, bf16[1,128,1024]{2,1,0:T(8,128)(2,1)S(1)}, u32[]{:S(2)}, u32[]{:S(2)}) collective-permute-start(bf16[1,128,1024]{2,1,0:T(8,128)(2,1)} %get-tuple-element.293), channel_id=1, source_target_pairs={{0,2},{1,3},{2,4},{3,5},{4,6},{5,7},{6,0},{7,1},{8,10},{9,11},{10,... | collective-permute-start | bytes 786440 | tf_op jit(solution)/shard_map/ppermute | solution.py:771
  343.6 25.9 %collective-permute-start.51 = (bf16[1,128,1024]{2,1,0:T(8,128)(2,1)}, bf16[1,128,1024]{2,1,0:T(8,128)(2,1)S(1)}, u32[]{:S(2)}, u32[]{:S(2)}) collective-permute-start(bf16[1,128,1024]{2,1,0:T(8,128)(2,1)} %get-tuple-element.294), channel_id=1, source_target_pairs={{0,4},{1,5},{2,6},{3,7},{4,0},{5,1},{6,2},{7,3},{8,12},{9,13},{10,... | collective-permute-start | bytes 786440 | tf_op jit(solution)/shard_map/ppermute | solution.py:771
  344.6 24.9 %collective-permute-start.52 = (bf16[1,128,1024]{2,1,0:T(8,128)(2,1)}, bf16[1,128,1024]{2,1,0:T(8,128)(2,1)S(1)}, u32[]{:S(2)}, u32[]{:S(2)}) collective-permute-start(bf16[1,128,1024]{2,1,0:T(8,128)(2,1)} %get-tuple-element.295), channel_id=1, source_target_pairs={{0,6},{1,7},{2,0},{3,1},{4,2},{5,3},{6,4},{7,5},{8,14},{9,15},{10,... | collective-permute-start | bytes 786440 | tf_op jit(solution)/shard_map/ppermute | solution.py:771
  347.4 16.4 %collective-permute-start.48 = (bf16[2,176,1024]{2,1,0:T(8,128)(2,1)}, bf16[2,176,1024]{2,1,0:T(8,128)(2,1)S(1)}, u32[]{:S(2)}, u32[]{:S(2)}) collective-permute-start(bf16[2,176,1024]{2,1,0:T(8,128)(2,1)} %get-tuple-element.289), channel_id=1, source_target_pairs={{0,1},{1,0},{2,3},{3,2},{4,5},{5,4},{6,7},{7,6},{8,9},{9,8},{10,11... | collective-permute-start | bytes 2162696 | tf_op jit(solution)/shard_map/ppermute | solution.py:771
  349.0 15.8 %collective-permute-start.49 = (bf16[2,176,1024]{2,1,0:T(8,128)(2,1)}, bf16[2,176,1024]{2,1,0:T(8,128)(2,1)S(1)}, u32[]{:S(2)}, u32[]{:S(2)}) collective-permute-start(bf16[2,176,1024]{2,1,0:T(8,128)(2,1)} %get-tuple-element.291), channel_id=1, source_target_pairs={{0,16},{1,17},{2,18},{3,19},{4,20},{5,21},{6,22},{7,23},{8,24},{9,... | collective-permute-start | bytes 2162696 | tf_op jit(solution)/shard_map/ppermute | solution.py:771
  369.6 17.9 %collective-permute-start.53 = (bf16[1,176,1024]{2,1,0:T(8,128)(2,1)}, bf16[1,176,1024]{2,1,0:T(8,128)(2,1)S(1)}, u32[]{:S(2)}, u32[]{:S(2)}) collective-permute-start(bf16[1,176,1024]{2,1,0:T(8,128)(2,1)} %get-tuple-element.303), channel_id=1, source_target_pairs={{0,2},{1,3},{2,4},{3,5},{4,6},{5,7},{6,0},{7,1},{8,10},{9,11},{10,... | collective-permute-start | bytes 1081352 | tf_op jit(solution)/shard_map/ppermute | solution.py:771
  370.2 17.3 %collective-permute-start.54 = (bf16[1,176,1024]{2,1,0:T(8,128)(2,1)}, bf16[1,176,1024]{2,1,0:T(8,128)(2,1)S(1)}, u32[]{:S(2)}, u32[]{:S(2)}) collective-permute-start(bf16[1,176,1024]{2,1,0:T(8,128)(2,1)} %get-tuple-element.304), channel_id=1, source_target_pairs={{0,6},{1,7},{2,0},{3,1},{4,2},{5,3},{6,4},{7,5},{8,14},{9,15},{10,... | collective-permute-start | bytes 1081352 | tf_op jit(solution)/shard_map/ppermute | solution.py:771
  402.9 22.7 %collective-permute-start.57 = (bf16[4,112,1024]{2,1,0:T(8,128)(2,1)}, bf16[4,112,1024]{2,1,0:T(8,128)(2,1)S(1)}, u32[]{:S(2)}, u32[]{:S(2)}) collective-permute-start(bf16[4,112,1024]{2,1,0:T(8,128)(2,1)} %get-tuple-element.310), channel_id=1, source_target_pairs={{0,16},{1,17},{2,18},{3,19},{4,20},{5,21},{6,22},{7,23},{8,24},{9,... | collective-permute-start | bytes 2752520 | tf_op jit(solution)/shard_map/ppermute | solution.py:771
  404.1 22.3 %collective-permute-start.58 = (bf16[4,112,1024]{2,1,0:T(8,128)(2,1)}, bf16[4,112,1024]{2,1,0:T(8,128)(2,1)S(1)}, u32[]{:S(2)}, u32[]{:S(2)}) collective-permute-start(bf16[4,112,1024]{2,1,0:T(8,128)(2,1)} %get-tuple-element.312), channel_id=1, source_target_pairs={{0,1},{1,0},{2,3},{3,2},{4,5},{5,4},{6,7},{7,6},{8,9},{9,8},{10,11... | collective-permute-start | bytes 2752520 | tf_op jit(solution)/shard_map/ppermute | solution.py:771
  404.6 17.8 %collective-permute-start.56 = (bf16[1,176,1024]{2,1,0:T(8,128)(2,1)}, bf16[1,176,1024]{2,1,0:T(8,128)(2,1)S(1)}, u32[]{:S(2)}, u32[]{:S(2)}) collective-permute-start(bf16[1,176,1024]{2,1,0:T(8,128)(2,1)} %get-tuple-element.308), channel_id=1, source_target_pairs={{0,4},{1,5},{2,6},{3,7},{4,0},{5,1},{6,2},{7,3},{8,12},{9,13},{10,... | collective-permute-start | bytes 1081352 | tf_op jit(solution)/shard_map/ppermute | solution.py:771
  431.2 11.7 %collective-permute-start.59 = (bf16[2,112,1024]{2,1,0:T(8,128)(2,1)}, bf16[2,112,1024]{2,1,0:T(8,128)(2,1)S(1)}, u32[]{:S(2)}, u32[]{:S(2)}) collective-permute-start(bf16[2,112,1024]{2,1,0:T(8,128)(2,1)} %get-tuple-element.315), channel_id=1, source_target_pairs={{0,1},{1,0},{2,3},{3,2},{4,5},{5,4},{6,7},{7,6},{8,9},{9,8},{10,11... | collective-permute-start | bytes 1376264 | tf_op jit(solution)/shard_map/ppermute | solution.py:771
  431.8 11.3 %collective-permute-start.60 = (bf16[2,112,1024]{2,1,0:T(8,128)(2,1)}, bf16[2,112,1024]{2,1,0:T(8,128)(2,1)S(1)}, u32[]{:S(2)}, u32[]{:S(2)}) collective-permute-start(bf16[2,112,1024]{2,1,0:T(8,128)(2,1)} %get-tuple-element.317), channel_id=1, source_target_pairs={{0,16},{1,17},{2,18},{3,19},{4,20},{5,21},{6,22},{7,23},{8,24},{9,... | collective-permute-start | bytes 1376264 | tf_op jit(solution)/shard_map/ppermute | solution.py:771
  447.2 21.7 %collective-permute-start.61 = (bf16[1,304,1024]{2,1,0:T(8,128)(2,1)}, bf16[1,304,1024]{2,1,0:T(8,128)(2,1)S(1)}, u32[]{:S(2)}, u32[]{:S(2)}) collective-permute-start(bf16[1,304,1024]{2,1,0:T(8,128)(2,1)} %add_last.2.own), channel_id=1, source_target_pairs={{0,16},{1,17},{2,18},{3,19},{4,20},{5,21},{6,22},{7,23},{8,24},{9,... | collective-permute-start | bytes 1867784 | tf_op jit(solution)/shard_map/ppermute | solution.py:771
  448.2 17.2 %collective-permute-start.63 = (bf16[1,112,1024]{2,1,0:T(8,128)(2,1)}, bf16[1,112,1024]{2,1,0:T(8,128)(2,1)S(1)}, u32[]{:S(2)}, u32[]{:S(2)}) collective-permute-start(bf16[1,112,1024]{2,1,0:T(8,128)(2,1)} %get-tuple-element.321), channel_id=1, source_target_pairs={{0,4},{1,5},{2,6},{3,7},{4,0},{5,1},{6,2},{7,3},{8,12},{9,13},{10,... | collective-permute-start | bytes 688136 | tf_op jit(solution)/shard_map/ppermute | solution.py:771
  450.1 15.3 %collective-permute-start.64 = (bf16[1,112,1024]{2,1,0:T(8,128)(2,1)}, bf16[1,112,1024]{2,1,0:T(8,128)(2,1)S(1)}, u32[]{:S(2)}, u32[]{:S(2)}) collective-permute-start(bf16[1,112,1024]{2,1,0:T(8,128)(2,1)} %get-tuple-element.322), channel_id=1, source_target_pairs={{0,6},{1,7},{2,0},{3,1},{4,2},{5,3},{6,4},{7,5},{8,14},{9,15},{10,... | collective-permute-start | bytes 688136 | tf_op jit(solution)/shard_map/ppermute | solution.py:771
  (70 other events, 532.0 us)
